TPU v7x, 32 devices: a whole 2x2x4 slice. The times are simulated.
32 devices in a mesh: row: 16 (over z, y, core), col: 2 (over x).
Axes of the slice: x: 2, y: 2, z: 4, core: 2. Of those that a mesh axis runs over, the one named last changes fastest.
Arguments:
- matrix: float32 [14336, 14336], P('row', 'col'), may hold values from -16 to 16, as said below
- panels: float32 [2, 14336, 128], P(None, 'row'), may hold values from -0.050111484 to 0.050111484
- factors: float32 [2, 128, 128], replicated, may hold values from -1.2 to 1.6, as said below
Outputs:
- updated: float32 [14336, 14336], P('row', 'col')
Inputs may be any that keep to these rules, and one draw needn't show every extreme that they name: symmetric: matrix[r, c] equals matrix[c, r]. Each factors[p] is upper triangular, with diagonal entries between 0.8 and 1.6.
All inputs are finite; a program needn't handle non-finite values.
Results may differ from a plain program's by a relative error of at most 0.0001.
Values sent between devices are 32-bit elements; how exact they have to be, the bound alone decides.
No kernel may reach another device: no remote copies, remote signals or barrier semaphores. Data moves between devices by JAX's collectives and lax.ppermute only.
A program may use at most 128 MiB of HBM per device.

v0:
```python
import jax
import jax.numpy as jnp
from jax import lax
from jax.sharding import PartitionSpec as P


def matmul(former, latter):
    return jnp.dot(former, latter, precision=lax.Precision.HIGHEST)


def transposed_dot(former, latter):
    return lax.dot_general(
        former, latter, (((0,), (0,)), ((), ())), precision=lax.Precision.HIGHEST
    )


def outer_drop(current, former, latter):
    return current - lax.dot_general(
        former, latter, (((1,), (1,)), ((), ())), precision=lax.Precision.HIGHEST
    )


def weights(forward, vectors, factor, correct):
    return matmul(forward, factor) - 0.5 * matmul(vectors, correct)


def row_sums(current, vector_rows, extra_terms):
    summed = lax.psum((transposed_dot(current, vector_rows),) + extra_terms, "row")
    return (summed[0], tuple(summed[1:]))


def shards(matrix, panels, factors):
    col_index = lax.axis_index("col")
    local_cols = matrix.shape[1]
    width = panels.shape[2]
    gathered = lax.all_gather(panels, "row", axis=1, tiled=True)
    vector_cols = lax.dynamic_slice_in_dim(gathered, col_index * local_cols, local_cols, 1)
    current = matrix
    first_rows, second_rows = (panels[0], panels[1])
    first_cols, second_cols = (vector_cols[0], vector_cols[1])
    factor_one, factor_two = (factors[0], factors[1])
    joined_rows = jnp.concatenate([first_rows, second_rows], axis=1)
    forward = lax.psum(matmul(current, jnp.concatenate([first_cols, second_cols], axis=1)), "col")
    forward_cols, summed = row_sums(
        current,
        joined_rows,
        (transposed_dot(joined_rows, forward), transposed_dot(joined_rows, joined_rows)),
    )
    mixed_gram, self_gram = summed
    gram_one = mixed_gram[:width, :width]
    cross_yv = mixed_gram[width:, :width].T
    gram_old = mixed_gram[width:, width:]
    cross_vv = self_gram[:width, width:]
    correct_one = matmul(factor_one.T, matmul(gram_one, factor_one))
    cross_wv = matmul(factor_one.T, cross_yv) - 0.5 * matmul(correct_one.T, cross_vv)
    gram_two = gram_old - matmul(cross_vv.T, cross_wv) - matmul(cross_wv.T, cross_vv)
    correct_two = matmul(factor_two.T, matmul(gram_two, factor_two))
    yrow_one = forward[:, :width]
    wrow_one = weights(yrow_one, first_rows, factor_one, correct_one)
    yrow_two = forward[:, width:] - matmul(first_rows, cross_wv) - matmul(wrow_one, cross_vv)
    wrow_two = weights(yrow_two, second_rows, factor_two, correct_two)
    ycol_one = forward_cols[:, :width]
    wcol_one = weights(ycol_one, first_cols, factor_one, correct_one)
    ycol_two = forward_cols[:, width:] - matmul(first_cols, cross_wv) - matmul(wcol_one, cross_vv)
    wcol_two = weights(ycol_two, second_cols, factor_two, correct_two)
    current = outer_drop(
        current,
        jnp.concatenate([first_rows, wrow_one, second_rows, wrow_two], axis=1),
        jnp.concatenate([wcol_one, first_cols, wcol_two, second_cols], axis=1),
    )
    return current


def solution(mesh):
    placed = (P("row", "col"), P(None, "row", None), P())
    return jax.shard_map(
        shards, mesh=mesh, in_specs=placed, out_specs=P("row", "col"), check_vma=False
    )
```

profile of v0, /device:TPU:0, one launch (start us, length us, event | category | flops | bytes accessed | tf_op | source)
XLA Modules:
  0.0 454.3 jit_solution(8078026947436948195)
XLA Ops:
  6.5 0.0 all-gather.2.cloned.1.call-start
  6.5 2.4 copy.4
  9.0 0.0 all-gather.2.cloned.1.call-update
  9.0 0.0 all-reduce.4.cloned.1.call-start
  9.0 1.2 slice_bitcast_fusion.1
  10.3 1.7 fusion.36
  12.0 114.1 %all-gather.2.cloned.1.call-done = f32[2,14336,128]{1,2,0:T(8,128)} async-done(((f32[2,896,128]{1,2,0:T(8,128)}), f32[2,14336,128]{1,2,0:T(8,128)}) %all-gather.2.cloned.1.call-update) | async-done | bytes 14680080 | tf_op jit(solution)/shard_map/all_gather | solution.py:36
  126.1 3.9 dynamic-slice_bitcast_fusion.1
  130.0 0.0 copy-start
  130.0 0.0 copy-start.2
  130.0 1.9 copy-done
  131.9 1.1 copy-done.2
  133.0 28.7 %fusion.26 = f32[896,256]{0,1:T(8,128)} fusion(f32[896,7168]{1,0:T(8,128)} %param.3, f32[7168,128]{0,1:T(8,128)S(1)} %get-tuple-element.9, f32[7168,128]{0,1:T(8,128)S(1)} %get-tuple-element.8), kind=kOutput, calls=%fused_computation.31 | convolution fusion | flops 19731841024 | bytes 33947648 | tf_op jit(solution)/shard_map/dot_general | solution.py:8
  161.7 0.0 all-reduce.4.cloned.1.call-update
  161.7 0.5 all-reduce.6.cloned.1.call-start
  162.2 28.8 %convolution_bitcast_fusion = f32[7168,256]{0,1:T(8,128)} fusion(f32[896,7168]{1,0:T(8,128)} %param.3, f32[896,128]{0,1:T(8,128)S(1)} %get-tuple-element.11, f32[896,128]{0,1:T(8,128)S(1)} %get-tuple-element.10), kind=kOutput, calls=%fused_computation.9 | convolution fusion | flops 19730235392 | bytes 33947648 | tf_op jit(solution)/shard_map/dot_general | solution.py:12
  191.1 6.1 %all-reduce.4.cloned.1.call-done = f32[896,256]{0,1:T(8,128)} async-done(((f32[896,256]{0,1:T(8,128)}), f32[896,256]{0,1:T(8,128)}) %all-reduce.4.cloned.1.call-update) | async-done | bytes 917520 | tf_op jit(solution)/shard_map/psum | solution.py:43
  197.2 2.9 fusion.37
  200.1 0.0 all-reduce.6.cloned.1.call-update
  200.1 1.2 copy-done.6
  201.3 0.0 copy-done.7
  201.3 0.6 fusion.38
  201.8 162.4 %all-reduce.6.cloned.1.call-done = (f32[256,256]{1,0:T(8,128)}, f32[256,256]{1,0:T(8,128)}, f32[7168,256]{0,1:T(8,128)}) async-done(((f32[256,256]{1,0:T(8,128)}, f32[256,256]{1,0:T(8,128)}, f32[7168,256]{0,1:T(8,128)}), (f32[256,256]{1,0:T(8,128)}, f32[256,256]{1,0:T(8,128)}, f32[7168,256]{0,1:T(8,128)})) %all-reduce.6.cloned.1.call-update) | async-done | bytes 7864336 | tf_op jit(solution)/shard_map/psum | solution.py:28
  364.3 1.0 convolution_bitcast_fusion.2
  365.3 1.0 fusion.41
  366.4 0.3 fusion.53
  366.6 1.1 fusion.35
  367.8 1.2 convolution_subtract_fusion.3
  369.0 0.0 copy-start.5
  369.0 6.9 %convolution_subtract_fusion.1 = f32[7168,128]{0,1:T(8,128)S(1)} fusion(f32[7168,128]{0,1:T(8,128)} %copy-done, f32[128,128]{0,1:T(8,128)S(1)} %fusion.35, f32[7168,256]{0,1:T(8,128)} %get-tuple-element.7), kind=kOutput, calls=%fused_computation.13 | convolution fusion | flops 1410203648 | bytes 11075584 | tf_op jit(solution)/shard_map/dot_general | solution.py:8
  375.9 0.0 copy-done.5
  375.9 3.6 fusion.17
  379.6 0.0 copy-done.4
  379.6 0.0 copy-start.1
  379.6 0.5 fusion.34
  380.1 0.2 convolution_subtract_fusion.2
  380.3 0.2 fusion.47
  380.5 0.3 fusion.45
  380.8 0.6 fusion.64
  381.4 0.5 fusion.30
  382.0 0.6 fusion.49
  382.5 4.4 fusion.12
  386.9 3.6 convolution_subtract_fusion
  390.6 0.0 copy-start.3
  390.6 3.6 fusion.43
  394.2 0.5 fusion.32
  394.7 4.1 fusion.11
  398.9 48.7 %fusion.8 = f32[896,7168]{1,0:T(8,128)} fusion(f32[896,7168]{1,0:T(8,128)} %param.3, f32[7168,128]{0,1:T(8,128)S(1)} %copy-done.3, f32[7168,128]{0,1:T(8,128)S(1)} %fusion.11, f32[7168,128]{0,1:T(8,128)S(1)} %copy-done.1, f32[7168,128]{0,1:T(8,128)S(1)} %fusion.12, f32[896,128]{0,1:T(8,128)S(1)} %fusion.32, f32[896,128]{0,1:T(8,128)S(1)} %get-tuple-element.11, ...), kind=kOutput, calls=%fused_computation.8 | convolution fusion | flops 39478820864 | bytes 67895296 | tf_op jit(solution)/shard_map/dot_general | solution.py:18
  (7 shorter events, 0.0 us)
Async XLA Ops:
  6.5 119.5 %all-gather.2.cloned.1.call-start = ((), (), s32[]{:S(2)}) async-start(), calls=%async_computation | async-start | bytes 15597568 | tf_op jit(solution)/shard_map/all_gather | solution.py:36
  9.0 188.2 %all-reduce.4.cloned.1.call-start = ((), (), s32[]{:S(2)}) async-start(), calls=%async_computation.1 | async-start | bytes 1835008 | tf_op jit(solution)/shard_map/psum | solution.py:43
  130.0 1.9 copy-start
  130.0 3.0 copy-start.2
  161.7 202.6 %all-reduce.6.cloned.1.call-start = ((), (), s32[]{:S(2)}) async-start(), calls=%async_computation.2 | async-start | bytes 15728640 | tf_op jit(solution)/shard_map/psum | solution.py:28
  200.1 1.2 copy-start.6
  200.1 1.2 copy-start.7
  369.0 7.0 %copy-start.5 = (f32[7168,256]{0,1:T(8,128)S(1)}, f32[7168,256]{0,1:T(8,128)}, u32[]{:S(2)}) copy-start(f32[7168,256]{0,1:T(8,128)} %get-tuple-element.7) | copy-start | bytes 22020100
  375.9 3.6 copy-start.4
  375.9 4.2 copy-start.8
  379.6 3.0 copy-start.1
  390.6 4.2 copy-start.3
Sparse Core Ops, SparseCore 0:
  9.6 116.4 all-gather.1
  161.8 35.2 all-reduce.3
  201.7 162.5 all-reduce.5
where the time goes:
time: 461 us; the launch traced here: 454 us
  waiting for transfers between devices  283 us (61%)
  matrix products  146 us (32%)
  between operations  13.6 us (3%)
  local copies, waits for them, and re-layouts  11.7 us (3%)
    psum x1, waiting for transfers between devices, row_sums(): lax.psum((transposed_dot(current, vector_rows),) + extra_terms, 'row')  162 us
    all_gather x1, waiting for transfers between devices, shards(): gathered = lax.all_gather(panels, 'row', axis=1, tiled=True)  114 us
    dot_general x21, matrix products, matmul(): return jnp.dot(former, latter, precision=lax.Precision.HIGHEST)  63.6 us
    dot_general x1, matrix products, outer_drop(): lax.dot_general(former, latter, (((1,), (1,)), ((), ())), precision=lax.P...  48.7 us
    dot_general x3, matrix products, transposed_dot(): lax.dot_general(former, latter, (((0,), (0,)), ((), ())), precision=lax.P...  33.5 us
  transfers between devices with their start and end apart: 3, of which 3 were waited for; matrix products, arithmetic and copies ran while one was open for 7% of the time, Pallas kernels for 0%

commit v1 on v0

v1 whole, which is shorter than its diff:
```python
import functools

import jax
import jax.numpy as jnp
from jax import lax
from jax.experimental import pallas as pl
from jax.experimental.pallas import tpu as pltpu
from jax.sharding import PartitionSpec as P

F32 = jnp.float32
BF16 = jnp.bfloat16
PLAIN = (((1,), (0,)), ((), ()))
BOTH_LAST = (((1,), (1,)), ((), ()))
BOTH_FIRST = (((0,), (0,)), ((), ()))
VMEM_BYTES = 48 * 1024 * 1024
STEPS = 2


def split(values):
    high = values.astype(BF16)
    return high, (values - high.astype(F32)).astype(BF16)


def product(former, latter, dims=PLAIN):
    dot = functools.partial(lax.dot_general, dimension_numbers=dims, preferred_element_type=F32)
    return dot(former[0], latter[0]) + (dot(former[0], latter[1]) + dot(former[1], latter[0]))


def small(former, latter, dims=PLAIN):
    return lax.dot_general(
        former, latter, dims, precision=lax.Precision.HIGHEST, preferred_element_type=F32
    )


def in_order(place, joined, pairs):
    odd = place[0] % 2 != 0
    depth, width = pairs[0][0].shape
    for number, (near, far) in enumerate(pairs):
        lanes = slice(number * width, (number + 1) * width)
        for top, block in ((0, jnp.where(odd, far[...], near[...])), (depth, jnp.where(odd, near[...], far[...]))):
            high, low = split(block)
            joined[0][top : top + depth, lanes] = high
            joined[1][top : top + depth, lanes] = low


def forward_kernel(first, last, place, block, *refs):
    pairs, refs, joined = (refs[:2], refs[2:4]), refs[4:-2], refs[-2:]
    step = pl.program_id(0)
    pl.when(step == 0)(lambda: in_order(place, joined, pairs))
    total = product(split(block[...]), (joined[0][...], joined[1][...]))
    if not first:
        total = total + refs[0][...]
        refs = refs[1:]
    if not last:
        refs[0][...] = total
        return
    own, kept, sent, inner = refs
    width = own.shape[2]
    one, two = total[:, :width], total[:, width:]
    swap = place[1] != 0
    kept[...] = jnp.where(swap, two, one)
    sent[...] = jnp.where(swap, one, two)

    @pl.when(step == 0)
    def _():
        inner[...] = jnp.zeros_like(inner)

    inner[0] += small(own[0], one, BOTH_FIRST)
    inner[1] += small(own[1], one, BOTH_FIRST)
    inner[2] += small(own[1], two, BOTH_FIRST)
    inner[3] += small(own[0], own[1], BOTH_FIRST)


def forward_step(place, matrix, slot, pairs, before, own):
    rows = matrix.shape[0]
    depth, width = pairs[0][0].shape
    tile = rows // STEPS
    first, last = before is None, own is not None
    whole = lambda shape: pl.BlockSpec(shape, lambda step, place: (0,) * len(shape))
    strip = lambda columns: pl.BlockSpec((tile, columns), lambda step, place: (step, 0))
    operands = [matrix, *pairs[0], *pairs[1]]
    specs = [pl.BlockSpec((tile, 2 * depth), lambda step, place: (step, (place[0] ^ slot) // 2))]
    specs += [whole((depth, width))] * 4
    if not first:
        operands.append(before)
        specs.append(strip(2 * width))
    outs, out_specs = [jax.ShapeDtypeStruct((rows, 2 * width), F32)], [strip(2 * width)]
    if last:
        operands.append(own)
        specs.append(pl.BlockSpec((2, tile, width), lambda step, place: (0, step, 0)))
        part = jax.ShapeDtypeStruct((rows, width), F32)
        outs = [part, part, jax.ShapeDtypeStruct((4, width, width), F32)]
        out_specs = [strip(width), strip(width), whole(outs[2].shape)]
    return pl.pallas_call(
        functools.partial(forward_kernel, first, last),
        grid_spec=pltpu.PrefetchScalarGridSpec(
            num_scalar_prefetch=1,
            grid=(STEPS,),
            in_specs=specs,
            out_specs=out_specs,
            scratch_shapes=[pltpu.VMEM((2 * depth, 2 * width), BF16)] * 2,
        ),
        out_shape=outs,
        compiler_params=pltpu.CompilerParams(vmem_limit_bytes=VMEM_BYTES),
        cost_estimate=pl.CostEstimate(
            flops=6 * rows * depth * 4 * width, bytes_accessed=8 * rows * depth, transcendentals=0
        ),
    )(place, *operands)


def mix_kernel(place, own, mine, other, inner, factors, high, low):
    one, two = factors[0], factors[1]
    gram_one, cross_yv, gram_old, cross_vv = inner[0], inner[1], inner[2], inner[3]
    correct_one = small(small(one, gram_one, BOTH_FIRST), one)
    cross_wv = small(one, cross_yv, (((0,), (1,)), ((), ()))) - 0.5 * small(
        correct_one, cross_vv, BOTH_FIRST
    )
    drop = small(cross_vv, cross_wv, BOTH_FIRST)
    gram_two = gram_old - drop - small(cross_wv, cross_vv, BOTH_FIRST)
    correct_two = small(small(two, gram_two, BOTH_FIRST), two)
    mixed = -small(small(one, cross_vv), two)
    edge = small(0.5 * small(correct_one, cross_vv) - cross_wv, two)
    swap = place[1] != 0
    y_one = jnp.where(swap, other[...], mine[...])
    y_two = jnp.where(swap, mine[...], other[...])
    v_one, v_two = own[0], own[1]
    p_one = small(v_one, one, BOTH_LAST) + small(v_two, mixed, BOTH_LAST)
    p_two = small(v_two, two, BOTH_LAST)
    q_one = (
        small(y_one, one)
        - small(v_one, 0.5 * (correct_one + correct_one.T))
        + small(v_two, edge, BOTH_LAST)
    )
    q_two = (
        small(y_one, mixed)
        + small(y_two, two)
        + small(v_one, edge)
        - small(v_two, 0.5 * (correct_two + correct_two.T))
    )
    turn = place[2] != 0
    parts = (jnp.where(turn, p_two, p_one), jnp.where(turn, p_one, p_two), q_one, q_two)
    width = v_one.shape[1]
    for number, part in enumerate(parts):
        lanes = slice(number * width, (number + 1) * width)
        high[:, lanes], low[:, lanes] = split(part)


def mix(place, own, mine, other, inner, factors):
    rows, width = mine.shape
    side = jax.ShapeDtypeStruct((rows, 4 * width), BF16)
    vmem = pl.BlockSpec(memory_space=pltpu.VMEM)
    return pl.pallas_call(
        mix_kernel,
        in_specs=[pl.BlockSpec(memory_space=pltpu.SMEM)] + [vmem] * 5,
        out_specs=[vmem, vmem],
        out_shape=[side, side],
        compiler_params=pltpu.CompilerParams(vmem_limit_bytes=VMEM_BYTES),
        cost_estimate=pl.CostEstimate(
            flops=12 * rows * width * 8 * width, bytes_accessed=32 * rows * width, transcendentals=0
        ),
    )(place, own, mine, other, inner, factors)


def update_kernel(first, place, block, high, low, *refs):
    pairs, out, joined = [refs[2 * n : 2 * n + 2] for n in range(4)], refs[-3], refs[-2:]
    pl.when(pl.program_id(0) == 0)(lambda: in_order(place, joined, pairs))
    side = (joined[0][...], joined[1][...])
    out[...] = block[...] - product((high[...], low[...]), side, BOTH_LAST)


def update_step(place, matrix, slot, sides, pairs, before):
    rows = matrix.shape[0]
    depth, width = pairs[0][0].shape
    tile = rows // STEPS
    first = before is None
    block = pl.BlockSpec((tile, 2 * depth), lambda step, place: (step, (place[0] ^ slot) // 2))
    strip = pl.BlockSpec((tile, 4 * width), lambda step, place: (step, 0))
    whole = pl.BlockSpec((depth, width), lambda step, place: (0, 0))
    operands = [matrix, *sides] + [part for pair in pairs for part in pair]
    specs = [block, strip, strip] + [whole] * 8
    aliases = {}
    if not first:
        aliases = {1 + len(operands): 0}
        operands.append(before)
        specs.append(pl.BlockSpec(memory_space=pl.ANY))
    return pl.pallas_call(
        functools.partial(update_kernel, first),
        grid_spec=pltpu.PrefetchScalarGridSpec(
            num_scalar_prefetch=1,
            grid=(STEPS,),
            in_specs=specs,
            out_specs=block,
            scratch_shapes=[pltpu.VMEM((2 * depth, 4 * width), BF16)] * 2,
        ),
        out_shape=jax.ShapeDtypeStruct(matrix.shape, F32),
        input_output_aliases=aliases,
        compiler_params=pltpu.CompilerParams(vmem_limit_bytes=VMEM_BYTES),
        cost_estimate=pl.CostEstimate(
            flops=6 * rows * depth * 8 * width, bytes_accessed=16 * rows * depth, transcendentals=0
        ),
    )(place, *operands)


def solution(mesh):
    row_count, col_count = mesh.shape["row"], mesh.shape["col"]
    group = row_count // col_count
    assert group * col_count == row_count and group >= 2 and group & (group - 1) == 0
    halves = col_count == 2

    def flip(values, axis, bit):
        count = mesh.shape[axis]
        return lax.ppermute(values, axis, [(i, i ^ bit) for i in range(count)])

    def transpose(values, turn):
        pairs = []
        for s in range(col_count):
            for b in range(group):
                for j in range(col_count):
                    source = (s * group + b) * col_count + j
                    pairs.append((source, ((j - turn) % col_count * group + b) * col_count + s))
        return lax.ppermute(values, ("row", "col"), pairs)

    def spread(own):
        found = {0: own}
        for d in range(2, group, 2):
            found[d] = flip(own, "row", d)
        for d in range(0, group, 2):
            found[d + 1] = flip(found[d], "row", 1)
        return found

    def total(values):
        for axis in ("col", "row"):
            count = mesh.shape[axis]
            if count & (count - 1):
                values = lax.psum(values, axis)
                continue
            bit = 1
            while bit < count:
                values = values + flip(values, axis, bit)
                bit *= 2
        return values

    def shards(matrix, panels, factors):
        row, col = lax.axis_index("row"), lax.axis_index("col")
        zero = jnp.zeros_like(row)
        place = jnp.stack(
            [row % group, col if halves else zero, row // group if halves else zero]
        ).astype(jnp.int32)
        vectors = [spread(transpose(panels[p], p)) for p in range(2)]
        partial = None
        for slot in range(0, group, 2):
            pairs = [(v[slot], v[slot + 1]) for v in vectors]
            last = slot + 2 == group
            found = forward_step(place, matrix, slot, pairs, partial, panels if last else None)
            partial = found[0]
        kept, sent, inner = found
        inner = total(inner * jnp.array([1, 1, 1, 1 / col_count], F32)[:, None, None])
        if halves:
            mine = kept + flip(sent, "col", 1)
            other = flip(mine, "col", 1)
            firsts, seconds = transpose(mine, 0), transpose(mine, 1)
        else:
            mine, other = lax.psum((kept, sent), "col")
            firsts, seconds = transpose(mine, 0), transpose(other, 1)
        products = [spread(firsts), spread(seconds)]
        sides = mix(place, panels, mine, other, inner, factors)
        updated = None
        for slot in range(0, group, 2):
            pairs = [(v[slot], v[slot + 1]) for v in products + vectors]
            updated = update_step(place, matrix, slot, sides, pairs, updated)
        return updated

    placed = (P("row", "col"), P(None, "row", None), P())
    return jax.shard_map(
        shards, mesh=mesh, in_specs=placed, out_specs=P("row", "col"), check_vma=False
    )
```

time: 461 us -> 231 us (0.50); the launches traced: 454 us -> 231 us
  waiting for transfers between devices: 283 us -> 94.5 us
  matrix products: 146 us -> 0 us
  Pallas kernels: 0 us -> 77.7 us
  starting transfers between devices: 0.55 us -> 53.2 us
  between operations: 13.6 us -> 0.23 us
  local copies, waits for them, and re-layouts: 11.7 us -> 4.81 us
    psum x2 -> x0, waiting for transfers between devices: 169 us -> none  [the longest x1 162 us: row_sums(): lax.psum((transposed_dot(current, vector_rows),) + extra_terms, 'row')]
    dot_general x25 -> x0, matrix products: 146 us -> none  [the longest x21 63.6 us: matmul(): return jnp.dot(former, latter, precision=lax.Precision.HIGHEST)]
    all_gather x1 -> x0, waiting for transfers between devices: 114 us -> none  [shards(): gathered = lax.all_gather(panels, 'row', axis=1, tiled=True)]
    ppermute x0 -> x39, waiting for transfers between devices: none -> 94.5 us  [the longest x35 74.6 us: flip(): return lax.ppermute(values, axis, [(i, i ^ bit) for i in range(count)])]
    pallas_call x0 -> x9, Pallas kernels: none -> 77.7 us  [the longest x4 42.8 us: update_step(): pl.pallas_call(functools.partial(update_kernel, first), grid_spec=pltpu.P...]
    ppermute x0 -> x39, starting transfers between devices: none -> 53.2 us  [the longest x35 39.7 us: flip(): return lax.ppermute(values, axis, [(i, i ^ bit) for i in range(count)])]
  transfers between devices with their start and end apart: 3 -> 39, of which waited for: 3 -> 13; matrix products, arithmetic and copies ran while one was open for 7% -> 0% of each run, Pallas kernels for 0% -> 24%
where the time goes in v1:
time: 231 us
  waiting for transfers between devices  94.5 us (41%)
  Pallas kernels  77.7 us (34%)
  starting transfers between devices  53.2 us (23%)
  local copies, waits for them, and re-layouts  4.81 us (2%)
    ppermute x35, waiting for transfers between devices, flip(): return lax.ppermute(values, axis, [(i, i ^ bit) for i in range(count)])  74.6 us
    pallas_call x4, Pallas kernels, update_step(): pl.pallas_call(functools.partial(update_kernel, first), grid_spec=pltpu.P...  42.8 us
    ppermute x35, starting transfers between devices, flip(): return lax.ppermute(values, axis, [(i, i ^ bit) for i in range(count)])  39.7 us
    pallas_call x4, Pallas kernels, forward_step(): pl.pallas_call(functools.partial(forward_kernel, first, last), grid_spec=...  28.7 us
    ppermute x4, waiting for transfers between devices, transpose(): return lax.ppermute(values, ('row', 'col'), pairs)  19.9 us
    ppermute x4, starting transfers between devices, transpose(): return lax.ppermute(values, ('row', 'col'), pairs)  13.5 us
    pallas_call x1, Pallas kernels, mix(): pl.pallas_call(mix_kernel, in_specs=[pl.BlockSpec(memory_space=pltpu.SMEM...  6.19 us
  transfers between devices with their start and end apart: 39, of which 13 were waited for; matrix products, arithmetic and copies ran while one was open for 0% of the time, Pallas kernels for 24%

profile of v1, /device:TPU:0, one launch (start us, length us, event | category | flops | bytes accessed | tf_op | source)
XLA Modules:
  0.0 230.9 jit_solution(12782267453995675132)
XLA Ops:
  0.0 1.2 slice_bitcast_fusion
  1.2 1.4 collective-permute-start
  2.6 5.8 %collective-permute-start.3 = (f32[896,128]{1,0:T(8,128)S(1)}, f32[896,128]{1,0:T(8,128)}, u32[]{:S(2)}, u32[]{:S(2)}) collective-permute-start(f32[896,128]{1,0:T(8,128)S(1)} %get-tuple-element.15), channel_id=1, source_target_pairs={{0,16},{1,0},{2,18},{3,2},{4,20},{5,4},{6,22},{7,6},{8,24},{9,8},{... | collective-permute-start | bytes 1376264 | tf_op jit(solution)/shard_map/ppermute | solution.py:221
  8.5 10.5 %collective-permute-done.3.refs_2_.refs_6_ = f32[896,128]{1,0:T(8,128)} collective-permute-done((f32[896,128]{1,0:T(8,128)S(1)}, f32[896,128]{1,0:T(8,128)}, u32[]{:S(2)}, u32[]{:S(2)}) %collective-permute-start.3) | collective-permute-done | bytes 458784 | tf_op jit(solution)/shard_map/ppermute | solution.py:221
  19.0 1.5 collective-permute-start.10
  20.6 0.5 collective-permute-start.12
  21.1 10.3 %collective-permute-start.6 = (f32[896,128]{1,0:T(8,128)}, f32[896,128]{1,0:T(8,128)S(1)}, u32[]{:S(2)}, u32[]{:S(2)}) collective-permute-start(f32[896,128]{1,0:T(8,128)} %collective-permute-done.refs_0_.refs_4_), channel_id=1, source_target_pairs={{0,8},{2,10},{4,12},{6,14},{8,0},{10,2},{12,4},{14,6},{16,24},{18,... | collective-permute-start | bytes 1376264 | tf_op jit(solution)/shard_map/ppermute | solution.py:212
  31.3 0.8 copy-done.1
  32.1 0.8 copy-done.3
  32.9 3.0 %collective-permute-start.1 = (f32[896,128]{1,0:T(8,128)}, f32[896,128]{1,0:T(8,128)S(1)}, u32[]{:S(2)}, u32[]{:S(2)}) collective-permute-start(f32[896,128]{1,0:T(8,128)} %collective-permute-done.refs_0_.refs_4_), channel_id=1, source_target_pairs={{0,12},{2,14},{4,8},{6,10},{8,4},{10,6},{12,0},{14,2},{16,28},{18,... | collective-permute-start | bytes 1376264 | tf_op jit(solution)/shard_map/ppermute | solution.py:212
  35.9 7.9 %collective-permute-start.4 = (f32[896,128]{1,0:T(8,128)}, f32[896,128]{1,0:T(8,128)S(1)}, u32[]{:S(2)}, u32[]{:S(2)}) collective-permute-start(f32[896,128]{1,0:T(8,128)} %collective-permute-done.3.refs_2_.refs_6_), channel_id=1, source_target_pairs={{0,12},{2,14},{4,8},{6,10},{8,4},{10,6},{12,0},{14,2},{16,28},{18,... | collective-permute-start | bytes 1376264 | tf_op jit(solution)/shard_map/ppermute | solution.py:212
  43.8 0.5 collective-permute-start.13
  44.4 8.3 %collective-permute-done.8.refs_2_.refs_6_ = f32[896,128]{1,0:T(8,128)S(1)} collective-permute-done((f32[896,128]{1,0:T(8,128)}, f32[896,128]{1,0:T(8,128)S(1)}, u32[]{:S(2)}, u32[]{:S(2)}) %collective-permute-start.8) | collective-permute-done | bytes 458784 | tf_op jit(solution)/shard_map/ppermute | solution.py:212
  52.7 10.8 %collective-permute-done.1.refs_0_.refs_4_ = f32[896,128]{1,0:T(8,128)S(1)} collective-permute-done((f32[896,128]{1,0:T(8,128)}, f32[896,128]{1,0:T(8,128)S(1)}, u32[]{:S(2)}, u32[]{:S(2)}) %collective-permute-start.1) | collective-permute-done | bytes 458784 | tf_op jit(solution)/shard_map/ppermute | solution.py:212
  63.5 1.0 copy-done.2
  64.5 1.0 copy-done.4
  65.5 6.0 %shard_map.46.refs_4_ = f32[896,256]{1,0:T(8,128)S(1)} custom-call(s32[3]{0:T(128)S(1)} %pad_add_fusion.place, f32[896,7168]{1,0:T(8,128)} %block.15, f32[896,128]{1,0:T(8,128)} %collective-permute-done.refs_0_.refs_4_, f32[896,128]{1,0:T(8,128)S(1)} %copy-done.2, f32[896,128]{1,0:T(8,128)} %collective-permute-done.3.refs_2_.refs_6_, f32[896,128]{1,0:T(8,128)S(1)} %copy-done.4), custom_call_target="tpu_custom_call" | custom-call | flops 2466250752 | bytes 6422528 | tf_op jit(solution)/shard_map/pallas_call | solution.py:94
  71.6 1.0 collective-permute-done.4.refs_2_.refs_6_
  72.6 0.5 collective-permute-start.5
  73.1 5.9 %shard_map.47.refs_4_ = f32[896,256]{1,0:T(8,128)S(1)} custom-call(s32[3]{0:T(128)S(1)} %pad_add_fusion.place, f32[896,7168]{1,0:T(8,128)} %block.15, f32[896,128]{1,0:T(8,128)S(1)} %collective-permute-done.10.refs_0_.refs_4_, f32[896,128]{1,0:T(8,128)S(1)} %collective-permute-done.11.refs_1_.refs_5_, ...), custom_call_target="tpu_custom_call" | custom-call | flops 2466250752 | bytes 6422528 | tf_op jit(solution)/shard_map/pallas_call | solution.py:94
  79.0 5.8 %shard_map.48.refs_4_ = f32[896,256]{1,0:T(8,128)S(1)} custom-call(s32[3]{0:T(128)S(1)} %pad_add_fusion.place, f32[896,7168]{1,0:T(8,128)} %block.15, f32[896,128]{1,0:T(8,128)S(1)} %collective-permute-done.6.refs_0_.refs_4_, f32[896,128]{1,0:T(8,128)S(1)} %collective-permute-done.7.refs_1_.refs_5_, f32[896,128]{1,0:T(8,128)S(1)} %collective-permute-done.8.refs_2_.refs_6_, ...), custom_call_target="tpu_custom_call" | custom-call | flops 2466250752 | bytes 6422528 | tf_op jit(solution)/shard_map/pallas_call | solution.py:94
  84.9 11.0 %shard_map.49 = (f32[896,128]{1,0:T(8,128)S(1)}, f32[896,128]{1,0:T(8,128)S(1)}, f32[4,128,128]{2,1,0:T(8,128)S(1)}) custom-call(s32[3]{0:T(128)S(1)} %pad_add_fusion.place, f32[896,7168]{1,0:T(8,128)} %block.15, f32[896,128]{1,0:T(8,128)S(1)} %collective-permute-done.1.refs_0_.refs_4_, f32[896,128]{1,0:T(8,128)S(1)} %collective-permute-done.2.refs_1_.refs_5_, ...), custom_call_target="tpu_custom_call" | custom-call | flops 2466250752 | bytes 6422528 | tf_op jit(solution)/shard_map/pallas_call | solution.py:94
  96.0 4.0 %collective-permute-start.18 = (f32[4,128,128]{2,1,0:T(8,128)S(1)}, f32[4,128,128]{2,1,0:T(8,128)S(1)}, u32[]{:S(2)}, u32[]{:S(2)}) collective-permute-start(f32[4,128,128]{2,1,0:T(8,128)S(1)} %broadcast_multiply_fusion), channel_id=1, source_target_pairs={{0,1},{1,0},{2,3},{3,2},{4,5},{5,4},{6,7},{7,6},{8,9},{9,8},{10,11... | collective-permute-start | bytes 786440 | tf_op jit(solution)/shard_map/ppermute | solution.py:212
  100.0 6.5 %collective-permute-done.18 = f32[4,128,128]{2,1,0:T(8,128)S(1)} collective-permute-done((f32[4,128,128]{2,1,0:T(8,128)S(1)}, f32[4,128,128]{2,1,0:T(8,128)S(1)}, u32[]{:S(2)}, u32[]{:S(2)}) %collective-permute-start.18) | collective-permute-done | bytes 262176 | tf_op jit(solution)/shard_map/ppermute | solution.py:212
  106.7 1.8 collective-permute-start.16
  108.5 0.6 collective-permute-start.20
  109.1 7.9 %collective-permute-done.20 = f32[4,128,128]{2,1,0:T(8,128)S(1)} collective-permute-done((f32[4,128,128]{2,1,0:T(8,128)S(1)}, f32[4,128,128]{2,1,0:T(8,128)S(1)}, u32[]{:S(2)}, u32[]{:S(2)}) %collective-permute-start.20) | collective-permute-done | bytes 262176 | tf_op jit(solution)/shard_map/ppermute | solution.py:212
  117.4 2.3 collective-permute-done.16
  119.7 0.7 collective-permute-start.23
  120.4 5.6 %collective-permute-start.26 = (f32[896,128]{1,0:T(8,128)S(1)}, f32[896,128]{1,0:T(8,128)S(1)}, u32[]{:S(2)}, u32[]{:S(2)}) collective-permute-start(f32[896,128]{1,0:T(8,128)S(1)} %add.24.mine), channel_id=1, source_target_pairs={{0,16},{1,0},{2,18},{3,2},{4,20},{5,4},{6,22},{7,6},{8,24},{9,8},{... | collective-permute-start | bytes 1376264 | tf_op jit(solution)/shard_map/ppermute | solution.py:221
  126.0 1.6 collective-permute-start.22
  127.6 9.3 %collective-permute-done.26.refs_2_ = f32[896,128]{1,0:T(8,128)S(1)} collective-permute-done((f32[896,128]{1,0:T(8,128)S(1)}, f32[896,128]{1,0:T(8,128)S(1)}, u32[]{:S(2)}, u32[]{:S(2)}) %collective-permute-start.26) | collective-permute-done | bytes 458784 | tf_op jit(solution)/shard_map/ppermute | solution.py:221
  136.9 0.5 collective-permute-start.33
  137.4 7.0 %collective-permute-done.17.other = f32[896,128]{1,0:T(8,128)S(1)} collective-permute-done((f32[896,128]{1,0:T(8,128)S(1)}, f32[896,128]{1,0:T(8,128)S(1)}, u32[]{:S(2)}, u32[]{:S(2)}) %collective-permute-start.17) | collective-permute-done | bytes 458784 | tf_op jit(solution)/shard_map/ppermute | solution.py:212
  144.5 0.5 collective-permute-start.35
  145.0 11.6 %collective-permute-done.22 = f32[4,128,128]{2,1,0:T(8,128)S(1)} collective-permute-done((f32[4,128,128]{2,1,0:T(8,128)S(1)}, f32[4,128,128]{2,1,0:T(8,128)S(1)}, u32[]{:S(2)}, u32[]{:S(2)}) %collective-permute-start.22) | collective-permute-done | bytes 262176 | tf_op jit(solution)/shard_map/ppermute | solution.py:212
  156.6 6.2 %shard_map.50 = (bf16[896,512]{1,0:T(8,128)(2,1)S(1)}, bf16[896,512]{1,0:T(8,128)(2,1)S(1)}) custom-call(s32[3]{0:T(128)S(1)} %pad_add_fusion.place, f32[2,896,128]{2,1,0:T(8,128)S(1)} %copy-done, f32[896,128]{1,0:T(8,128)S(1)} %add.24.mine, f32[896,128]{1,0:T(8,128)S(1)} %collective-permute-done.17.other, f32[4,128,128]{2,1,0:T(8,128)S(1)} %add.29.inner, ...), custom_call_target="tpu_custom_call" | custom-call | flops 1409286144 | bytes 3670016 | tf_op jit(solution)/shard_map/pallas_call | solution.py:152
  162.9 2.0 collective-permute-start.31
  164.9 2.9 %collective-permute-start.27 = (f32[896,128]{1,0:T(8,128)S(1)}, f32[896,128]{1,0:T(8,128)S(1)}, u32[]{:S(2)}, u32[]{:S(2)}) collective-permute-start(f32[896,128]{1,0:T(8,128)S(1)} %collective-permute-done.26.refs_2_), channel_id=1, source_target_pairs={{0,12},{2,14},{4,8},{6,10},{8,4},{10,6},{12,0},{14,2},{16,28},{18,... | collective-permute-start | bytes 1376264 | tf_op jit(solution)/shard_map/ppermute | solution.py:212
  167.8 2.1 collective-permute-done.29.refs_0_
  169.9 10.8 %shard_map.51.refs_8_ = f32[896,7168]{1,0:T(8,128)} custom-call(s32[3]{0:T(128)S(1)} %pad_add_fusion.place, f32[896,7168]{1,0:T(8,128)} %block.15, bf16[896,512]{1,0:T(8,128)(2,1)S(1)} %get-tuple-element.13.high, bf16[896,512]{1,0:T(8,128)(2,1)S(1)} %get-tuple-element.14.low, f32[896,128]{1,0:T(8,128)S(1)} %collective-permute-done.23.refs_0_, ...), custom_call_target="tpu_custom_call" | custom-call | flops 4932501504 | bytes 12845056 | tf_op jit(solution)/shard_map/pallas_call | solution.py:186
  180.8 0.5 collective-permute-start.30
  181.3 8.2 %collective-permute-done.24.refs_0_ = f32[896,128]{1,0:T(8,128)S(1)} collective-permute-done((f32[896,128]{1,0:T(8,128)S(1)}, f32[896,128]{1,0:T(8,128)S(1)}, u32[]{:S(2)}, u32[]{:S(2)}) %collective-permute-start.24) | collective-permute-done | bytes 458784 | tf_op jit(solution)/shard_map/ppermute | solution.py:212
  189.5 8.9 %collective-permute-done.27.refs_2_ = f32[896,128]{1,0:T(8,128)S(1)} collective-permute-done((f32[896,128]{1,0:T(8,128)S(1)}, f32[896,128]{1,0:T(8,128)S(1)}, u32[]{:S(2)}, u32[]{:S(2)}) %collective-permute-start.27) | collective-permute-done | bytes 458784 | tf_op jit(solution)/shard_map/ppermute | solution.py:212
  198.4 0.5 collective-permute-start.28
  198.9 10.7 %shard_map.52.refs_8_ = f32[896,7168]{1,0:T(8,128)} custom-call(s32[3]{0:T(128)S(1)} %pad_add_fusion.place, f32[896,7168]{1,0:T(8,128)} %block.15, bf16[896,512]{1,0:T(8,128)(2,1)S(1)} %get-tuple-element.13.high, bf16[896,512]{1,0:T(8,128)(2,1)S(1)} %get-tuple-element.14.low, ...), custom_call_target="tpu_custom_call", output_to_operand_aliasing={{}: (12, {})} | custom-call | flops 4932501504 | bytes 12845056 | tf_op jit(solution)/shard_map/pallas_call | solution.py:186
  209.6 10.6 %shard_map.53.refs_8_ = f32[896,7168]{1,0:T(8,128)} custom-call(s32[3]{0:T(128)S(1)} %pad_add_fusion.place, f32[896,7168]{1,0:T(8,128)} %block.15, bf16[896,512]{1,0:T(8,128)(2,1)S(1)} %get-tuple-element.13.high, bf16[896,512]{1,0:T(8,128)(2,1)S(1)} %get-tuple-element.14.low, ...), custom_call_target="tpu_custom_call", output_to_operand_aliasing={{}: (12, {})} | custom-call | flops 4932501504 | bytes 12845056 | tf_op jit(solution)/shard_map/pallas_call | solution.py:186
  220.3 10.6 %shard_map.54 = f32[896,7168]{1,0:T(8,128)} custom-call(s32[3]{0:T(128)S(1)} %pad_add_fusion.place, f32[896,7168]{1,0:T(8,128)} %block.15, bf16[896,512]{1,0:T(8,128)(2,1)S(1)} %get-tuple-element.13.high, bf16[896,512]{1,0:T(8,128)(2,1)S(1)} %get-tuple-element.14.low, ...), custom_call_target="tpu_custom_call", output_to_operand_aliasing={{}: (12, {})} | custom-call | flops 4932501504 | bytes 12845056 | tf_op jit(solution)/shard_map/pallas_call | solution.py:186
  (64 shorter events, 1.1 us)
Async XLA Ops:
  1.2 7.3 %collective-permute-start = (f32[896,128]{1,0:T(8,128)S(1)}, f32[896,128]{1,0:T(8,128)}, u32[]{:S(2)}, u32[]{:S(2)}) collective-permute-start(f32[896,128]{1,0:T(8,128)S(1)} %get-tuple-element.16), channel_id=1, source_target_pairs={{0,0},{1,16},{2,2},{3,18},{4,4},{5,20},{6,6},{7,22},{8,8},{9,24},{... | collective-permute-start | bytes 1376264 | tf_op jit(solution)/shard_map/ppermute | solution.py:221
  2.6 16.4 %collective-permute-start.3 = (f32[896,128]{1,0:T(8,128)S(1)}, f32[896,128]{1,0:T(8,128)}, u32[]{:S(2)}, u32[]{:S(2)}) collective-permute-start(f32[896,128]{1,0:T(8,128)S(1)} %get-tuple-element.15), channel_id=1, source_target_pairs={{0,16},{1,0},{2,18},{3,2},{4,20},{5,4},{6,22},{7,6},{8,24},{9,8},{... | collective-permute-start | bytes 1376264 | tf_op jit(solution)/shard_map/ppermute | solution.py:221
  8.5 22.8 %collective-permute-start.14 = (f32[896,128]{1,0:T(8,128)}, f32[896,128]{1,0:T(8,128)S(1)}, u32[]{:S(2)}, u32[]{:S(2)}) collective-permute-start(f32[896,128]{1,0:T(8,128)} %collective-permute-done.refs_0_.refs_4_), channel_id=1, source_target_pairs={{0,2},{2,0},{4,6},{6,4},{8,10},{10,8},{12,14},{14,12},{16,18},{18,... | collective-permute-start | bytes 1376264 | tf_op jit(solution)/shard_map/ppermute | solution.py:212
  19.0 13.1 %collective-permute-start.15 = (f32[896,128]{1,0:T(8,128)}, f32[896,128]{1,0:T(8,128)S(1)}, u32[]{:S(2)}, u32[]{:S(2)}) collective-permute-start(f32[896,128]{1,0:T(8,128)} %collective-permute-done.3.refs_2_.refs_6_), channel_id=1, source_target_pairs={{0,2},{2,0},{4,6},{6,4},{8,10},{10,8},{12,14},{14,12},{16,18},{18,... | collective-permute-start | bytes 1376264 | tf_op jit(solution)/shard_map/ppermute | solution.py:212
  19.0 16.8 %collective-permute-start.10 = (f32[896,128]{1,0:T(8,128)}, f32[896,128]{1,0:T(8,128)S(1)}, u32[]{:S(2)}, u32[]{:S(2)}) collective-permute-start(f32[896,128]{1,0:T(8,128)} %collective-permute-done.refs_0_.refs_4_), channel_id=1, source_target_pairs={{0,4},{2,6},{4,0},{6,2},{8,12},{10,14},{12,8},{14,10},{16,20},{18,... | collective-permute-start | bytes 1376264 | tf_op jit(solution)/shard_map/ppermute | solution.py:212
  20.6 23.2 %collective-permute-start.12 = (f32[896,128]{1,0:T(8,128)}, f32[896,128]{1,0:T(8,128)S(1)}, u32[]{:S(2)}, u32[]{:S(2)}) collective-permute-start(f32[896,128]{1,0:T(8,128)} %collective-permute-done.3.refs_2_.refs_6_), channel_id=1, source_target_pairs={{0,4},{2,6},{4,0},{6,2},{8,12},{10,14},{12,8},{14,10},{16,20},{18,... | collective-permute-start | bytes 1376264 | tf_op jit(solution)/shard_map/ppermute | solution.py:212
  21.1 22.7 %collective-permute-start.6 = (f32[896,128]{1,0:T(8,128)}, f32[896,128]{1,0:T(8,128)S(1)}, u32[]{:S(2)}, u32[]{:S(2)}) collective-permute-start(f32[896,128]{1,0:T(8,128)} %collective-permute-done.refs_0_.refs_4_), channel_id=1, source_target_pairs={{0,8},{2,10},{4,12},{6,14},{8,0},{10,2},{12,4},{14,6},{16,24},{18,... | collective-permute-start | bytes 1376264 | tf_op jit(solution)/shard_map/ppermute | solution.py:212
  31.3 0.8 copy-start.1
  32.1 20.6 %collective-permute-start.8 = (f32[896,128]{1,0:T(8,128)}, f32[896,128]{1,0:T(8,128)S(1)}, u32[]{:S(2)}, u32[]{:S(2)}) collective-permute-start(f32[896,128]{1,0:T(8,128)} %collective-permute-done.3.refs_2_.refs_6_), channel_id=1, source_target_pairs={{0,8},{2,10},{4,12},{6,14},{8,0},{10,2},{12,4},{14,6},{16,24},{18,... | collective-permute-start | bytes 1376264 | tf_op jit(solution)/shard_map/ppermute | solution.py:212
  32.1 0.8 copy-start.3
  32.9 30.6 %collective-permute-start.1 = (f32[896,128]{1,0:T(8,128)}, f32[896,128]{1,0:T(8,128)S(1)}, u32[]{:S(2)}, u32[]{:S(2)}) collective-permute-start(f32[896,128]{1,0:T(8,128)} %collective-permute-done.refs_0_.refs_4_), channel_id=1, source_target_pairs={{0,12},{2,14},{4,8},{6,10},{8,4},{10,6},{12,0},{14,2},{16,28},{18,... | collective-permute-start | bytes 1376264 | tf_op jit(solution)/shard_map/ppermute | solution.py:212
  35.9 36.7 %collective-permute-start.4 = (f32[896,128]{1,0:T(8,128)}, f32[896,128]{1,0:T(8,128)S(1)}, u32[]{:S(2)}, u32[]{:S(2)}) collective-permute-start(f32[896,128]{1,0:T(8,128)} %collective-permute-done.3.refs_2_.refs_6_), channel_id=1, source_target_pairs={{0,12},{2,14},{4,8},{6,10},{8,4},{10,6},{12,0},{14,2},{16,28},{18,... | collective-permute-start | bytes 1376264 | tf_op jit(solution)/shard_map/ppermute | solution.py:212
  43.8 28.8 %collective-permute-start.11 = (f32[896,128]{1,0:T(8,128)S(1)}, f32[896,128]{1,0:T(8,128)S(1)}, u32[]{:S(2)}, u32[]{:S(2)}) collective-permute-start(f32[896,128]{1,0:T(8,128)S(1)} %collective-permute-done.10.refs_0_.refs_4_), channel_id=1, source_target_pairs={{0,2},{2,0},{4,6},{6,4},{8,10},{10,8},{12,14},{14,12},{16,18},{18,... | collective-permute-start | bytes 1376264 | tf_op jit(solution)/shard_map/ppermute | solution.py:212
  43.8 29.3 %collective-permute-start.13 = (f32[896,128]{1,0:T(8,128)S(1)}, f32[896,128]{1,0:T(8,128)}, u32[]{:S(2)}, u32[]{:S(2)}) collective-permute-start(f32[896,128]{1,0:T(8,128)S(1)} %collective-permute-done.12.refs_2_.refs_6_), channel_id=1, source_target_pairs={{0,2},{2,0},{4,6},{6,4},{8,10},{10,8},{12,14},{14,12},{16,18},{18,... | collective-permute-start | bytes 1376264 | tf_op jit(solution)/shard_map/ppermute | solution.py:212
  52.7 26.3 %collective-permute-start.7 = (f32[896,128]{1,0:T(8,128)S(1)}, f32[896,128]{1,0:T(8,128)S(1)}, u32[]{:S(2)}, u32[]{:S(2)}) collective-permute-start(f32[896,128]{1,0:T(8,128)S(1)} %collective-permute-done.6.refs_0_.refs_4_), channel_id=1, source_target_pairs={{0,2},{2,0},{4,6},{6,4},{8,10},{10,8},{12,14},{14,12},{16,18},{18,... | collective-permute-start | bytes 1376264 | tf_op jit(solution)/shard_map/ppermute | solution.py:212
  63.5 15.5 %collective-permute-start.9 = (f32[896,128]{1,0:T(8,128)S(1)}, f32[896,128]{1,0:T(8,128)S(1)}, u32[]{:S(2)}, u32[]{:S(2)}) collective-permute-start(f32[896,128]{1,0:T(8,128)S(1)} %collective-permute-done.8.refs_2_.refs_6_), channel_id=1, source_target_pairs={{0,2},{2,0},{4,6},{6,4},{8,10},{10,8},{12,14},{14,12},{16,18},{18,... | collective-permute-start | bytes 1376264 | tf_op jit(solution)/shard_map/ppermute | solution.py:212
  63.5 1.0 copy-start.2
  64.5 1.0 copy-start.4
  71.6 13.3 %copy-start = (f32[2,896,128]{2,1,0:T(8,128)S(1)}, f32[2,896,128]{2,1,0:T(8,128)}, u32[]{:S(2)}) copy-start(f32[2,896,128]{2,1,0:T(8,128)} %own.1) | copy-start | bytes 2752516
  72.6 12.2 %collective-permute-start.2 = (f32[896,128]{1,0:T(8,128)S(1)}, f32[896,128]{1,0:T(8,128)S(1)}, u32[]{:S(2)}, u32[]{:S(2)}) collective-permute-start(f32[896,128]{1,0:T(8,128)S(1)} %collective-permute-done.1.refs_0_.refs_4_), channel_id=1, source_target_pairs={{0,2},{2,0},{4,6},{6,4},{8,10},{10,8},{12,14},{14,12},{16,18},{18,... | collective-permute-start | bytes 1376264 | tf_op jit(solution)/shard_map/ppermute | solution.py:212
  72.6 12.2 %collective-permute-start.5 = (f32[896,128]{1,0:T(8,128)S(1)}, f32[896,128]{1,0:T(8,128)S(1)}, u32[]{:S(2)}, u32[]{:S(2)}) collective-permute-start(f32[896,128]{1,0:T(8,128)S(1)} %collective-permute-done.4.refs_2_.refs_6_), channel_id=1, source_target_pairs={{0,2},{2,0},{4,6},{6,4},{8,10},{10,8},{12,14},{14,12},{16,18},{18,... | collective-permute-start | bytes 1376264 | tf_op jit(solution)/shard_map/ppermute | solution.py:212
  79.0 16.9 %copy-start.7 = (f32[4]{0:T(128)S(1)}, f32[4]{0:T(128)}, u32[]{:S(2)}) copy-start(f32[4]{0:T(128)} %constant.36.clone) | copy-start | bytes 52
  79.0 77.6 %copy-start.6 = (f32[2,128,128]{2,1,0:T(8,128)S(1)}, f32[2,128,128]{2,1,0:T(8,128)}, u32[]{:S(2)}) copy-start(f32[2,128,128]{2,1,0:T(8,128)} %factors.1) | copy-start | bytes 393220
  84.8 85.1 %copy-start.5 = (f32[896,128]{1,0:T(8,128)S(1)}, f32[896,128]{1,0:T(8,128)}, u32[]{:S(2)}) copy-start(f32[896,128]{1,0:T(8,128)} %copy-done.3) | copy-start | bytes 1376260
  96.0 10.5 %collective-permute-start.18 = (f32[4,128,128]{2,1,0:T(8,128)S(1)}, f32[4,128,128]{2,1,0:T(8,128)S(1)}, u32[]{:S(2)}, u32[]{:S(2)}) collective-permute-start(f32[4,128,128]{2,1,0:T(8,128)S(1)} %broadcast_multiply_fusion), channel_id=1, source_target_pairs={{0,1},{1,0},{2,3},{3,2},{4,5},{5,4},{6,7},{7,6},{8,9},{9,8},{10,11... | collective-permute-start | bytes 786440 | tf_op jit(solution)/shard_map/ppermute | solution.py:212
  106.6 1.9 collective-permute-start.19
  106.7 12.9 %collective-permute-start.16 = (f32[896,128]{1,0:T(8,128)S(1)}, f32[896,128]{1,0:T(8,128)S(1)}, u32[]{:S(2)}, u32[]{:S(2)}) collective-permute-start(f32[896,128]{1,0:T(8,128)S(1)} %get-tuple-element.11), channel_id=1, source_target_pairs={{0,1},{1,0},{2,3},{3,2},{4,5},{5,4},{6,7},{7,6},{8,9},{9,8},{10,11... | collective-permute-start | bytes 1376264 | tf_op jit(solution)/shard_map/ppermute | solution.py:212
  108.5 8.4 %collective-permute-start.20 = (f32[4,128,128]{2,1,0:T(8,128)S(1)}, f32[4,128,128]{2,1,0:T(8,128)S(1)}, u32[]{:S(2)}, u32[]{:S(2)}) collective-permute-start(f32[4,128,128]{2,1,0:T(8,128)S(1)} %add.26), channel_id=1, source_target_pairs={{0,4},{2,6},{4,0},{6,2},{8,12},{10,14},{12,8},{14,10},{16,20},{18,... | collective-permute-start | bytes 786440 | tf_op jit(solution)/shard_map/ppermute | solution.py:212
  117.0 8.9 %collective-permute-start.21 = (f32[4,128,128]{2,1,0:T(8,128)S(1)}, f32[4,128,128]{2,1,0:T(8,128)S(1)}, u32[]{:S(2)}, u32[]{:S(2)}) collective-permute-start(f32[4,128,128]{2,1,0:T(8,128)S(1)} %add.27), channel_id=1, source_target_pairs={{0,8},{2,10},{4,12},{6,14},{8,0},{10,2},{12,4},{14,6},{16,24},{18,... | collective-permute-start | bytes 786440 | tf_op jit(solution)/shard_map/ppermute | solution.py:212
  119.7 7.9 %collective-permute-start.23 = (f32[896,128]{1,0:T(8,128)S(1)}, f32[896,128]{1,0:T(8,128)S(1)}, u32[]{:S(2)}, u32[]{:S(2)}) collective-permute-start(f32[896,128]{1,0:T(8,128)S(1)} %add.24.mine), channel_id=1, source_target_pairs={{0,0},{1,16},{2,2},{3,18},{4,4},{5,20},{6,6},{7,22},{8,8},{9,24},{... | collective-permute-start | bytes 1376264 | tf_op jit(solution)/shard_map/ppermute | solution.py:221
  120.4 16.5 %collective-permute-start.26 = (f32[896,128]{1,0:T(8,128)S(1)}, f32[896,128]{1,0:T(8,128)S(1)}, u32[]{:S(2)}, u32[]{:S(2)}) collective-permute-start(f32[896,128]{1,0:T(8,128)S(1)} %add.24.mine), channel_id=1, source_target_pairs={{0,16},{1,0},{2,18},{3,2},{4,20},{5,4},{6,22},{7,6},{8,24},{9,8},{... | collective-permute-start | bytes 1376264 | tf_op jit(solution)/shard_map/ppermute | solution.py:221
  125.9 18.5 %collective-permute-start.17 = (f32[896,128]{1,0:T(8,128)S(1)}, f32[896,128]{1,0:T(8,128)S(1)}, u32[]{:S(2)}, u32[]{:S(2)}) collective-permute-start(f32[896,128]{1,0:T(8,128)S(1)} %add.24.mine), channel_id=1, source_target_pairs={{0,1},{1,0},{2,3},{3,2},{4,5},{5,4},{6,7},{7,6},{8,9},{9,8},{10,11... | collective-permute-start | bytes 1376264 | tf_op jit(solution)/shard_map/ppermute | solution.py:212
  126.0 30.5 %collective-permute-start.22 = (f32[4,128,128]{2,1,0:T(8,128)S(1)}, f32[4,128,128]{2,1,0:T(8,128)S(1)}, u32[]{:S(2)}, u32[]{:S(2)}) collective-permute-start(f32[4,128,128]{2,1,0:T(8,128)S(1)} %add.28), channel_id=1, source_target_pairs={{0,16},{2,18},{4,20},{6,22},{8,24},{10,26},{12,28},{14,30},{16,0},... | collective-permute-start | bytes 786440 | tf_op jit(solution)/shard_map/ppermute | solution.py:212
  127.6 35.3 %collective-permute-start.37 = (f32[896,128]{1,0:T(8,128)S(1)}, f32[896,128]{1,0:T(8,128)S(1)}, u32[]{:S(2)}, u32[]{:S(2)}) collective-permute-start(f32[896,128]{1,0:T(8,128)S(1)} %collective-permute-done.23.refs_0_), channel_id=1, source_target_pairs={{0,2},{2,0},{4,6},{6,4},{8,10},{10,8},{12,14},{14,12},{16,18},{18,... | collective-permute-start | bytes 1376264 | tf_op jit(solution)/shard_map/ppermute | solution.py:212
  136.9 28.0 %collective-permute-start.38 = (f32[896,128]{1,0:T(8,128)S(1)}, f32[896,128]{1,0:T(8,128)S(1)}, u32[]{:S(2)}, u32[]{:S(2)}) collective-permute-start(f32[896,128]{1,0:T(8,128)S(1)} %collective-permute-done.26.refs_2_), channel_id=1, source_target_pairs={{0,2},{2,0},{4,6},{6,4},{8,10},{10,8},{12,14},{14,12},{16,18},{18,... | collective-permute-start | bytes 1376264 | tf_op jit(solution)/shard_map/ppermute | solution.py:212
  136.9 28.0 %collective-permute-start.33 = (f32[896,128]{1,0:T(8,128)S(1)}, f32[896,128]{1,0:T(8,128)S(1)}, u32[]{:S(2)}, u32[]{:S(2)}) collective-permute-start(f32[896,128]{1,0:T(8,128)S(1)} %collective-permute-done.23.refs_0_), channel_id=1, source_target_pairs={{0,4},{2,6},{4,0},{6,2},{8,12},{10,14},{12,8},{14,10},{16,20},{18,... | collective-permute-start | bytes 1376264 | tf_op jit(solution)/shard_map/ppermute | solution.py:212
  144.5 23.3 %collective-permute-start.35 = (f32[896,128]{1,0:T(8,128)S(1)}, f32[896,128]{1,0:T(8,128)S(1)}, u32[]{:S(2)}, u32[]{:S(2)}) collective-permute-start(f32[896,128]{1,0:T(8,128)S(1)} %collective-permute-done.26.refs_2_), channel_id=1, source_target_pairs={{0,4},{2,6},{4,0},{6,2},{8,12},{10,14},{12,8},{14,10},{16,20},{18,... | collective-permute-start | bytes 1376264 | tf_op jit(solution)/shard_map/ppermute | solution.py:212
  156.5 13.4 %collective-permute-start.29 = (f32[896,128]{1,0:T(8,128)S(1)}, f32[896,128]{1,0:T(8,128)S(1)}, u32[]{:S(2)}, u32[]{:S(2)}) collective-permute-start(f32[896,128]{1,0:T(8,128)S(1)} %collective-permute-done.23.refs_0_), channel_id=1, source_target_pairs={{0,8},{2,10},{4,12},{6,14},{8,0},{10,2},{12,4},{14,6},{16,24},{18,... | collective-permute-start | bytes 1376264 | tf_op jit(solution)/shard_map/ppermute | solution.py:212
  162.9 17.9 %collective-permute-start.31 = (f32[896,128]{1,0:T(8,128)S(1)}, f32[896,128]{1,0:T(8,128)S(1)}, u32[]{:S(2)}, u32[]{:S(2)}) collective-permute-start(f32[896,128]{1,0:T(8,128)S(1)} %collective-permute-done.26.refs_2_), channel_id=1, source_target_pairs={{0,8},{2,10},{4,12},{6,14},{8,0},{10,2},{12,4},{14,6},{16,24},{18,... | collective-permute-start | bytes 1376264 | tf_op jit(solution)/shard_map/ppermute | solution.py:212
  164.9 24.6 %collective-permute-start.24 = (f32[896,128]{1,0:T(8,128)S(1)}, f32[896,128]{1,0:T(8,128)S(1)}, u32[]{:S(2)}, u32[]{:S(2)}) collective-permute-start(f32[896,128]{1,0:T(8,128)S(1)} %collective-permute-done.23.refs_0_), channel_id=1, source_target_pairs={{0,12},{2,14},{4,8},{6,10},{8,4},{10,6},{12,0},{14,2},{16,28},{18,... | collective-permute-start | bytes 1376264 | tf_op jit(solution)/shard_map/ppermute | solution.py:212
  164.9 33.5 %collective-permute-start.27 = (f32[896,128]{1,0:T(8,128)S(1)}, f32[896,128]{1,0:T(8,128)S(1)}, u32[]{:S(2)}, u32[]{:S(2)}) collective-permute-start(f32[896,128]{1,0:T(8,128)S(1)} %collective-permute-done.26.refs_2_), channel_id=1, source_target_pairs={{0,12},{2,14},{4,8},{6,10},{8,4},{10,6},{12,0},{14,2},{16,28},{18,... | collective-permute-start | bytes 1376264 | tf_op jit(solution)/shard_map/ppermute | solution.py:212
  167.8 30.6 %collective-permute-start.34 = (f32[896,128]{1,0:T(8,128)S(1)}, f32[896,128]{1,0:T(8,128)S(1)}, u32[]{:S(2)}, u32[]{:S(2)}) collective-permute-start(f32[896,128]{1,0:T(8,128)S(1)} %collective-permute-done.33.refs_0_), channel_id=1, source_target_pairs={{0,2},{2,0},{4,6},{6,4},{8,10},{10,8},{12,14},{14,12},{16,18},{18,... | collective-permute-start | bytes 1376264 | tf_op jit(solution)/shard_map/ppermute | solution.py:212
  169.9 29.0 %collective-permute-start.36 = (f32[896,128]{1,0:T(8,128)S(1)}, f32[896,128]{1,0:T(8,128)S(1)}, u32[]{:S(2)}, u32[]{:S(2)}) collective-permute-start(f32[896,128]{1,0:T(8,128)S(1)} %collective-permute-done.35.refs_2_), channel_id=1, source_target_pairs={{0,2},{2,0},{4,6},{6,4},{8,10},{10,8},{12,14},{14,12},{16,18},{18,... | collective-permute-start | bytes 1376264 | tf_op jit(solution)/shard_map/ppermute | solution.py:212
  180.8 28.8 %collective-permute-start.30 = (f32[896,128]{1,0:T(8,128)S(1)}, f32[896,128]{1,0:T(8,128)S(1)}, u32[]{:S(2)}, u32[]{:S(2)}) collective-permute-start(f32[896,128]{1,0:T(8,128)S(1)} %collective-permute-done.29.refs_0_), channel_id=1, source_target_pairs={{0,2},{2,0},{4,6},{6,4},{8,10},{10,8},{12,14},{14,12},{16,18},{18,... | collective-permute-start | bytes 1376264 | tf_op jit(solution)/shard_map/ppermute | solution.py:212
  189.5 20.1 %collective-permute-start.32 = (f32[896,128]{1,0:T(8,128)S(1)}, f32[896,128]{1,0:T(8,128)S(1)}, u32[]{:S(2)}, u32[]{:S(2)}) collective-permute-start(f32[896,128]{1,0:T(8,128)S(1)} %collective-permute-done.31.refs_2_), channel_id=1, source_target_pairs={{0,2},{2,0},{4,6},{6,4},{8,10},{10,8},{12,14},{14,12},{16,18},{18,... | collective-permute-start | bytes 1376264 | tf_op jit(solution)/shard_map/ppermute | solution.py:212
  198.4 21.9 %collective-permute-start.25 = (f32[896,128]{1,0:T(8,128)S(1)}, f32[896,128]{1,0:T(8,128)S(1)}, u32[]{:S(2)}, u32[]{:S(2)}) collective-permute-start(f32[896,128]{1,0:T(8,128)S(1)} %collective-permute-done.24.refs_0_), channel_id=1, source_target_pairs={{0,2},{2,0},{4,6},{6,4},{8,10},{10,8},{12,14},{14,12},{16,18},{18,... | collective-permute-start | bytes 1376264 | tf_op jit(solution)/shard_map/ppermute | solution.py:212
  198.4 21.9 %collective-permute-start.28 = (f32[896,128]{1,0:T(8,128)S(1)}, f32[896,128]{1,0:T(8,128)S(1)}, u32[]{:S(2)}, u32[]{:S(2)}) collective-permute-start(f32[896,128]{1,0:T(8,128)S(1)} %collective-permute-done.27.refs_2_), channel_id=1, source_target_pairs={{0,2},{2,0},{4,6},{6,4},{8,10},{10,8},{12,14},{14,12},{16,18},{18,... | collective-permute-start | bytes 1376264 | tf_op jit(solution)/shard_map/ppermute | solution.py:212

commit v2 on v1

v2 whole, which is shorter than its diff:
```python
import functools

import jax
import jax.numpy as jnp
from jax import lax
from jax.experimental import pallas as pl
from jax.experimental.pallas import tpu as pltpu
from jax.sharding import PartitionSpec as P

F32 = jnp.float32
BF16 = jnp.bfloat16
PLAIN = (((1,), (0,)), ((), ()))
BOTH_LAST = (((1,), (1,)), ((), ()))
BOTH_FIRST = (((0,), (0,)), ((), ()))
VMEM_BYTES = 48 * 1024 * 1024
GATES = (True, True, False, False)
FORWARD = ((0,), (2, 4), (6,))
UPDATE = ((0,), (2, 4), (6,))


def split(values):
    high = values.astype(BF16)
    return high, (values - high.astype(F32)).astype(BF16)


def product(former, latter, dims=PLAIN):
    dot = functools.partial(lax.dot_general, dimension_numbers=dims, preferred_element_type=F32)
    return dot(former[0], latter[0]) + (dot(former[0], latter[1]) + dot(former[1], latter[0]))


def small(former, latter, dims=PLAIN):
    return lax.dot_general(
        former, latter, dims, precision=lax.Precision.HIGHEST, preferred_element_type=F32
    )


def in_order(place, joined, blocks):
    depth, width = blocks[0].shape
    for number, block in enumerate(blocks):
        turn = (place[0] + number) % 2
        rows = pl.ds(pl.multiple_of(turn * depth, depth), depth)
        lanes = slice(number // 2 * width, (number // 2 + 1) * width)
        joined[0][rows, lanes], joined[1][rows, lanes] = split(block[...])


def each_pair(place, joined, blocks, count):
    size = len(blocks) // count
    for turn in range(count):
        now = jnp.logical_and(pl.program_id(0) == turn, pl.program_id(1) == 0)
        pl.when(now)(
            functools.partial(in_order, place, joined, blocks[turn * size : (turn + 1) * size])
        )


def forward_kernel(first, last, count, share, place, block, *refs):
    blocks, refs, joined = refs[: 4 * count], refs[4 * count : -2], refs[-2:]
    pair, step = pl.program_id(0), pl.program_id(1)
    each_pair(place, joined, blocks, count)
    tile = block.shape[0]
    rows = pl.ds(pl.multiple_of(step * tile, tile), tile)
    found = product(split(block[...]), (joined[0][...], joined[1][...]))
    if first:
        own, total, token, high, low, cross = refs
    elif last:
        before, high, low, cross, kept, sent, inner, total = refs
    else:
        before, total, token = refs
    if not last:
        token[...] = jnp.zeros_like(token)

    @pl.when(pair == 0)
    def _():
        total[rows] = found if first else before[rows] + found

    @pl.when(pair != 0)
    def _():
        total[rows] += found

    if first:
        width = own.shape[2]

        @pl.when(pair == 0)
        def _():
            turned = split(jnp.concatenate([own[0, rows].T, own[1, rows].T], axis=0))
            high[step], low[step] = turned
            other = share * product((turned[0][:width], turned[1][:width]), split(own[1, rows]))
            cross[...] = jnp.where(step == 0, 0.0, cross[...]) + other

    if last:
        width = kept.shape[1]

        @pl.when(pair == count - 1)
        def _():
            strip = total[rows]
            one, two = strip[:, :width], strip[:, width:]
            swap = place[1] != 0
            kept[rows] = jnp.where(swap, two, one)
            sent[rows] = jnp.where(swap, one, two)

            @pl.when(step == 0)
            def _():
                inner[...] = jnp.zeros_like(inner)
                inner[3] = cross[...]

            sums = product((high[step], low[step]), split(strip))
            inner[0] += sums[:width, :width]
            inner[1] += sums[width:, :width]
            inner[2] += sums[width:, width:]


def whole(shape):
    return pl.BlockSpec(shape, lambda pair, step, place: (0,) * len(shape))


def forward_step(place, matrix, slots, blocks, own, before, last, share):
    rows = matrix.shape[0]
    depth, width = blocks[0].shape
    tile, count, start = rows // 2, len(slots), slots[0]
    first = before is None
    operands = [matrix, *blocks]
    specs = [
        pl.BlockSpec(
            (tile, 2 * depth),
            lambda pair, step, place: (step, (place[0] ^ (start + 2 * pair)) // 2),
        )
    ]
    total = jax.ShapeDtypeStruct((rows, 2 * width), F32)
    outs, scratch = [total, jax.ShapeDtypeStruct((8, 128), jnp.int32)], []
    if first:
        operands.append(own)
        outs += [jax.ShapeDtypeStruct((2, 2 * width, tile), BF16)] * 2
        outs += [jax.ShapeDtypeStruct((width, width), F32)]
    else:
        operands.append(before[0])
    if last:
        operands += before[2:]
        part = jax.ShapeDtypeStruct((rows, width), F32)
        outs, scratch = [part, part, jax.ShapeDtypeStruct((4, width, width), F32)], [total]
    specs += [whole(operand.shape) for operand in operands[1:]]
    found = pl.pallas_call(
        functools.partial(forward_kernel, first, last, count, share),
        grid_spec=pltpu.PrefetchScalarGridSpec(
            num_scalar_prefetch=1,
            grid=(count, 2),
            in_specs=specs,
            out_specs=[whole(out.shape) for out in outs],
            scratch_shapes=[pltpu.VMEM(one.shape, one.dtype) for one in scratch]
            + [pltpu.VMEM((2 * depth, 2 * width), BF16)] * 2,
        ),
        out_shape=outs,
        compiler_params=pltpu.CompilerParams(vmem_limit_bytes=VMEM_BYTES),
        cost_estimate=pl.CostEstimate(
            flops=6 * rows * depth * 4 * width * count,
            bytes_accessed=8 * rows * depth * count,
            transcendentals=0,
        ),
    )(place, *operands)
    return list(found) if first or last else list(found) + before[2:]


def mix_kernel(place, own, mine, other, inner, factors, high, low):
    one, two = factors[0], factors[1]
    gram_one, cross_yv, gram_old, cross_vv = inner[0], inner[1], inner[2], inner[3]
    correct_one = small(small(one, gram_one, BOTH_FIRST), one)
    cross_wv = small(one, cross_yv, (((0,), (1,)), ((), ()))) - 0.5 * small(
        correct_one, cross_vv, BOTH_FIRST
    )
    drop = small(cross_vv, cross_wv, BOTH_FIRST)
    gram_two = gram_old - drop - small(cross_wv, cross_vv, BOTH_FIRST)
    correct_two = small(small(two, gram_two, BOTH_FIRST), two)
    mixed = -small(small(one, cross_vv), two)
    edge = small(0.5 * small(correct_one, cross_vv) - cross_wv, two)
    swap = place[1] != 0
    y_one = split(jnp.where(swap, other[...], mine[...]))
    y_two = split(jnp.where(swap, mine[...], other[...]))
    v_one, v_two = split(own[0]), split(own[1])
    correct_one = 0.5 * (correct_one + correct_one.T)
    correct_two = 0.5 * (correct_two + correct_two.T)
    one, two, mixed, edge = split(one), split(two), split(mixed), split(edge)
    p_one = product(v_one, one, BOTH_LAST) + product(v_two, mixed, BOTH_LAST)
    p_two = product(v_two, two, BOTH_LAST)
    q_one = product(y_one, one) - product(v_one, split(correct_one)) + product(v_two, edge, BOTH_LAST)
    q_two = product(y_one, mixed) + product(y_two, two) + product(v_one, edge)
    q_two = q_two - product(v_two, split(correct_two))
    turn = place[2] != 0
    parts = (jnp.where(turn, p_two, p_one), jnp.where(turn, p_one, p_two), q_one, q_two)
    width = own.shape[2]
    for number, part in enumerate(parts):
        lanes = slice(number * width, (number + 1) * width)
        high[:, lanes], low[:, lanes] = split(part)


def mix(place, own, *operands):
    _, rows, width = own.shape
    side = jax.ShapeDtypeStruct((rows, 4 * width), BF16)
    vmem = pl.BlockSpec(memory_space=pltpu.VMEM)
    return pl.pallas_call(
        mix_kernel,
        in_specs=[pl.BlockSpec(memory_space=pltpu.SMEM)] + [vmem] * (1 + len(operands)),
        out_specs=[vmem, vmem],
        out_shape=[side, side],
        compiler_params=pltpu.CompilerParams(vmem_limit_bytes=VMEM_BYTES),
        cost_estimate=pl.CostEstimate(
            flops=12 * rows * width * 8 * width, bytes_accessed=32 * rows * width, transcendentals=0
        ),
    )(place, own, *operands)


def update_kernel(count, place, block, high, low, *refs):
    blocks, out, token, joined = refs[: 8 * count], refs[-4], refs[-3], refs[-2:]
    token[...] = jnp.zeros_like(token)
    each_pair(place, joined, blocks, count)
    tile = block.shape[0]
    rows = pl.ds(pl.multiple_of(pl.program_id(1) * tile, tile), tile)
    side = (joined[0][...], joined[1][...])
    out[...] = block[...] - product((high[rows], low[rows]), side, BOTH_LAST)


def update_step(place, matrix, slots, sides, blocks, before):
    rows = matrix.shape[0]
    depth, width = blocks[0].shape
    tile, count, start = rows // 2, len(slots), slots[0]
    block = pl.BlockSpec(
        (tile, 2 * depth),
        lambda pair, step, place: (step, (place[0] ^ (start + 2 * pair)) // 2),
    )
    operands = [matrix, *sides, *blocks]
    specs = [block] + [whole(operand.shape) for operand in operands[1:]]
    aliases = {}
    if before is not None:
        aliases = {1 + len(operands): 0}
        operands.append(before[0])
        specs.append(pl.BlockSpec(memory_space=pl.ANY))
    return pl.pallas_call(
        functools.partial(update_kernel, count),
        grid_spec=pltpu.PrefetchScalarGridSpec(
            num_scalar_prefetch=1,
            grid=(count, 2),
            in_specs=specs,
            out_specs=[block, whole((8, 128))],
            scratch_shapes=[pltpu.VMEM((2 * depth, 4 * width), BF16)] * 2,
        ),
        out_shape=[
            jax.ShapeDtypeStruct(matrix.shape, F32),
            jax.ShapeDtypeStruct((8, 128), jnp.int32),
        ],
        input_output_aliases=aliases,
        compiler_params=pltpu.CompilerParams(vmem_limit_bytes=VMEM_BYTES),
        cost_estimate=pl.CostEstimate(
            flops=6 * rows * depth * 8 * width * count,
            bytes_accessed=16 * rows * depth * count,
            transcendentals=0,
        ),
    )(place, *operands)


def steer(values, cost):
    anywhere = pl.BlockSpec(memory_space=pl.ANY)
    return pl.pallas_call(
        lambda *refs: None,
        in_specs=[anywhere] * len(values),
        out_specs=[anywhere] * len(values),
        out_shape=[jax.ShapeDtypeStruct(part.shape, part.dtype) for part in values],
        input_output_aliases={n: n for n in range(len(values))},
        cost_estimate=pl.CostEstimate(flops=int(cost * 1e9), bytes_accessed=0, transcendentals=0),
    )(*values)


def after(token, values):
    return jnp.where(token[0, 0] != 0, jnp.zeros_like(values), values)


def solution(mesh):
    row_count, col_count = mesh.shape["row"], mesh.shape["col"]
    group = row_count // col_count
    everyone = row_count * col_count
    assert group * col_count == row_count and group >= 4 and everyone & (everyone - 1) == 0
    halves = col_count == 2

    def flip(values, mask):
        return lax.ppermute(values, ("row", "col"), [(n, n ^ mask) for n in range(everyone)])

    def flip_row(values, mask):
        return flip(values, mask * col_count)

    def transpose(values, turn):
        pairs = []
        for s in range(col_count):
            for b in range(group):
                for j in range(col_count):
                    source = (s * group + b) * col_count + j
                    pairs.append((source, ((j - turn) % col_count * group + b) * col_count + s))
        return lax.ppermute(values, ("row", "col"), pairs)

    def spread(own, work, stages, gates):
        found = {0: own}

        def swapped(d, token=None):
            gone = found[d] if token is None else [after(token, part) for part in found[d]]
            return [part for n in range(2) for part in (found[d][n], flip_row(gone[n], 1))]

        if group == 8:
            ahead = flip_row(own[1], 2), flip_row(own[0], 4)
            behind = flip_row(own[0], 2), flip_row(own[1], 4)
            found[2], found[4] = [behind[0], ahead[0]], [ahead[1], behind[1]]
            token = None
            for number, slots in enumerate(stages):
                if 6 in slots:
                    if 6 not in found:
                        found[6] = [flip_row(ahead[1], 2), flip_row(ahead[0], 4)]
                    blocks = [swapped(d, token if gates[1] and d == 6 else None) for d in slots]
                else:
                    blocks = [swapped(d) for d in slots]
                token = work(slots, blocks)
                if number == 0 and gates[0]:
                    gone = [after(token, part) for part in ahead]
                    found[6] = [flip_row(gone[1], 2), flip_row(gone[0], 4)]
            return
        for d in range(2, group, 2):
            found[d] = [flip_row(part, d) for part in own]
        for d in range(0, group, 2):
            work((d,), [swapped(d)])

    def shards(matrix, panels, factors):
        row, col = lax.axis_index("row"), lax.axis_index("col")
        zero = jnp.zeros_like(row)
        place = jnp.stack(
            [row % group, col if halves else zero, row // group if halves else zero]
        ).astype(jnp.int32)
        vectors, sums, outs = {}, [None], [None]

        def forward(slots, blocks):
            vectors.update(zip(slots, blocks))
            sums[0] = forward_step(
                place,
                matrix,
                slots,
                sum(blocks, []),
                panels,
                sums[0],
                slots[-1] + 2 == group,
                1 / col_count,
            )
            return sums[0][1]

        spread([transpose(panels[0], 0), transpose(panels[1], 1)], forward, FORWARD, GATES[:2])
        kept, sent, inner = sums[0]
        if halves:
            mine = kept + flip(sent, 1)
            other = flip(mine, 1)
            blocks = [transpose(mine, 0), transpose(mine, 1)]
        else:
            mine, other = lax.psum((kept, sent), "col")
            blocks = [transpose(mine, 0), transpose(other, 1)]
        blocks = steer(blocks, 40)
        masks = [1 << n for n in range(everyone.bit_length() - 1)]
        for mask in masks[:2]:
            inner = inner + flip(inner, mask)
        masks = masks[2:]
        while masks:
            now, masks = masks[:2], masks[2:]
            reach = now + [now[0] ^ now[1]] if len(now) == 2 else now
            inner = sum([flip(inner, mask) for mask in reach], inner)
        sides = mix(place, panels, mine, other, inner, factors)

        def update(slots, blocks):
            pairs = sum([block + vectors[slot] for slot, block in zip(slots, blocks)], [])
            outs[0] = update_step(place, matrix, slots, sides, pairs, outs[0])
            return outs[0][1]

        spread(blocks, update, UPDATE, GATES[2:])
        return outs[0][0]

    placed = (P("row", "col"), P(None, "row", None), P())
    return jax.shard_map(
        shards, mesh=mesh, in_specs=placed, out_specs=P("row", "col"), check_vma=False
    )
```

time: 231 us -> 200 us (0.87)
  waiting for transfers between devices: 94.5 us -> 73.8 us
  Pallas kernels: 77.7 us -> 67.4 us
  starting transfers between devices: 53.2 us -> 45 us
  local copies, waits for them, and re-layouts: 4.81 us -> 7.89 us
  other arithmetic: 0.42 us -> 3.07 us
    ppermute x35 -> x36, waiting for transfers between devices: 74.6 us -> 57.1 us  [flip(): lax.ppermute(values, ('row', 'col'), [(n, n ^ mask) for n in range(everyo...]
    pallas_call x8 -> x7, Pallas kernels: 71.5 us -> 62.5 us  [the longest x3 39.4 us: update_step(): pl.pallas_call(functools.partial(update_kernel, count), grid_spec=pltpu.P...]
    ppermute x35 -> x36, starting transfers between devices: 39.7 us -> 31.2 us  [flip(): lax.ppermute(values, ('row', 'col'), [(n, n ^ mask) for n in range(everyo...]
    ppermute x4, waiting for transfers between devices: 19.9 us -> 16.8 us  [transpose(): return lax.ppermute(values, ('row', 'col'), pairs)]
    add x6 -> x5, other arithmetic: 0.26 us -> 2.86 us  [the longest x2 1.27 us: shards(): inner = sum([flip(inner, mask) for mask in reach], inner)]
    unnamed x16 -> x52, local copies, waits for them, and re-layouts: 3.6 us -> 5.64 us
  transfers between devices with their start and end apart: 39 -> 40, of which waited for: 13 -> 15; matrix products, arithmetic and copies ran while one was open for 0% -> 2% of each run, Pallas kernels for 24% -> 25%
where the time goes in v2:
time: 200 us; the launch traced here: 199 us
  waiting for transfers between devices  73.8 us (37%)
  Pallas kernels  67.4 us (34%)
  starting transfers between devices  45 us (22%)
  local copies, waits for them, and re-layouts  7.89 us (4%)
  other arithmetic  3.07 us (2%)
    ppermute x36, waiting for transfers between devices, flip(): lax.ppermute(values, ('row', 'col'), [(n, n ^ mask) for n in range(everyo...  57.1 us
    pallas_call x3, Pallas kernels, update_step(): pl.pallas_call(functools.partial(update_kernel, count), grid_spec=pltpu.P...  39.4 us
    ppermute x36, starting transfers between devices, flip(): lax.ppermute(values, ('row', 'col'), [(n, n ^ mask) for n in range(everyo...  31.2 us
    pallas_call x3, Pallas kernels, forward_step(): pl.pallas_call(functools.partial(forward_kernel, first, last, count, shar...  23.1 us
    ppermute x4, waiting for transfers between devices, transpose(): return lax.ppermute(values, ('row', 'col'), pairs)  16.8 us
    ppermute x4, starting transfers between devices, transpose(): return lax.ppermute(values, ('row', 'col'), pairs)  13.8 us
    unnamed x52, local copies, waits for them, and re-layouts  5.64 us
    pallas_call x1, Pallas kernels, mix(): pl.pallas_call(mix_kernel, in_specs=[pl.BlockSpec(memory_space=pltpu.SMEM...  4.81 us
  transfers between devices with their start and end apart: 40, of which 15 were waited for; matrix products, arithmetic and copies ran while one was open for 2% of the time, Pallas kernels for 25%

profile of v2, /device:TPU:0, one launch (start us, length us, event | category | flops | bytes accessed | tf_op | source)
XLA Modules:
  0.0 198.9 jit_solution(9127388170124446245)
XLA Ops:
  0.0 1.2 slice_bitcast_fusion
  1.2 0.7 collective-permute-start
  1.9 6.6 %collective-permute-start.2 = (f32[896,128]{1,0:T(8,128)S(1)}, f32[896,128]{1,0:T(8,128)S(1)}, u32[]{:S(2)}, u32[]{:S(2)}) collective-permute-start(f32[896,128]{1,0:T(8,128)S(1)} %get-tuple-element.39), channel_id=1, source_target_pairs={{0,16},{1,0},{2,18},{3,2},{4,20},{5,4},{6,22},{7,6},{8,24},{9,8},{... | collective-permute-start | bytes 1376264 | tf_op jit(solution)/shard_map/ppermute | solution.py:293
  8.5 10.4 %collective-permute-done.2.refs_2_.refs_6_ = f32[896,128]{1,0:T(8,128)S(1)} collective-permute-done((f32[896,128]{1,0:T(8,128)S(1)}, f32[896,128]{1,0:T(8,128)S(1)}, u32[]{:S(2)}, u32[]{:S(2)}) %collective-permute-start.2) | collective-permute-done | bytes 458784 | tf_op jit(solution)/shard_map/ppermute | solution.py:293
  18.9 10.4 %collective-permute-start.4 = (f32[896,128]{1,0:T(8,128)S(1)}, f32[896,128]{1,0:T(8,128)S(1)}, u32[]{:S(2)}, u32[]{:S(2)}) collective-permute-start(f32[896,128]{1,0:T(8,128)S(1)} %collective-permute-done.refs_0_.refs_4_), channel_id=1, source_target_pairs={{0,8},{1,9},{2,10},{3,11},{4,12},{5,13},{6,14},{7,15},{8,0},{9,1},... | collective-permute-start | bytes 1376264 | tf_op jit(solution)/shard_map/ppermute | solution.py:281
  29.3 1.5 collective-permute-start.8
  31.5 1.2 copy-done.4
  32.7 6.1 %shard_map.37 = (f32[896,256]{1,0:T(8,128)S(1)}, s32[8,128]{1,0:T(8,128)S(1)}, bf16[2,256,448]{2,1,0:T(8,128)(2,1)S(1)}, bf16[2,256,448]{2,1,0:T(8,128)(2,1)S(1)}, f32[128,128]{1,0:T(8,128)S(1)}) custom-call(s32[3]{0:T(128)S(1)} %pad_add_fusion.place, f32[896,7168]{1,0:T(8,128)} %block.11, f32[896,128]{1,0:T(8,128)S(1)} %collective-permute-done.refs_0_.refs_4_, ...), custom_call_target="tpu_custom_call" | custom-call | flops 2466250752 | bytes 6422528 | tf_op jit(solution)/shard_map/pallas_call | solution.py:140
  39.9 0.7 collective-permute-done.4.refs_4_.refs_12_
  40.7 2.0 collective-permute-done.8.refs_2_.refs_6_
  42.7 7.6 %collective-permute-done.11.refs_6_.refs_14_ = f32[896,128]{1,0:T(8,128)S(1)} collective-permute-done((f32[896,128]{1,0:T(8,128)S(1)}, f32[896,128]{1,0:T(8,128)S(1)}, u32[]{:S(2)}, u32[]{:S(2)}) %collective-permute-start.11) | collective-permute-done | bytes 458784 | tf_op jit(solution)/shard_map/ppermute | solution.py:281
  50.3 1.5 collective-permute-done.6.refs_0_.refs_4_
  51.8 0.8 collective-permute-start.14
  52.7 1.6 collective-permute-start.5
  54.4 9.7 %shard_map.38 = (f32[896,256]{1,0:T(8,128)S(1)}, s32[8,128]{1,0:T(8,128)S(1)}) custom-call(s32[3]{0:T(128)S(1)} %pad_add_fusion.place, f32[896,7168]{1,0:T(8,128)} %block.11, f32[896,128]{1,0:T(8,128)S(1)} %collective-permute-done.6.refs_0_.refs_4_, f32[896,128]{1,0:T(8,128)S(1)} %collective-permute-done.7.refs_1_.refs_5_, ...), custom_call_target="tpu_custom_call" | custom-call | flops 4932501504 | bytes 12845056 | tf_op jit(solution)/shard_map/pallas_call | solution.py:140
  66.0 1.2 collective-permute-done.15.refs_3_.refs_7_
  67.2 0.7 collective-permute-done.13.refs_1_.refs_5_
  67.9 7.3 %shard_map.39 = (f32[896,128]{1,0:T(8,128)S(1)}, f32[896,128]{1,0:T(8,128)S(1)}, f32[4,128,128]{2,1,0:T(8,128)S(1)}) custom-call(s32[3]{0:T(128)S(1)} %pad_add_fusion.place, f32[896,7168]{1,0:T(8,128)} %block.11, f32[896,128]{1,0:T(8,128)S(1)} %collective-permute-done.5.refs_0_.refs_4_, f32[896,128]{1,0:T(8,128)S(1)} %collective-permute-done.13.refs_1_.refs_5_, ...), custom_call_target="tpu_custom_call" | custom-call | flops 2466250752 | bytes 6422528 | tf_op jit(solution)/shard_map/pallas_call | solution.py:140
  75.2 3.4 %collective-permute-start.16 = (f32[896,128]{1,0:T(8,128)S(1)}, f32[896,128]{1,0:T(8,128)S(1)}, u32[]{:S(2)}, u32[]{:S(2)}) collective-permute-start(f32[896,128]{1,0:T(8,128)S(1)} %get-tuple-element.30), channel_id=1, source_target_pairs={{0,1},{1,0},{2,3},{3,2},{4,5},{5,4},{6,7},{7,6},{8,9},{9,8},{10,11... | collective-permute-start | bytes 1376264 | tf_op jit(solution)/shard_map/ppermute | solution.py:281
  78.7 11.2 %collective-permute-done.16 = f32[896,128]{1,0:T(8,128)S(1)} collective-permute-done((f32[896,128]{1,0:T(8,128)S(1)}, f32[896,128]{1,0:T(8,128)S(1)}, u32[]{:S(2)}, u32[]{:S(2)}) %collective-permute-start.16) | collective-permute-done | bytes 458784 | tf_op jit(solution)/shard_map/ppermute | solution.py:281
  89.9 0.8 add.27.mine
  90.8 5.1 %collective-permute-start.24 = (f32[896,128]{1,0:T(8,128)}, f32[896,128]{1,0:T(8,128)}, u32[]{:S(2)}, u32[]{:S(2)}) collective-permute-start(f32[896,128]{1,0:T(8,128)} %add.27.mine), channel_id=1, source_target_pairs={{0,0},{1,16},{2,2},{3,18},{4,4},{5,20},{6,6},{7,22},{8,8},{9,24},{... | collective-permute-start | bytes 1376264 | tf_op jit(solution)/shard_map/ppermute | solution.py:293
  95.8 1.5 collective-permute-start.25
  98.0 0.9 collective-permute-done.19
  99.0 0.7 add.29
  99.7 1.1 collective-permute-start.20
  100.8 0.8 collective-permute-start.21
  101.6 1.7 collective-permute-start.22
  103.3 6.3 %collective-permute-done.25.refs_1_ = f32[896,128]{1,0:T(8,128)} collective-permute-done((f32[896,128]{1,0:T(8,128)}, f32[896,128]{1,0:T(8,128)}, u32[]{:S(2)}, u32[]{:S(2)}) %collective-permute-start.25) | collective-permute-done | bytes 458784 | tf_op jit(solution)/shard_map/ppermute | solution.py:293
  109.7 1.1 collective-permute-start.32
  110.8 8.7 %collective-permute-done.21 = f32[4,128,128]{2,1,0:T(8,128)} collective-permute-done((f32[4,128,128]{2,1,0:T(8,128)}, f32[4,128,128]{2,1,0:T(8,128)}, u32[]{:S(2)}, u32[]{:S(2)}) %collective-permute-start.21) | collective-permute-done | bytes 262176 | tf_op jit(solution)/shard_map/ppermute | solution.py:281
  119.5 5.3 %collective-permute-done.22 = f32[4,128,128]{2,1,0:T(8,128)} collective-permute-done((f32[4,128,128]{2,1,0:T(8,128)}, f32[4,128,128]{2,1,0:T(8,128)}, u32[]{:S(2)}, u32[]{:S(2)}) %collective-permute-start.22) | collective-permute-done | bytes 262176 | tf_op jit(solution)/shard_map/ppermute | solution.py:281
  124.8 1.2 add_add_fusion
  126.1 1.3 collective-permute-start.23
  127.4 2.1 %collective-permute-start.26 = (f32[896,128]{1,0:T(8,128)}, f32[896,128]{1,0:T(8,128)S(1)}, u32[]{:S(2)}, u32[]{:S(2)}) collective-permute-start(f32[896,128]{1,0:T(8,128)} %get-tuple-element.34.refs_0_), channel_id=1, source_target_pairs={{0,8},{1,9},{2,10},{3,11},{4,12},{5,13},{6,14},{7,15},{8,0},{9,1},... | collective-permute-start | bytes 1376264 | tf_op jit(solution)/shard_map/ppermute | solution.py:281
  129.5 10.3 %collective-permute-done.23 = f32[4,128,128]{2,1,0:T(8,128)S(1)} collective-permute-done((f32[4,128,128]{2,1,0:T(8,128)S(1)}, f32[4,128,128]{2,1,0:T(8,128)S(1)}, u32[]{:S(2)}, u32[]{:S(2)}) %collective-permute-start.23) | collective-permute-done | bytes 262176 | tf_op jit(solution)/shard_map/ppermute | solution.py:281
  139.8 1.1 collective-permute-start.29
  141.1 4.8 %shard_map.40 = (bf16[896,512]{1,0:T(8,128)(2,1)S(1)}, bf16[896,512]{1,0:T(8,128)(2,1)S(1)}) custom-call(s32[3]{0:T(128)S(1)} %pad_add_fusion.place, f32[2,896,128]{2,1,0:T(8,128)S(1)} %copy-done.5, f32[896,128]{1,0:T(8,128)} %add.27.mine, f32[896,128]{1,0:T(8,128)} %collective-permute-done.17.other, f32[4,128,128]{2,1,0:T(8,128)S(1)} %add.33.inner, ...), custom_call_target="tpu_custom_call" | custom-call | flops 1409286144 | bytes 3670016 | tf_op jit(solution)/shard_map/pallas_call | solution.py:197
  146.5 0.9 collective-permute-start.27
  147.4 6.0 %collective-permute-done.29.refs_2_ = f32[896,128]{1,0:T(8,128)S(1)} collective-permute-done((f32[896,128]{1,0:T(8,128)}, f32[896,128]{1,0:T(8,128)S(1)}, u32[]{:S(2)}, u32[]{:S(2)}) %collective-permute-start.29) | collective-permute-done | bytes 458784 | tf_op jit(solution)/shard_map/ppermute | solution.py:281
  153.5 0.8 collective-permute-done.36.refs_10_
  154.4 1.0 copy-done.18
  155.4 1.0 copy-done.20
  156.4 10.8 %shard_map.42 = (f32[896,7168]{1,0:T(8,128)}, s32[8,128]{1,0:T(8,128)}) custom-call(s32[3]{0:T(128)S(1)} %pad_add_fusion.place, f32[896,7168]{1,0:T(8,128)} %block.11, bf16[896,512]{1,0:T(8,128)(2,1)S(1)} %get-tuple-element.32.high, bf16[896,512]{1,0:T(8,128)(2,1)S(1)} %get-tuple-element.33.low, f32[896,128]{1,0:T(8,128)} %get-tuple-element.34.refs_0_, ...), custom_call_target="tpu_custom_call" | custom-call | flops 4932501504 | bytes 12845056 | tf_op jit(solution)/shard_map/pallas_call | solution.py:234
  167.9 18.1 %shard_map.43 = (f32[896,7168]{1,0:T(8,128)}, s32[8,128]{1,0:T(8,128)}) custom-call(s32[3]{0:T(128)S(1)} %pad_add_fusion.place, f32[896,7168]{1,0:T(8,128)} %block.11, bf16[896,512]{1,0:T(8,128)(2,1)} %copy-done, bf16[896,512]{1,0:T(8,128)(2,1)} %copy-done.2, f32[896,128]{1,0:T(8,128)S(1)} %collective-permute-done.32.refs_0_, ...), custom_call_target="tpu_custom_call", output_to_operand_aliasing={{0}: (20, {})} | custom-call | flops 9865003008 | bytes 25690112 | tf_op jit(solution)/shard_map/pallas_call | solution.py:234
  186.0 1.2 copy-done.1
  187.2 1.2 copy-done.3
  188.3 10.6 %shard_map.44 = (f32[896,7168]{1,0:T(8,128)}, s32[8,128]{1,0:T(8,128)}) custom-call(s32[3]{0:T(128)S(1)} %pad_add_fusion.place, f32[896,7168]{1,0:T(8,128)} %block.11, bf16[896,512]{1,0:T(8,128)(2,1)S(1)} %copy-done.1, bf16[896,512]{1,0:T(8,128)(2,1)S(1)} %copy-done.3, ...), custom_call_target="tpu_custom_call", output_to_operand_aliasing={{0}: (12, {})} | custom-call | flops 4932501504 | bytes 12845056 | tf_op jit(solution)/shard_map/pallas_call | solution.py:234
  (105 shorter events, 4.8 us)
Async XLA Ops:
  1.2 7.3 %collective-permute-start = (f32[896,128]{1,0:T(8,128)S(1)}, f32[896,128]{1,0:T(8,128)S(1)}, u32[]{:S(2)}, u32[]{:S(2)}) collective-permute-start(f32[896,128]{1,0:T(8,128)S(1)} %get-tuple-element.40), channel_id=1, source_target_pairs={{0,0},{1,16},{2,2},{3,18},{4,4},{5,20},{6,6},{7,22},{8,8},{9,24},{... | collective-permute-start | bytes 1376264 | tf_op jit(solution)/shard_map/ppermute | solution.py:293
  1.9 17.0 %collective-permute-start.2 = (f32[896,128]{1,0:T(8,128)S(1)}, f32[896,128]{1,0:T(8,128)S(1)}, u32[]{:S(2)}, u32[]{:S(2)}) collective-permute-start(f32[896,128]{1,0:T(8,128)S(1)} %get-tuple-element.39), channel_id=1, source_target_pairs={{0,16},{1,0},{2,18},{3,2},{4,20},{5,4},{6,22},{7,6},{8,24},{9,8},{... | collective-permute-start | bytes 1376264 | tf_op jit(solution)/shard_map/ppermute | solution.py:293
  8.5 43.3 %copy-start.15 = (f32[896,128]{1,0:T(8,128)}, f32[896,128]{1,0:T(8,128)S(1)}, u32[]{:S(2)}) copy-start(f32[896,128]{1,0:T(8,128)S(1)} %collective-permute-done.refs_0_.refs_4_) | copy-start | bytes 1376260
  8.5 22.4 %collective-permute-start.1 = (f32[896,128]{1,0:T(8,128)S(1)}, f32[896,128]{1,0:T(8,128)S(1)}, u32[]{:S(2)}, u32[]{:S(2)}) collective-permute-start(f32[896,128]{1,0:T(8,128)S(1)} %collective-permute-done.refs_0_.refs_4_), channel_id=1, source_target_pairs={{0,2},{1,3},{2,0},{3,1},{4,6},{5,7},{6,4},{7,5},{8,10},{9,11},{10,... | collective-permute-start | bytes 1376264 | tf_op jit(solution)/shard_map/ppermute | solution.py:281
  18.9 33.8 %copy-start.17 = (f32[896,128]{1,0:T(8,128)}, f32[896,128]{1,0:T(8,128)S(1)}, u32[]{:S(2)}) copy-start(f32[896,128]{1,0:T(8,128)S(1)} %collective-permute-done.2.refs_2_.refs_6_) | copy-start | bytes 1376260
  18.9 12.6 %collective-permute-start.3 = (f32[896,128]{1,0:T(8,128)S(1)}, f32[896,128]{1,0:T(8,128)}, u32[]{:S(2)}, u32[]{:S(2)}) collective-permute-start(f32[896,128]{1,0:T(8,128)S(1)} %collective-permute-done.2.refs_2_.refs_6_), channel_id=1, source_target_pairs={{0,2},{1,3},{2,0},{3,1},{4,6},{5,7},{6,4},{7,5},{8,10},{9,11},{10,... | collective-permute-start | bytes 1376264 | tf_op jit(solution)/shard_map/ppermute | solution.py:281
  18.9 21.7 %collective-permute-start.4 = (f32[896,128]{1,0:T(8,128)S(1)}, f32[896,128]{1,0:T(8,128)S(1)}, u32[]{:S(2)}, u32[]{:S(2)}) collective-permute-start(f32[896,128]{1,0:T(8,128)S(1)} %collective-permute-done.refs_0_.refs_4_), channel_id=1, source_target_pairs={{0,8},{1,9},{2,10},{3,11},{4,12},{5,13},{6,14},{7,15},{8,0},{9,1},... | collective-permute-start | bytes 1376264 | tf_op jit(solution)/shard_map/ppermute | solution.py:281
  29.3 13.4 %collective-permute-start.8 = (f32[896,128]{1,0:T(8,128)S(1)}, f32[896,128]{1,0:T(8,128)S(1)}, u32[]{:S(2)}, u32[]{:S(2)}) collective-permute-start(f32[896,128]{1,0:T(8,128)S(1)} %collective-permute-done.2.refs_2_.refs_6_), channel_id=1, source_target_pairs={{0,4},{1,5},{2,6},{3,7},{4,0},{5,1},{6,2},{7,3},{8,12},{9,13},{10,... | collective-permute-start | bytes 1376264 | tf_op jit(solution)/shard_map/ppermute | solution.py:281
  30.8 19.5 %collective-permute-start.11 = (f32[896,128]{1,0:T(8,128)S(1)}, f32[896,128]{1,0:T(8,128)S(1)}, u32[]{:S(2)}, u32[]{:S(2)}) collective-permute-start(f32[896,128]{1,0:T(8,128)S(1)} %collective-permute-done.2.refs_2_.refs_6_), channel_id=1, source_target_pairs={{0,8},{1,9},{2,10},{3,11},{4,12},{5,13},{6,14},{7,15},{8,0},{9,1},... | collective-permute-start | bytes 1376264 | tf_op jit(solution)/shard_map/ppermute | solution.py:281
  30.9 20.9 %collective-permute-start.6 = (f32[896,128]{1,0:T(8,128)S(1)}, f32[896,128]{1,0:T(8,128)S(1)}, u32[]{:S(2)}, u32[]{:S(2)}) collective-permute-start(f32[896,128]{1,0:T(8,128)S(1)} %collective-permute-done.refs_0_.refs_4_), channel_id=1, source_target_pairs={{0,4},{1,5},{2,6},{3,7},{4,0},{5,1},{6,2},{7,3},{8,12},{9,13},{10,... | collective-permute-start | bytes 1376264 | tf_op jit(solution)/shard_map/ppermute | solution.py:281
  40.7 12.0 %collective-permute-start.10 = (f32[896,128]{1,0:T(8,128)S(1)}, f32[896,128]{1,0:T(8,128)S(1)}, u32[]{:S(2)}, u32[]{:S(2)}) collective-permute-start(f32[896,128]{1,0:T(8,128)S(1)} %collective-permute-done.4.refs_4_.refs_12_), channel_id=1, source_target_pairs={{0,2},{1,3},{2,0},{3,1},{4,6},{5,7},{6,4},{7,5},{8,10},{9,11},{10,... | collective-permute-start | bytes 1376264 | tf_op jit(solution)/shard_map/ppermute | solution.py:281
  42.7 11.7 %collective-permute-start.9 = (f32[896,128]{1,0:T(8,128)S(1)}, f32[896,128]{1,0:T(8,128)S(1)}, u32[]{:S(2)}, u32[]{:S(2)}) collective-permute-start(f32[896,128]{1,0:T(8,128)S(1)} %collective-permute-done.8.refs_2_.refs_6_), channel_id=1, source_target_pairs={{0,2},{1,3},{2,0},{3,1},{4,6},{5,7},{6,4},{7,5},{8,10},{9,11},{10,... | collective-permute-start | bytes 1376264 | tf_op jit(solution)/shard_map/ppermute | solution.py:281
  50.3 4.0 %collective-permute-start.12 = (f32[896,128]{1,0:T(8,128)S(1)}, f32[896,128]{1,0:T(8,128)S(1)}, u32[]{:S(2)}, u32[]{:S(2)}) collective-permute-start(f32[896,128]{1,0:T(8,128)S(1)} %collective-permute-done.11.refs_6_.refs_14_), channel_id=1, source_target_pairs={{0,2},{1,3},{2,0},{3,1},{4,6},{5,7},{6,4},{7,5},{8,10},{9,11},{10,... | collective-permute-start | bytes 1376264 | tf_op jit(solution)/shard_map/ppermute | solution.py:281
  51.8 2.6 %collective-permute-start.7 = (f32[896,128]{1,0:T(8,128)S(1)}, f32[896,128]{1,0:T(8,128)S(1)}, u32[]{:S(2)}, u32[]{:S(2)}) collective-permute-start(f32[896,128]{1,0:T(8,128)S(1)} %collective-permute-done.6.refs_0_.refs_4_), channel_id=1, source_target_pairs={{0,2},{1,3},{2,0},{3,1},{4,6},{5,7},{6,4},{7,5},{8,10},{9,11},{10,... | collective-permute-start | bytes 1376264 | tf_op jit(solution)/shard_map/ppermute | solution.py:281
  51.8 13.4 %collective-permute-start.14 = (f32[896,128]{1,0:T(8,128)S(1)}, f32[896,128]{1,0:T(8,128)S(1)}, u32[]{:S(2)}, u32[]{:S(2)}) collective-permute-start(f32[896,128]{1,0:T(8,128)S(1)} %broadcast_select_fusion.1), channel_id=1, source_target_pairs={{0,8},{1,9},{2,10},{3,11},{4,12},{5,13},{6,14},{7,15},{8,0},{9,1},... | collective-permute-start | bytes 1376264 | tf_op jit(solution)/shard_map/ppermute | solution.py:281
  52.7 12.7 %collective-permute-start.5 = (f32[896,128]{1,0:T(8,128)S(1)}, f32[896,128]{1,0:T(8,128)S(1)}, u32[]{:S(2)}, u32[]{:S(2)}) collective-permute-start(f32[896,128]{1,0:T(8,128)S(1)} %broadcast_select_fusion.3), channel_id=1, source_target_pairs={{0,4},{1,5},{2,6},{3,7},{4,0},{5,1},{6,2},{7,3},{8,12},{9,13},{10,... | collective-permute-start | bytes 1376264 | tf_op jit(solution)/shard_map/ppermute | solution.py:281
  65.3 1.9 collective-permute-start.15
  65.5 2.4 %collective-permute-start.13 = (f32[896,128]{1,0:T(8,128)S(1)}, f32[896,128]{1,0:T(8,128)S(1)}, u32[]{:S(2)}, u32[]{:S(2)}) collective-permute-start(f32[896,128]{1,0:T(8,128)S(1)} %broadcast_select_fusion.2), channel_id=1, source_target_pairs={{0,2},{1,3},{2,0},{3,1},{4,6},{5,7},{6,4},{7,5},{8,10},{9,11},{10,... | collective-permute-start | bytes 1376264 | tf_op jit(solution)/shard_map/ppermute | solution.py:281
  75.2 14.7 %collective-permute-start.16 = (f32[896,128]{1,0:T(8,128)S(1)}, f32[896,128]{1,0:T(8,128)S(1)}, u32[]{:S(2)}, u32[]{:S(2)}) collective-permute-start(f32[896,128]{1,0:T(8,128)S(1)} %get-tuple-element.30), channel_id=1, source_target_pairs={{0,1},{1,0},{2,3},{3,2},{4,5},{5,4},{6,7},{7,6},{8,9},{9,8},{10,11... | collective-permute-start | bytes 1376264 | tf_op jit(solution)/shard_map/ppermute | solution.py:281
  78.6 18.7 %collective-permute-start.18 = (f32[4,128,128]{2,1,0:T(8,128)S(1)}, f32[4,128,128]{2,1,0:T(8,128)S(1)}, u32[]{:S(2)}, u32[]{:S(2)}) collective-permute-start(f32[4,128,128]{2,1,0:T(8,128)S(1)} %get-tuple-element.31), channel_id=1, source_target_pairs={{0,1},{1,0},{2,3},{3,2},{4,5},{5,4},{6,7},{7,6},{8,9},{9,8},{10,11... | collective-permute-start | bytes 786440 | tf_op jit(solution)/shard_map/ppermute | solution.py:281
  90.8 10.9 %collective-permute-start.24 = (f32[896,128]{1,0:T(8,128)}, f32[896,128]{1,0:T(8,128)}, u32[]{:S(2)}, u32[]{:S(2)}) collective-permute-start(f32[896,128]{1,0:T(8,128)} %add.27.mine), channel_id=1, source_target_pairs={{0,0},{1,16},{2,2},{3,18},{4,4},{5,20},{6,6},{7,22},{8,8},{9,24},{... | collective-permute-start | bytes 1376264 | tf_op jit(solution)/shard_map/ppermute | solution.py:293
  95.8 13.8 %collective-permute-start.25 = (f32[896,128]{1,0:T(8,128)}, f32[896,128]{1,0:T(8,128)}, u32[]{:S(2)}, u32[]{:S(2)}) collective-permute-start(f32[896,128]{1,0:T(8,128)} %add.27.mine), channel_id=1, source_target_pairs={{0,16},{1,0},{2,18},{3,2},{4,20},{5,4},{6,22},{7,6},{8,24},{9,8},{... | collective-permute-start | bytes 1376264 | tf_op jit(solution)/shard_map/ppermute | solution.py:293
  97.4 1.6 collective-permute-start.19
  97.4 32.1 %collective-permute-start.17 = (f32[896,128]{1,0:T(8,128)}, f32[896,128]{1,0:T(8,128)}, u32[]{:S(2)}, u32[]{:S(2)}) collective-permute-start(f32[896,128]{1,0:T(8,128)} %add.27.mine), channel_id=1, source_target_pairs={{0,1},{1,0},{2,3},{3,2},{4,5},{5,4},{6,7},{7,6},{8,9},{9,8},{10,11... | collective-permute-start | bytes 1376264 | tf_op jit(solution)/shard_map/ppermute | solution.py:281
  99.7 41.4 %copy-start.5 = (f32[2,896,128]{2,1,0:T(8,128)S(1)}, f32[2,896,128]{2,1,0:T(8,128)}, u32[]{:S(2)}) copy-start(f32[2,896,128]{2,1,0:T(8,128)} %own.1) | copy-start | bytes 2752516
  99.7 41.4 %copy-start.25 = (f32[2,128,128]{2,1,0:T(8,128)S(1)}, f32[2,128,128]{2,1,0:T(8,128)}, u32[]{:S(2)}) copy-start(f32[2,128,128]{2,1,0:T(8,128)} %factors.1) | copy-start | bytes 393220
  99.7 54.7 %copy-start.16 = (f32[896,128]{1,0:T(8,128)S(1)}, f32[896,128]{1,0:T(8,128)}, u32[]{:S(2)}) copy-start(f32[896,128]{1,0:T(8,128)} %copy-done.15) | copy-start | bytes 1376260
  99.7 10.0 %collective-permute-start.20 = (f32[4,128,128]{2,1,0:T(8,128)}, f32[4,128,128]{2,1,0:T(8,128)}, u32[]{:S(2)}, u32[]{:S(2)}) collective-permute-start(f32[4,128,128]{2,1,0:T(8,128)} %add.29), channel_id=1, source_target_pairs={{0,4},{1,5},{2,6},{3,7},{4,0},{5,1},{6,2},{7,3},{8,12},{9,13},{10,... | collective-permute-start | bytes 786440 | tf_op jit(solution)/shard_map/ppermute | solution.py:281
  100.8 18.7 %collective-permute-start.21 = (f32[4,128,128]{2,1,0:T(8,128)}, f32[4,128,128]{2,1,0:T(8,128)}, u32[]{:S(2)}, u32[]{:S(2)}) collective-permute-start(f32[4,128,128]{2,1,0:T(8,128)} %add.29), channel_id=1, source_target_pairs={{0,8},{1,9},{2,10},{3,11},{4,12},{5,13},{6,14},{7,15},{8,0},{9,1},... | collective-permute-start | bytes 786440 | tf_op jit(solution)/shard_map/ppermute | solution.py:281
  101.6 23.2 %collective-permute-start.22 = (f32[4,128,128]{2,1,0:T(8,128)}, f32[4,128,128]{2,1,0:T(8,128)}, u32[]{:S(2)}, u32[]{:S(2)}) collective-permute-start(f32[4,128,128]{2,1,0:T(8,128)} %add.29), channel_id=1, source_target_pairs={{0,12},{1,13},{2,14},{3,15},{4,8},{5,9},{6,10},{7,11},{8,4},{9,5},... | collective-permute-start | bytes 786440 | tf_op jit(solution)/shard_map/ppermute | solution.py:281
  109.6 58.2 %copy-start.8 = (f32[896,128]{1,0:T(8,128)S(1)}, f32[896,128]{1,0:T(8,128)}, u32[]{:S(2)}) copy-start(f32[896,128]{1,0:T(8,128)} %copy-done.7) | copy-start | bytes 1376260
  109.6 58.3 %copy-start.11 = (f32[896,128]{1,0:T(8,128)S(1)}, f32[896,128]{1,0:T(8,128)}, u32[]{:S(2)}) copy-start(f32[896,128]{1,0:T(8,128)} %copy-done.10) | copy-start | bytes 1376260
  109.6 58.3 %copy-start.14 = (f32[896,128]{1,0:T(8,128)S(1)}, f32[896,128]{1,0:T(8,128)}, u32[]{:S(2)}) copy-start(f32[896,128]{1,0:T(8,128)} %copy-done.13) | copy-start | bytes 1376260
  109.6 31.4 %collective-permute-start.38 = (f32[896,128]{1,0:T(8,128)}, f32[896,128]{1,0:T(8,128)S(1)}, u32[]{:S(2)}, u32[]{:S(2)}) collective-permute-start(f32[896,128]{1,0:T(8,128)} %get-tuple-element.34.refs_0_), channel_id=1, source_target_pairs={{0,2},{1,3},{2,0},{3,1},{4,6},{5,7},{6,4},{7,5},{8,10},{9,11},{10,... | collective-permute-start | bytes 1376264 | tf_op jit(solution)/shard_map/ppermute | solution.py:281
  109.7 31.3 %collective-permute-start.32 = (f32[896,128]{1,0:T(8,128)}, f32[896,128]{1,0:T(8,128)S(1)}, u32[]{:S(2)}, u32[]{:S(2)}) collective-permute-start(f32[896,128]{1,0:T(8,128)} %get-tuple-element.34.refs_0_), channel_id=1, source_target_pairs={{0,4},{1,5},{2,6},{3,7},{4,0},{5,1},{6,2},{7,3},{8,12},{9,13},{10,... | collective-permute-start | bytes 1376264 | tf_op jit(solution)/shard_map/ppermute | solution.py:281
  126.1 13.8 %collective-permute-start.23 = (f32[4,128,128]{2,1,0:T(8,128)S(1)}, f32[4,128,128]{2,1,0:T(8,128)S(1)}, u32[]{:S(2)}, u32[]{:S(2)}) collective-permute-start(f32[4,128,128]{2,1,0:T(8,128)S(1)} %add_add_fusion), channel_id=1, source_target_pairs={{0,16},{1,17},{2,18},{3,19},{4,20},{5,21},{6,22},{7,23},{8,24},{9,... | collective-permute-start | bytes 786440 | tf_op jit(solution)/shard_map/ppermute | solution.py:281
  127.4 18.6 %collective-permute-start.26 = (f32[896,128]{1,0:T(8,128)}, f32[896,128]{1,0:T(8,128)S(1)}, u32[]{:S(2)}, u32[]{:S(2)}) collective-permute-start(f32[896,128]{1,0:T(8,128)} %get-tuple-element.34.refs_0_), channel_id=1, source_target_pairs={{0,8},{1,9},{2,10},{3,11},{4,12},{5,13},{6,14},{7,15},{8,0},{9,1},... | collective-permute-start | bytes 1376264 | tf_op jit(solution)/shard_map/ppermute | solution.py:281
  129.5 17.0 %collective-permute-start.39 = (f32[896,128]{1,0:T(8,128)}, f32[896,128]{1,0:T(8,128)S(1)}, u32[]{:S(2)}, u32[]{:S(2)}) collective-permute-start(f32[896,128]{1,0:T(8,128)} %get-tuple-element.35.refs_2_), channel_id=1, source_target_pairs={{0,2},{1,3},{2,0},{3,1},{4,6},{5,7},{6,4},{7,5},{8,10},{9,11},{10,... | collective-permute-start | bytes 1376264 | tf_op jit(solution)/shard_map/ppermute | solution.py:281
  139.8 13.6 %collective-permute-start.29 = (f32[896,128]{1,0:T(8,128)}, f32[896,128]{1,0:T(8,128)S(1)}, u32[]{:S(2)}, u32[]{:S(2)}) collective-permute-start(f32[896,128]{1,0:T(8,128)} %get-tuple-element.35.refs_2_), channel_id=1, source_target_pairs={{0,4},{1,5},{2,6},{3,7},{4,0},{5,1},{6,2},{7,3},{8,12},{9,13},{10,... | collective-permute-start | bytes 1376264 | tf_op jit(solution)/shard_map/ppermute | solution.py:281
  141.0 13.3 %collective-permute-start.36 = (f32[896,128]{1,0:T(8,128)}, f32[896,128]{1,0:T(8,128)S(1)}, u32[]{:S(2)}, u32[]{:S(2)}) collective-permute-start(f32[896,128]{1,0:T(8,128)} %get-tuple-element.35.refs_2_), channel_id=1, source_target_pairs={{0,8},{1,9},{2,10},{3,11},{4,12},{5,13},{6,14},{7,15},{8,0},{9,1},... | collective-permute-start | bytes 1376264 | tf_op jit(solution)/shard_map/ppermute | solution.py:281
  141.0 13.4 %collective-permute-start.33 = (f32[896,128]{1,0:T(8,128)S(1)}, f32[896,128]{1,0:T(8,128)S(1)}, u32[]{:S(2)}, u32[]{:S(2)}) collective-permute-start(f32[896,128]{1,0:T(8,128)S(1)} %collective-permute-done.32.refs_0_), channel_id=1, source_target_pairs={{0,2},{1,3},{2,0},{3,1},{4,6},{5,7},{6,4},{7,5},{8,10},{9,11},{10,... | collective-permute-start | bytes 1376264 | tf_op jit(solution)/shard_map/ppermute | solution.py:281
  146.0 21.9 %collective-permute-start.35 = (f32[896,128]{1,0:T(8,128)S(1)}, f32[896,128]{1,0:T(8,128)S(1)}, u32[]{:S(2)}, u32[]{:S(2)}) collective-permute-start(f32[896,128]{1,0:T(8,128)S(1)} %collective-permute-done.26.refs_8_), channel_id=1, source_target_pairs={{0,2},{1,3},{2,0},{3,1},{4,6},{5,7},{6,4},{7,5},{8,10},{9,11},{10,... | collective-permute-start | bytes 1376264 | tf_op jit(solution)/shard_map/ppermute | solution.py:281
  146.5 20.7 %collective-permute-start.27 = (f32[896,128]{1,0:T(8,128)S(1)}, f32[896,128]{1,0:T(8,128)S(1)}, u32[]{:S(2)}, u32[]{:S(2)}) collective-permute-start(f32[896,128]{1,0:T(8,128)S(1)} %collective-permute-done.26.refs_8_), channel_id=1, source_target_pairs={{0,4},{1,5},{2,6},{3,7},{4,0},{5,1},{6,2},{7,3},{8,12},{9,13},{10,... | collective-permute-start | bytes 1376264 | tf_op jit(solution)/shard_map/ppermute | solution.py:281
  153.4 14.4 %collective-permute-start.34 = (f32[896,128]{1,0:T(8,128)S(1)}, f32[896,128]{1,0:T(8,128)S(1)}, u32[]{:S(2)}, u32[]{:S(2)}) collective-permute-start(f32[896,128]{1,0:T(8,128)S(1)} %collective-permute-done.29.refs_2_), channel_id=1, source_target_pairs={{0,2},{1,3},{2,0},{3,1},{4,6},{5,7},{6,4},{7,5},{8,10},{9,11},{10,... | collective-permute-start | bytes 1376264 | tf_op jit(solution)/shard_map/ppermute | solution.py:281
  154.3 13.5 %collective-permute-start.30 = (f32[896,128]{1,0:T(8,128)S(1)}, f32[896,128]{1,0:T(8,128)S(1)}, u32[]{:S(2)}, u32[]{:S(2)}) collective-permute-start(f32[896,128]{1,0:T(8,128)S(1)} %collective-permute-done.29.refs_2_), channel_id=1, source_target_pairs={{0,8},{1,9},{2,10},{3,11},{4,12},{5,13},{6,14},{7,15},{8,0},{9,1},... | collective-permute-start | bytes 1376264 | tf_op jit(solution)/shard_map/ppermute | solution.py:281
  154.4 13.5 %collective-permute-start.37 = (f32[896,128]{1,0:T(8,128)S(1)}, f32[896,128]{1,0:T(8,128)S(1)}, u32[]{:S(2)}, u32[]{:S(2)}) collective-permute-start(f32[896,128]{1,0:T(8,128)S(1)} %collective-permute-done.36.refs_10_), channel_id=1, source_target_pairs={{0,2},{1,3},{2,0},{3,1},{4,6},{5,7},{6,4},{7,5},{8,10},{9,11},{10,... | collective-permute-start | bytes 1376264 | tf_op jit(solution)/shard_map/ppermute | solution.py:281
  167.2 18.7 %collective-permute-start.28 = (f32[896,128]{1,0:T(8,128)S(1)}, f32[896,128]{1,0:T(8,128)S(1)}, u32[]{:S(2)}, u32[]{:S(2)}) collective-permute-start(f32[896,128]{1,0:T(8,128)S(1)} %collective-permute-done.27.refs_0_), channel_id=1, source_target_pairs={{0,2},{1,3},{2,0},{3,1},{4,6},{5,7},{6,4},{7,5},{8,10},{9,11},{10,... | collective-permute-start | bytes 1376264 | tf_op jit(solution)/shard_map/ppermute | solution.py:281
  167.7 18.2 %collective-permute-start.31 = (f32[896,128]{1,0:T(8,128)S(1)}, f32[896,128]{1,0:T(8,128)S(1)}, u32[]{:S(2)}, u32[]{:S(2)}) collective-permute-start(f32[896,128]{1,0:T(8,128)S(1)} %collective-permute-done.30.refs_2_), channel_id=1, source_target_pairs={{0,2},{1,3},{2,0},{3,1},{4,6},{5,7},{6,4},{7,5},{8,10},{9,11},{10,... | collective-permute-start | bytes 1376264 | tf_op jit(solution)/shard_map/ppermute | solution.py:281
  (18 other events, 265.6 us)

commit v3 on v2

--- a/solution.py
+++ b/solution.py
@@ -13,7 +13,7 @@
 BOTH_LAST = (((1,), (1,)), ((), ()))
 BOTH_FIRST = (((0,), (0,)), ((), ()))
 VMEM_BYTES = 48 * 1024 * 1024
-GATES = (True, True, False, False)
+GATES = (True, True, True, True)
 FORWARD = ((0,), (2, 4), (6,))
 UPDATE = ((0,), (2, 4), (6,))
 
@@ -353,14 +353,14 @@
             mine, other = lax.psum((kept, sent), "col")
             blocks = [transpose(mine, 0), transpose(other, 1)]
         blocks = steer(blocks, 40)
-        masks = [1 << n for n in range(everyone.bit_length() - 1)]
-        for mask in masks[:2]:
-            inner = inner + flip(inner, mask)
-        masks = masks[2:]
-        while masks:
-            now, masks = masks[:2], masks[2:]
-            reach = now + [now[0] ^ now[1]] if len(now) == 2 else now
-            inner = sum([flip(inner, mask) for mask in reach], inner)
+        odd = row % 2 != 0
+        upper, lower = inner[:2], inner[2:]
+        part = jnp.where(odd, lower, upper) + flip_row(jnp.where(odd, upper, lower), 1)
+        masks = [1 << n for n in range(everyone.bit_length() - 1) if 1 << n != col_count]
+        for mask in masks:
+            part = part + flip(part, mask)
+        there = flip_row(part, 1)
+        inner = jnp.concatenate([jnp.where(odd, there, part), jnp.where(odd, part, there)], axis=0)
         sides = mix(place, panels, mine, other, inner, factors)
 
         def update(slots, blocks):

time: 200 us -> 193 us (0.965)
  waiting for transfers between devices: 73.8 us -> 58.9 us
  local copies, waits for them, and re-layouts: 7.89 us -> 12.4 us
    ppermute x36, waiting for transfers between devices: 57.1 us -> 48.4 us  [flip(): lax.ppermute(values, ('row', 'col'), [(n, n ^ mask) for n in range(everyo...]
    ppermute x4, waiting for transfers between devices: 16.8 us -> 10.4 us  [transpose(): return lax.ppermute(values, ('row', 'col'), pairs)]
    unnamed x52 -> x56, local copies, waits for them, and re-layouts: 5.64 us -> 8.92 us
  transfers between devices with their start and end apart: 40 -> 40, of which waited for: 15 -> 19; matrix products, arithmetic and copies ran while one was open for 2% -> 3% of each run, Pallas kernels for 25% -> 26%
where the time goes in v3:
time: 193 us; the launch traced here: 192 us
  Pallas kernels  67.8 us (35%)
  waiting for transfers between devices  58.9 us (31%)
  starting transfers between devices  45.8 us (24%)
  local copies, waits for them, and re-layouts  12.4 us (6%)
  other arithmetic  3.78 us (2%)
  between operations  2.99 us (2%)
    ppermute x36, waiting for transfers between devices, flip(): lax.ppermute(values, ('row', 'col'), [(n, n ^ mask) for n in range(everyo...  48.4 us
    pallas_call x3, Pallas kernels, update_step(): pl.pallas_call(functools.partial(update_kernel, count), grid_spec=pltpu.P...  39.7 us
    ppermute x36, starting transfers between devices, flip(): lax.ppermute(values, ('row', 'col'), [(n, n ^ mask) for n in range(everyo...  32.1 us
    pallas_call x3, Pallas kernels, forward_step(): pl.pallas_call(functools.partial(forward_kernel, first, last, count, shar...  23.3 us
    ppermute x4, starting transfers between devices, transpose(): return lax.ppermute(values, ('row', 'col'), pairs)  13.7 us
    ppermute x4, waiting for transfers between devices, transpose(): return lax.ppermute(values, ('row', 'col'), pairs)  10.4 us
    unnamed x56, local copies, waits for them, and re-layouts  8.92 us
    pallas_call x1, Pallas kernels, mix(): pl.pallas_call(mix_kernel, in_specs=[pl.BlockSpec(memory_space=pltpu.SMEM...  4.81 us
  transfers between devices with their start and end apart: 40, of which 19 were waited for; matrix products, arithmetic and copies ran while one was open for 3% of the time, Pallas kernels for 26%

profile of v3, /device:TPU:0, one launch (start us, length us, event | category | flops | bytes accessed | tf_op | source)
XLA Modules:
  0.0 191.7 jit_solution(562637216645680280)
XLA Ops:
  0.0 1.2 slice_bitcast_fusion
  1.2 0.7 collective-permute-start
  1.9 6.6 %collective-permute-start.2 = (f32[896,128]{1,0:T(8,128)S(1)}, f32[896,128]{1,0:T(8,128)S(1)}, u32[]{:S(2)}, u32[]{:S(2)}) collective-permute-start(f32[896,128]{1,0:T(8,128)S(1)} %get-tuple-element.43), channel_id=1, source_target_pairs={{0,16},{1,0},{2,18},{3,2},{4,20},{5,4},{6,22},{7,6},{8,24},{9,8},{... | collective-permute-start | bytes 1376264 | tf_op jit(solution)/shard_map/ppermute | solution.py:293
  8.5 10.4 %collective-permute-done.2.refs_2_.refs_6_ = f32[896,128]{1,0:T(8,128)S(1)} collective-permute-done((f32[896,128]{1,0:T(8,128)S(1)}, f32[896,128]{1,0:T(8,128)S(1)}, u32[]{:S(2)}, u32[]{:S(2)}) %collective-permute-start.2) | collective-permute-done | bytes 458784 | tf_op jit(solution)/shard_map/ppermute | solution.py:293
  18.9 10.4 %collective-permute-start.4 = (f32[896,128]{1,0:T(8,128)S(1)}, f32[896,128]{1,0:T(8,128)S(1)}, u32[]{:S(2)}, u32[]{:S(2)}) collective-permute-start(f32[896,128]{1,0:T(8,128)S(1)} %collective-permute-done.refs_0_.refs_4_), channel_id=1, source_target_pairs={{0,8},{1,9},{2,10},{3,11},{4,12},{5,13},{6,14},{7,15},{8,0},{9,1},... | collective-permute-start | bytes 1376264 | tf_op jit(solution)/shard_map/ppermute | solution.py:281
  29.3 1.5 collective-permute-start.8
  31.5 1.2 copy-done.4
  32.7 6.1 %shard_map.37 = (f32[896,256]{1,0:T(8,128)S(1)}, s32[8,128]{1,0:T(8,128)S(1)}, bf16[2,256,448]{2,1,0:T(8,128)(2,1)S(1)}, bf16[2,256,448]{2,1,0:T(8,128)(2,1)S(1)}, f32[128,128]{1,0:T(8,128)S(1)}) custom-call(s32[3]{0:T(128)S(1)} %pad_add_fusion.place, f32[896,7168]{1,0:T(8,128)} %block.11, f32[896,128]{1,0:T(8,128)S(1)} %collective-permute-done.refs_0_.refs_4_, ...), custom_call_target="tpu_custom_call" | custom-call | flops 2466250752 | bytes 6422528 | tf_op jit(solution)/shard_map/pallas_call | solution.py:140
  40.7 2.0 %collective-permute-done.8.refs_2_.refs_6_ = f32[896,128]{1,0:T(8,128)S(1)} collective-permute-done((f32[896,128]{1,0:T(8,128)S(1)}, f32[896,128]{1,0:T(8,128)S(1)}, u32[]{:S(2)}, u32[]{:S(2)}) %collective-permute-start.8) | collective-permute-done | bytes 458784 | tf_op jit(solution)/shard_map/ppermute | solution.py:281
  42.7 7.6 %collective-permute-done.11.refs_6_.refs_14_ = f32[896,128]{1,0:T(8,128)S(1)} collective-permute-done((f32[896,128]{1,0:T(8,128)S(1)}, f32[896,128]{1,0:T(8,128)S(1)}, u32[]{:S(2)}, u32[]{:S(2)}) %collective-permute-start.11) | collective-permute-done | bytes 458784 | tf_op jit(solution)/shard_map/ppermute | solution.py:281
  50.3 1.5 collective-permute-done.6.refs_0_.refs_4_
  51.8 0.8 collective-permute-start.14
  52.7 1.6 collective-permute-start.5
  54.4 9.7 %shard_map.38 = (f32[896,256]{1,0:T(8,128)S(1)}, s32[8,128]{1,0:T(8,128)S(1)}) custom-call(s32[3]{0:T(128)S(1)} %pad_add_fusion.place, f32[896,7168]{1,0:T(8,128)} %block.11, f32[896,128]{1,0:T(8,128)S(1)} %collective-permute-done.6.refs_0_.refs_4_, f32[896,128]{1,0:T(8,128)S(1)} %collective-permute-done.7.refs_1_.refs_5_, ...), custom_call_target="tpu_custom_call" | custom-call | flops 4932501504 | bytes 12845056 | tf_op jit(solution)/shard_map/pallas_call | solution.py:140
  65.3 0.8 broadcast_select_fusion.4
  66.1 0.8 broadcast_select_fusion.6
  67.5 0.7 collective-permute-done.15.refs_3_.refs_7_
  68.2 1.1 collective-permute-done.13.refs_1_.refs_5_
  69.3 1.2 copy-done.22
  70.5 1.0 copy-done.24
  71.5 1.0 copy-done.26
  72.6 7.6 %shard_map.39 = (f32[896,128]{1,0:T(8,128)S(1)}, f32[896,128]{1,0:T(8,128)S(1)}, f32[4,128,128]{2,1,0:T(8,128)S(1)}) custom-call(s32[3]{0:T(128)S(1)} %pad_add_fusion.place, f32[896,7168]{1,0:T(8,128)} %block.11, f32[896,128]{1,0:T(8,128)S(1)} %collective-permute-done.5.refs_0_.refs_4_, f32[896,128]{1,0:T(8,128)} %collective-permute-done.13.refs_1_.refs_5_, ...), custom_call_target="tpu_custom_call" | custom-call | flops 2466250752 | bytes 6422528 | tf_op jit(solution)/shard_map/pallas_call | solution.py:140
  80.2 3.4 %collective-permute-start.16 = (f32[896,128]{1,0:T(8,128)S(1)}, f32[896,128]{1,0:T(8,128)S(1)}, u32[]{:S(2)}, u32[]{:S(2)}) collective-permute-start(f32[896,128]{1,0:T(8,128)S(1)} %get-tuple-element.32), channel_id=1, source_target_pairs={{0,1},{1,0},{2,3},{3,2},{4,5},{5,4},{6,7},{7,6},{8,9},{9,8},{10,11... | collective-permute-start | bytes 1376264 | tf_op jit(solution)/shard_map/ppermute | solution.py:281
  83.7 1.3 collective-permute-done.18
  85.1 9.8 %collective-permute-done.16 = f32[896,128]{1,0:T(8,128)S(1)} collective-permute-done((f32[896,128]{1,0:T(8,128)S(1)}, f32[896,128]{1,0:T(8,128)S(1)}, u32[]{:S(2)}, u32[]{:S(2)}) %collective-permute-start.16) | collective-permute-done | bytes 458784 | tf_op jit(solution)/shard_map/ppermute | solution.py:281
  94.9 0.8 add.27.mine
  95.8 5.1 %collective-permute-start.24 = (f32[896,128]{1,0:T(8,128)}, f32[896,128]{1,0:T(8,128)}, u32[]{:S(2)}, u32[]{:S(2)}) collective-permute-start(f32[896,128]{1,0:T(8,128)} %add.27.mine), channel_id=1, source_target_pairs={{0,0},{1,16},{2,2},{3,18},{4,4},{5,20},{6,6},{7,22},{8,8},{9,24},{... | collective-permute-start | bytes 1376264 | tf_op jit(solution)/shard_map/ppermute | solution.py:293
  100.8 1.4 collective-permute-start.25
  102.3 0.8 collective-permute-start.20
  103.1 4.2 %collective-permute-done.20 = f32[2,128,128]{2,1,0:T(8,128)S(1)} collective-permute-done((f32[2,128,128]{2,1,0:T(8,128)S(1)}, f32[2,128,128]{2,1,0:T(8,128)S(1)}, u32[]{:S(2)}, u32[]{:S(2)}) %collective-permute-start.20) | collective-permute-done | bytes 131104 | tf_op jit(solution)/shard_map/ppermute | solution.py:281
  107.3 0.9 collective-permute-start.21
  108.2 6.0 %collective-permute-done.21 = f32[2,128,128]{2,1,0:T(8,128)S(1)} collective-permute-done((f32[2,128,128]{2,1,0:T(8,128)S(1)}, f32[2,128,128]{2,1,0:T(8,128)S(1)}, u32[]{:S(2)}, u32[]{:S(2)}) %collective-permute-start.21) | collective-permute-done | bytes 131104 | tf_op jit(solution)/shard_map/ppermute | solution.py:281
  114.2 1.1 collective-permute-start.22
  115.3 2.7 %collective-permute-start.17 = (f32[896,128]{1,0:T(8,128)}, f32[896,128]{1,0:T(8,128)}, u32[]{:S(2)}, u32[]{:S(2)}) collective-permute-start(f32[896,128]{1,0:T(8,128)} %add.27.mine), channel_id=1, source_target_pairs={{0,1},{1,0},{2,3},{3,2},{4,5},{5,4},{6,7},{7,6},{8,9},{9,8},{10,11... | collective-permute-start | bytes 1376264 | tf_op jit(solution)/shard_map/ppermute | solution.py:281
  118.0 9.0 %collective-permute-done.22 = f32[2,128,128]{2,1,0:T(8,128)S(1)} collective-permute-done((f32[2,128,128]{2,1,0:T(8,128)S(1)}, f32[2,128,128]{2,1,0:T(8,128)S(1)}, u32[]{:S(2)}, u32[]{:S(2)}) %collective-permute-start.22) | collective-permute-done | bytes 131104 | tf_op jit(solution)/shard_map/ppermute | solution.py:281
  127.9 0.8 collective-permute-done.23
  128.7 0.9 broadcast_select_fusion.9
  130.0 1.8 collective-permute-start.32
  132.0 4.8 %shard_map.40 = (bf16[896,512]{1,0:T(8,128)(2,1)S(1)}, bf16[896,512]{1,0:T(8,128)(2,1)S(1)}) custom-call(s32[3]{0:T(128)S(1)} %pad_add_fusion.place, f32[2,896,128]{2,1,0:T(8,128)S(1)} %copy-done.5, f32[896,128]{1,0:T(8,128)} %add.27.mine, f32[896,128]{1,0:T(8,128)} %collective-permute-done.17.other, f32[4,128,128]{2,1,0:T(8,128)S(1)} %pad_maximum_fusion.inner, ...), custom_call_target="tpu_custom_call" | custom-call | flops 1409286144 | bytes 3670016 | tf_op jit(solution)/shard_map/pallas_call | solution.py:197
  136.9 1.8 collective-permute-start.35
  138.7 1.0 copy-done.18
  139.7 1.0 copy-done.20
  140.7 10.8 %shard_map.42 = (f32[896,7168]{1,0:T(8,128)}, s32[8,128]{1,0:T(8,128)S(1)}) custom-call(s32[3]{0:T(128)S(1)} %pad_add_fusion.place, f32[896,7168]{1,0:T(8,128)} %block.11, bf16[896,512]{1,0:T(8,128)(2,1)S(1)} %get-tuple-element.34.high, bf16[896,512]{1,0:T(8,128)(2,1)S(1)} %get-tuple-element.35.low, f32[896,128]{1,0:T(8,128)} %get-tuple-element.36.refs_0_, ...), custom_call_target="tpu_custom_call" | custom-call | flops 4932501504 | bytes 12845056 | tf_op jit(solution)/shard_map/pallas_call | solution.py:234
  156.6 18.1 %shard_map.43 = (f32[896,7168]{1,0:T(8,128)}, s32[8,128]{1,0:T(8,128)S(1)}) custom-call(s32[3]{0:T(128)S(1)} %pad_add_fusion.place, f32[896,7168]{1,0:T(8,128)} %block.11, bf16[896,512]{1,0:T(8,128)(2,1)} %copy-done, bf16[896,512]{1,0:T(8,128)(2,1)} %copy-done.2, f32[896,128]{1,0:T(8,128)S(1)} %collective-permute-done.30.refs_0_, ...), custom_call_target="tpu_custom_call", output_to_operand_aliasing={{0}: (20, {})} | custom-call | flops 9865003008 | bytes 25690112 | tf_op jit(solution)/shard_map/pallas_call | solution.py:234
  176.7 1.2 collective-permute-done.39.refs_3_
  178.5 1.2 copy-done.1
  179.7 1.2 copy-done.3
  180.9 10.8 %shard_map.44 = (f32[896,7168]{1,0:T(8,128)}, s32[8,128]{1,0:T(8,128)}) custom-call(s32[3]{0:T(128)S(1)} %pad_add_fusion.place, f32[896,7168]{1,0:T(8,128)} %block.11, bf16[896,512]{1,0:T(8,128)(2,1)S(1)} %copy-done.1, bf16[896,512]{1,0:T(8,128)(2,1)S(1)} %copy-done.3, ...), custom_call_target="tpu_custom_call", output_to_operand_aliasing={{0}: (12, {})} | custom-call | flops 4932501504 | bytes 12845056 | tf_op jit(solution)/shard_map/pallas_call | solution.py:234
  (119 shorter events, 11.2 us)
Async XLA Ops:
  1.2 7.3 %collective-permute-start = (f32[896,128]{1,0:T(8,128)S(1)}, f32[896,128]{1,0:T(8,128)S(1)}, u32[]{:S(2)}, u32[]{:S(2)}) collective-permute-start(f32[896,128]{1,0:T(8,128)S(1)} %get-tuple-element.44), channel_id=1, source_target_pairs={{0,0},{1,16},{2,2},{3,18},{4,4},{5,20},{6,6},{7,22},{8,8},{9,24},{... | collective-permute-start | bytes 1376264 | tf_op jit(solution)/shard_map/ppermute | solution.py:293
  1.9 17.0 %collective-permute-start.2 = (f32[896,128]{1,0:T(8,128)S(1)}, f32[896,128]{1,0:T(8,128)S(1)}, u32[]{:S(2)}, u32[]{:S(2)}) collective-permute-start(f32[896,128]{1,0:T(8,128)S(1)} %get-tuple-element.43), channel_id=1, source_target_pairs={{0,16},{1,0},{2,18},{3,2},{4,20},{5,4},{6,22},{7,6},{8,24},{9,8},{... | collective-permute-start | bytes 1376264 | tf_op jit(solution)/shard_map/ppermute | solution.py:293
  8.5 43.3 %copy-start.15 = (f32[896,128]{1,0:T(8,128)}, f32[896,128]{1,0:T(8,128)S(1)}, u32[]{:S(2)}) copy-start(f32[896,128]{1,0:T(8,128)S(1)} %collective-permute-done.refs_0_.refs_4_) | copy-start | bytes 1376260
  8.5 22.4 %collective-permute-start.1 = (f32[896,128]{1,0:T(8,128)S(1)}, f32[896,128]{1,0:T(8,128)S(1)}, u32[]{:S(2)}, u32[]{:S(2)}) collective-permute-start(f32[896,128]{1,0:T(8,128)S(1)} %collective-permute-done.refs_0_.refs_4_), channel_id=1, source_target_pairs={{0,2},{1,3},{2,0},{3,1},{4,6},{5,7},{6,4},{7,5},{8,10},{9,11},{10,... | collective-permute-start | bytes 1376264 | tf_op jit(solution)/shard_map/ppermute | solution.py:281
  18.9 33.8 %copy-start.17 = (f32[896,128]{1,0:T(8,128)}, f32[896,128]{1,0:T(8,128)S(1)}, u32[]{:S(2)}) copy-start(f32[896,128]{1,0:T(8,128)S(1)} %collective-permute-done.2.refs_2_.refs_6_) | copy-start | bytes 1376260
  18.9 12.6 %collective-permute-start.3 = (f32[896,128]{1,0:T(8,128)S(1)}, f32[896,128]{1,0:T(8,128)}, u32[]{:S(2)}, u32[]{:S(2)}) collective-permute-start(f32[896,128]{1,0:T(8,128)S(1)} %collective-permute-done.2.refs_2_.refs_6_), channel_id=1, source_target_pairs={{0,2},{1,3},{2,0},{3,1},{4,6},{5,7},{6,4},{7,5},{8,10},{9,11},{10,... | collective-permute-start | bytes 1376264 | tf_op jit(solution)/shard_map/ppermute | solution.py:281
  18.9 21.7 %collective-permute-start.4 = (f32[896,128]{1,0:T(8,128)S(1)}, f32[896,128]{1,0:T(8,128)S(1)}, u32[]{:S(2)}, u32[]{:S(2)}) collective-permute-start(f32[896,128]{1,0:T(8,128)S(1)} %collective-permute-done.refs_0_.refs_4_), channel_id=1, source_target_pairs={{0,8},{1,9},{2,10},{3,11},{4,12},{5,13},{6,14},{7,15},{8,0},{9,1},... | collective-permute-start | bytes 1376264 | tf_op jit(solution)/shard_map/ppermute | solution.py:281
  29.3 13.4 %collective-permute-start.8 = (f32[896,128]{1,0:T(8,128)S(1)}, f32[896,128]{1,0:T(8,128)S(1)}, u32[]{:S(2)}, u32[]{:S(2)}) collective-permute-start(f32[896,128]{1,0:T(8,128)S(1)} %collective-permute-done.2.refs_2_.refs_6_), channel_id=1, source_target_pairs={{0,4},{1,5},{2,6},{3,7},{4,0},{5,1},{6,2},{7,3},{8,12},{9,13},{10,... | collective-permute-start | bytes 1376264 | tf_op jit(solution)/shard_map/ppermute | solution.py:281
  30.8 19.5 %collective-permute-start.11 = (f32[896,128]{1,0:T(8,128)S(1)}, f32[896,128]{1,0:T(8,128)S(1)}, u32[]{:S(2)}, u32[]{:S(2)}) collective-permute-start(f32[896,128]{1,0:T(8,128)S(1)} %collective-permute-done.2.refs_2_.refs_6_), channel_id=1, source_target_pairs={{0,8},{1,9},{2,10},{3,11},{4,12},{5,13},{6,14},{7,15},{8,0},{9,1},... | collective-permute-start | bytes 1376264 | tf_op jit(solution)/shard_map/ppermute | solution.py:281
  30.9 20.9 %collective-permute-start.6 = (f32[896,128]{1,0:T(8,128)S(1)}, f32[896,128]{1,0:T(8,128)S(1)}, u32[]{:S(2)}, u32[]{:S(2)}) collective-permute-start(f32[896,128]{1,0:T(8,128)S(1)} %collective-permute-done.refs_0_.refs_4_), channel_id=1, source_target_pairs={{0,4},{1,5},{2,6},{3,7},{4,0},{5,1},{6,2},{7,3},{8,12},{9,13},{10,... | collective-permute-start | bytes 1376264 | tf_op jit(solution)/shard_map/ppermute | solution.py:281
  38.8 28.2 %copy-start.23 = (bf16[2,256,448]{2,1,0:T(8,128)(2,1)}, bf16[2,256,448]{2,1,0:T(8,128)(2,1)S(1)}, u32[]{:S(2)}) copy-start(bf16[2,256,448]{2,1,0:T(8,128)(2,1)S(1)} %get-tuple-element.28.refs_5_) | copy-start | bytes 1376260
  40.7 12.0 %collective-permute-start.10 = (f32[896,128]{1,0:T(8,128)S(1)}, f32[896,128]{1,0:T(8,128)S(1)}, u32[]{:S(2)}, u32[]{:S(2)}) collective-permute-start(f32[896,128]{1,0:T(8,128)S(1)} %collective-permute-done.4.refs_4_.refs_12_), channel_id=1, source_target_pairs={{0,2},{1,3},{2,0},{3,1},{4,6},{5,7},{6,4},{7,5},{8,10},{9,11},{10,... | collective-permute-start | bytes 1376264 | tf_op jit(solution)/shard_map/ppermute | solution.py:281
  42.7 11.7 %collective-permute-start.9 = (f32[896,128]{1,0:T(8,128)S(1)}, f32[896,128]{1,0:T(8,128)S(1)}, u32[]{:S(2)}, u32[]{:S(2)}) collective-permute-start(f32[896,128]{1,0:T(8,128)S(1)} %collective-permute-done.8.refs_2_.refs_6_), channel_id=1, source_target_pairs={{0,2},{1,3},{2,0},{3,1},{4,6},{5,7},{6,4},{7,5},{8,10},{9,11},{10,... | collective-permute-start | bytes 1376264 | tf_op jit(solution)/shard_map/ppermute | solution.py:281
  50.3 29.8 %copy-start.6 = (f32[896,128]{1,0:T(8,128)}, f32[896,128]{1,0:T(8,128)S(1)}, u32[]{:S(2)}) copy-start(f32[896,128]{1,0:T(8,128)S(1)} %collective-permute-done.11.refs_6_.refs_14_) | copy-start | bytes 1376260
  50.3 4.0 %collective-permute-start.12 = (f32[896,128]{1,0:T(8,128)S(1)}, f32[896,128]{1,0:T(8,128)S(1)}, u32[]{:S(2)}, u32[]{:S(2)}) collective-permute-start(f32[896,128]{1,0:T(8,128)S(1)} %collective-permute-done.11.refs_6_.refs_14_), channel_id=1, source_target_pairs={{0,2},{1,3},{2,0},{3,1},{4,6},{5,7},{6,4},{7,5},{8,10},{9,11},{10,... | collective-permute-start | bytes 1376264 | tf_op jit(solution)/shard_map/ppermute | solution.py:281
  51.8 28.4 %copy-start.7 = (f32[896,128]{1,0:T(8,128)}, f32[896,128]{1,0:T(8,128)S(1)}, u32[]{:S(2)}) copy-start(f32[896,128]{1,0:T(8,128)S(1)} %collective-permute-done.6.refs_0_.refs_4_) | copy-start | bytes 1376260
  51.8 2.6 %collective-permute-start.7 = (f32[896,128]{1,0:T(8,128)S(1)}, f32[896,128]{1,0:T(8,128)S(1)}, u32[]{:S(2)}, u32[]{:S(2)}) collective-permute-start(f32[896,128]{1,0:T(8,128)S(1)} %collective-permute-done.6.refs_0_.refs_4_), channel_id=1, source_target_pairs={{0,2},{1,3},{2,0},{3,1},{4,6},{5,7},{6,4},{7,5},{8,10},{9,11},{10,... | collective-permute-start | bytes 1376264 | tf_op jit(solution)/shard_map/ppermute | solution.py:281
  51.8 13.4 %collective-permute-start.14 = (f32[896,128]{1,0:T(8,128)S(1)}, f32[896,128]{1,0:T(8,128)S(1)}, u32[]{:S(2)}, u32[]{:S(2)}) collective-permute-start(f32[896,128]{1,0:T(8,128)S(1)} %broadcast_select_fusion.5), channel_id=1, source_target_pairs={{0,8},{1,9},{2,10},{3,11},{4,12},{5,13},{6,14},{7,15},{8,0},{9,1},... | collective-permute-start | bytes 1376264 | tf_op jit(solution)/shard_map/ppermute | solution.py:281
  52.7 13.3 %collective-permute-start.5 = (f32[896,128]{1,0:T(8,128)S(1)}, f32[896,128]{1,0:T(8,128)S(1)}, u32[]{:S(2)}, u32[]{:S(2)}) collective-permute-start(f32[896,128]{1,0:T(8,128)S(1)} %broadcast_select_fusion.7), channel_id=1, source_target_pairs={{0,4},{1,5},{2,6},{3,7},{4,0},{5,1},{6,2},{7,3},{8,12},{9,13},{10,... | collective-permute-start | bytes 1376264 | tf_op jit(solution)/shard_map/ppermute | solution.py:281
  66.1 2.2 %collective-permute-start.15 = (f32[896,128]{1,0:T(8,128)}, f32[896,128]{1,0:T(8,128)}, u32[]{:S(2)}, u32[]{:S(2)}) collective-permute-start(f32[896,128]{1,0:T(8,128)} %broadcast_select_fusion.4), channel_id=1, source_target_pairs={{0,2},{1,3},{2,0},{3,1},{4,6},{5,7},{6,4},{7,5},{8,10},{9,11},{10,... | collective-permute-start | bytes 1376264 | tf_op jit(solution)/shard_map/ppermute | solution.py:281
  66.9 2.4 %collective-permute-start.13 = (f32[896,128]{1,0:T(8,128)}, f32[896,128]{1,0:T(8,128)}, u32[]{:S(2)}, u32[]{:S(2)}) collective-permute-start(f32[896,128]{1,0:T(8,128)} %broadcast_select_fusion.6), channel_id=1, source_target_pairs={{0,2},{1,3},{2,0},{3,1},{4,6},{5,7},{6,4},{7,5},{8,10},{9,11},{10,... | collective-permute-start | bytes 1376264 | tf_op jit(solution)/shard_map/ppermute | solution.py:281
  80.2 14.8 %collective-permute-start.16 = (f32[896,128]{1,0:T(8,128)S(1)}, f32[896,128]{1,0:T(8,128)S(1)}, u32[]{:S(2)}, u32[]{:S(2)}) collective-permute-start(f32[896,128]{1,0:T(8,128)S(1)} %get-tuple-element.32), channel_id=1, source_target_pairs={{0,1},{1,0},{2,3},{3,2},{4,5},{5,4},{6,7},{7,6},{8,9},{9,8},{10,11... | collective-permute-start | bytes 1376264 | tf_op jit(solution)/shard_map/ppermute | solution.py:281
  83.6 1.4 collective-permute-start.18
  85.0 17.2 %collective-permute-start.19 = (f32[2,128,128]{2,1,0:T(8,128)S(1)}, f32[2,128,128]{2,1,0:T(8,128)S(1)}, u32[]{:S(2)}, u32[]{:S(2)}) collective-permute-start(f32[2,128,128]{2,1,0:T(8,128)S(1)} %select_add_fusion), channel_id=1, source_target_pairs={{0,1},{1,0},{2,3},{3,2},{4,5},{5,4},{6,7},{7,6},{8,9},{9,8},{10,11... | collective-permute-start | bytes 393224 | tf_op jit(solution)/shard_map/ppermute | solution.py:281
  95.8 31.5 %collective-permute-start.24 = (f32[896,128]{1,0:T(8,128)}, f32[896,128]{1,0:T(8,128)}, u32[]{:S(2)}, u32[]{:S(2)}) collective-permute-start(f32[896,128]{1,0:T(8,128)} %add.27.mine), channel_id=1, source_target_pairs={{0,0},{1,16},{2,2},{3,18},{4,4},{5,20},{6,6},{7,22},{8,8},{9,24},{... | collective-permute-start | bytes 1376264 | tf_op jit(solution)/shard_map/ppermute | solution.py:293
  100.8 26.4 %collective-permute-start.25 = (f32[896,128]{1,0:T(8,128)}, f32[896,128]{1,0:T(8,128)}, u32[]{:S(2)}, u32[]{:S(2)}) collective-permute-start(f32[896,128]{1,0:T(8,128)} %add.27.mine), channel_id=1, source_target_pairs={{0,16},{1,0},{2,18},{3,2},{4,20},{5,4},{6,22},{7,6},{8,24},{9,8},{... | collective-permute-start | bytes 1376264 | tf_op jit(solution)/shard_map/ppermute | solution.py:293
  102.3 5.0 %collective-permute-start.20 = (f32[2,128,128]{2,1,0:T(8,128)S(1)}, f32[2,128,128]{2,1,0:T(8,128)S(1)}, u32[]{:S(2)}, u32[]{:S(2)}) collective-permute-start(f32[2,128,128]{2,1,0:T(8,128)S(1)} %add.30), channel_id=1, source_target_pairs={{0,4},{1,5},{2,6},{3,7},{4,0},{5,1},{6,2},{7,3},{8,12},{9,13},{10,... | collective-permute-start | bytes 393224 | tf_op jit(solution)/shard_map/ppermute | solution.py:281
  107.3 6.9 %collective-permute-start.21 = (f32[2,128,128]{2,1,0:T(8,128)S(1)}, f32[2,128,128]{2,1,0:T(8,128)S(1)}, u32[]{:S(2)}, u32[]{:S(2)}) collective-permute-start(f32[2,128,128]{2,1,0:T(8,128)S(1)} %add.31), channel_id=1, source_target_pairs={{0,8},{1,9},{2,10},{3,11},{4,12},{5,13},{6,14},{7,15},{8,0},{9,1},... | collective-permute-start | bytes 393224 | tf_op jit(solution)/shard_map/ppermute | solution.py:281
  114.2 12.9 %collective-permute-start.22 = (f32[2,128,128]{2,1,0:T(8,128)S(1)}, f32[2,128,128]{2,1,0:T(8,128)S(1)}, u32[]{:S(2)}, u32[]{:S(2)}) collective-permute-start(f32[2,128,128]{2,1,0:T(8,128)S(1)} %add.32), channel_id=1, source_target_pairs={{0,16},{1,17},{2,18},{3,19},{4,20},{5,21},{6,22},{7,23},{8,24},{9,... | collective-permute-start | bytes 393224 | tf_op jit(solution)/shard_map/ppermute | solution.py:281
  115.3 16.4 %collective-permute-start.17 = (f32[896,128]{1,0:T(8,128)}, f32[896,128]{1,0:T(8,128)}, u32[]{:S(2)}, u32[]{:S(2)}) collective-permute-start(f32[896,128]{1,0:T(8,128)} %add.27.mine), channel_id=1, source_target_pairs={{0,1},{1,0},{2,3},{3,2},{4,5},{5,4},{6,7},{7,6},{8,9},{9,8},{10,11... | collective-permute-start | bytes 1376264 | tf_op jit(solution)/shard_map/ppermute | solution.py:281
  127.1 1.5 collective-permute-start.23
  127.3 29.3 %copy-start.8 = (f32[896,128]{1,0:T(8,128)S(1)}, f32[896,128]{1,0:T(8,128)}, u32[]{:S(2)}) copy-start(f32[896,128]{1,0:T(8,128)} %copy-done.7) | copy-start | bytes 1376260
  127.3 29.3 %copy-start.11 = (f32[896,128]{1,0:T(8,128)S(1)}, f32[896,128]{1,0:T(8,128)}, u32[]{:S(2)}) copy-start(f32[896,128]{1,0:T(8,128)} %copy-done.10) | copy-start | bytes 1376260
  127.3 29.3 %copy-start.14 = (f32[896,128]{1,0:T(8,128)S(1)}, f32[896,128]{1,0:T(8,128)}, u32[]{:S(2)}) copy-start(f32[896,128]{1,0:T(8,128)} %copy-done.13) | copy-start | bytes 1376260
  127.3 9.6 %collective-permute-start.26 = (f32[896,128]{1,0:T(8,128)}, f32[896,128]{1,0:T(8,128)S(1)}, u32[]{:S(2)}, u32[]{:S(2)}) collective-permute-start(f32[896,128]{1,0:T(8,128)} %get-tuple-element.36.refs_0_), channel_id=1, source_target_pairs={{0,2},{1,3},{2,0},{3,1},{4,6},{5,7},{6,4},{7,5},{8,10},{9,11},{10,... | collective-permute-start | bytes 1376264 | tf_op jit(solution)/shard_map/ppermute | solution.py:281
  127.8 10.9 %collective-permute-start.27 = (f32[896,128]{1,0:T(8,128)}, f32[896,128]{1,0:T(8,128)S(1)}, u32[]{:S(2)}, u32[]{:S(2)}) collective-permute-start(f32[896,128]{1,0:T(8,128)} %get-tuple-element.37.refs_2_), channel_id=1, source_target_pairs={{0,2},{1,3},{2,0},{3,1},{4,6},{5,7},{6,4},{7,5},{8,10},{9,11},{10,... | collective-permute-start | bytes 1376264 | tf_op jit(solution)/shard_map/ppermute | solution.py:281
  129.6 23.0 %collective-permute-start.30 = (f32[896,128]{1,0:T(8,128)}, f32[896,128]{1,0:T(8,128)S(1)}, u32[]{:S(2)}, u32[]{:S(2)}) collective-permute-start(f32[896,128]{1,0:T(8,128)} %get-tuple-element.36.refs_0_), channel_id=1, source_target_pairs={{0,4},{1,5},{2,6},{3,7},{4,0},{5,1},{6,2},{7,3},{8,12},{9,13},{10,... | collective-permute-start | bytes 1376264 | tf_op jit(solution)/shard_map/ppermute | solution.py:281
  130.0 22.8 %collective-permute-start.32 = (f32[896,128]{1,0:T(8,128)}, f32[896,128]{1,0:T(8,128)S(1)}, u32[]{:S(2)}, u32[]{:S(2)}) collective-permute-start(f32[896,128]{1,0:T(8,128)} %get-tuple-element.37.refs_2_), channel_id=1, source_target_pairs={{0,4},{1,5},{2,6},{3,7},{4,0},{5,1},{6,2},{7,3},{8,12},{9,13},{10,... | collective-permute-start | bytes 1376264 | tf_op jit(solution)/shard_map/ppermute | solution.py:281
  131.7 21.5 %collective-permute-start.28 = (f32[896,128]{1,0:T(8,128)}, f32[896,128]{1,0:T(8,128)S(1)}, u32[]{:S(2)}, u32[]{:S(2)}) collective-permute-start(f32[896,128]{1,0:T(8,128)} %get-tuple-element.36.refs_0_), channel_id=1, source_target_pairs={{0,8},{1,9},{2,10},{3,11},{4,12},{5,13},{6,14},{7,15},{8,0},{9,1},... | collective-permute-start | bytes 1376264 | tf_op jit(solution)/shard_map/ppermute | solution.py:281
  136.9 16.9 %collective-permute-start.35 = (f32[896,128]{1,0:T(8,128)}, f32[896,128]{1,0:T(8,128)S(1)}, u32[]{:S(2)}, u32[]{:S(2)}) collective-permute-start(f32[896,128]{1,0:T(8,128)} %get-tuple-element.37.refs_2_), channel_id=1, source_target_pairs={{0,8},{1,9},{2,10},{3,11},{4,12},{5,13},{6,14},{7,15},{8,0},{9,1},... | collective-permute-start | bytes 1376264 | tf_op jit(solution)/shard_map/ppermute | solution.py:281
  152.7 1.9 collective-permute-start.31
  152.8 2.4 %collective-permute-start.33 = (f32[896,128]{1,0:T(8,128)S(1)}, f32[896,128]{1,0:T(8,128)S(1)}, u32[]{:S(2)}, u32[]{:S(2)}) collective-permute-start(f32[896,128]{1,0:T(8,128)S(1)} %collective-permute-done.32.refs_2_), channel_id=1, source_target_pairs={{0,2},{1,3},{2,0},{3,1},{4,6},{5,7},{6,4},{7,5},{8,10},{9,11},{10,... | collective-permute-start | bytes 1376264 | tf_op jit(solution)/shard_map/ppermute | solution.py:281
  153.3 2.6 %collective-permute-start.34 = (f32[896,128]{1,0:T(8,128)S(1)}, f32[896,128]{1,0:T(8,128)S(1)}, u32[]{:S(2)}, u32[]{:S(2)}) collective-permute-start(f32[896,128]{1,0:T(8,128)S(1)} %collective-permute-done.28.refs_8_), channel_id=1, source_target_pairs={{0,2},{1,3},{2,0},{3,1},{4,6},{5,7},{6,4},{7,5},{8,10},{9,11},{10,... | collective-permute-start | bytes 1376264 | tf_op jit(solution)/shard_map/ppermute | solution.py:281
  153.8 2.8 %collective-permute-start.36 = (f32[896,128]{1,0:T(8,128)S(1)}, f32[896,128]{1,0:T(8,128)S(1)}, u32[]{:S(2)}, u32[]{:S(2)}) collective-permute-start(f32[896,128]{1,0:T(8,128)S(1)} %collective-permute-done.35.refs_10_), channel_id=1, source_target_pairs={{0,2},{1,3},{2,0},{3,1},{4,6},{5,7},{6,4},{7,5},{8,10},{9,11},{10,... | collective-permute-start | bytes 1376264 | tf_op jit(solution)/shard_map/ppermute | solution.py:281
  153.8 22.1 %collective-permute-start.38 = (f32[896,128]{1,0:T(8,128)S(1)}, f32[896,128]{1,0:T(8,128)S(1)}, u32[]{:S(2)}, u32[]{:S(2)}) collective-permute-start(f32[896,128]{1,0:T(8,128)S(1)} %broadcast_select_fusion.1), channel_id=1, source_target_pairs={{0,8},{1,9},{2,10},{3,11},{4,12},{5,13},{6,14},{7,15},{8,0},{9,1},... | collective-permute-start | bytes 1376264 | tf_op jit(solution)/shard_map/ppermute | solution.py:281
  154.6 21.6 %collective-permute-start.29 = (f32[896,128]{1,0:T(8,128)S(1)}, f32[896,128]{1,0:T(8,128)S(1)}, u32[]{:S(2)}, u32[]{:S(2)}) collective-permute-start(f32[896,128]{1,0:T(8,128)S(1)} %broadcast_select_fusion.3), channel_id=1, source_target_pairs={{0,4},{1,5},{2,6},{3,7},{4,0},{5,1},{6,2},{7,3},{8,12},{9,13},{10,... | collective-permute-start | bytes 1376264 | tf_op jit(solution)/shard_map/ppermute | solution.py:281
  176.0 1.9 collective-permute-start.39
  176.2 2.3 %collective-permute-start.37 = (f32[896,128]{1,0:T(8,128)S(1)}, f32[896,128]{1,0:T(8,128)S(1)}, u32[]{:S(2)}, u32[]{:S(2)}) collective-permute-start(f32[896,128]{1,0:T(8,128)S(1)} %broadcast_select_fusion.2), channel_id=1, source_target_pairs={{0,2},{1,3},{2,0},{3,1},{4,6},{5,7},{6,4},{7,5},{8,10},{9,11},{10,... | collective-permute-start | bytes 1376264 | tf_op jit(solution)/shard_map/ppermute | solution.py:281
  (20 other events, 176.7 us)

commit v4 on v3

--- a/solution.py
+++ b/solution.py
@@ -12,7 +12,7 @@
 PLAIN = (((1,), (0,)), ((), ()))
 BOTH_LAST = (((1,), (1,)), ((), ()))
 BOTH_FIRST = (((0,), (0,)), ((), ()))
-VMEM_BYTES = 48 * 1024 * 1024
+VMEM_BYTES = 36 * 1024 * 1024
 GATES = (True, True, True, True)
 FORWARD = ((0,), (2, 4), (6,))
 UPDATE = ((0,), (2, 4), (6,))

time: 193 us -> 190 us (0.984)
    unnamed x56 -> x50, local copies, waits for them, and re-layouts: 8.92 us -> 7.58 us
where the time goes in v4:
time: 190 us; the launch traced here: 189 us
  Pallas kernels  66.7 us (35%)
  waiting for transfers between devices  59 us (31%)
  starting transfers between devices  45.7 us (24%)
  local copies, waits for them, and re-layouts  11 us (6%)
  other arithmetic  3.74 us (2%)
  between operations  2.98 us (2%)
    ppermute x36, waiting for transfers between devices, flip(): lax.ppermute(values, ('row', 'col'), [(n, n ^ mask) for n in range(everyo...  48.6 us
    pallas_call x3, Pallas kernels, update_step(): pl.pallas_call(functools.partial(update_kernel, count), grid_spec=pltpu.P...  38.6 us
    ppermute x36, starting transfers between devices, flip(): lax.ppermute(values, ('row', 'col'), [(n, n ^ mask) for n in range(everyo...  31.9 us
    pallas_call x3, Pallas kernels, forward_step(): pl.pallas_call(functools.partial(forward_kernel, first, last, count, shar...  23.3 us
    ppermute x4, starting transfers between devices, transpose(): return lax.ppermute(values, ('row', 'col'), pairs)  13.7 us
    ppermute x4, waiting for transfers between devices, transpose(): return lax.ppermute(values, ('row', 'col'), pairs)  10.4 us
    unnamed x50, local copies, waits for them, and re-layouts  7.58 us
    pallas_call x1, Pallas kernels, mix(): pl.pallas_call(mix_kernel, in_specs=[pl.BlockSpec(memory_space=pltpu.SMEM...  4.81 us
  transfers between devices with their start and end apart: 40, of which 19 were waited for; matrix products, arithmetic and copies ran while one was open for 3% of the time, Pallas kernels for 26%

profile of v4, /device:TPU:0, one launch (start us, length us, event | category | flops | bytes accessed | tf_op | source)
XLA Modules:
  0.0 189.1 jit_solution(7272044947231542262)
XLA Ops:
  0.0 1.2 slice_bitcast_fusion
  1.2 0.7 collective-permute-start
  1.9 6.6 %collective-permute-start.2 = (f32[896,128]{1,0:T(8,128)S(1)}, f32[896,128]{1,0:T(8,128)S(1)}, u32[]{:S(2)}, u32[]{:S(2)}) collective-permute-start(f32[896,128]{1,0:T(8,128)S(1)} %get-tuple-element.43), channel_id=1, source_target_pairs={{0,16},{1,0},{2,18},{3,2},{4,20},{5,4},{6,22},{7,6},{8,24},{9,8},{... | collective-permute-start | bytes 1376264 | tf_op jit(solution)/shard_map/ppermute | solution.py:293
  8.5 10.4 %collective-permute-done.2.refs_2_.refs_6_ = f32[896,128]{1,0:T(8,128)S(1)} collective-permute-done((f32[896,128]{1,0:T(8,128)S(1)}, f32[896,128]{1,0:T(8,128)S(1)}, u32[]{:S(2)}, u32[]{:S(2)}) %collective-permute-start.2) | collective-permute-done | bytes 458784 | tf_op jit(solution)/shard_map/ppermute | solution.py:293
  18.9 10.4 %collective-permute-start.4 = (f32[896,128]{1,0:T(8,128)S(1)}, f32[896,128]{1,0:T(8,128)S(1)}, u32[]{:S(2)}, u32[]{:S(2)}) collective-permute-start(f32[896,128]{1,0:T(8,128)S(1)} %collective-permute-done.refs_0_.refs_4_), channel_id=1, source_target_pairs={{0,8},{1,9},{2,10},{3,11},{4,12},{5,13},{6,14},{7,15},{8,0},{9,1},... | collective-permute-start | bytes 1376264 | tf_op jit(solution)/shard_map/ppermute | solution.py:281
  29.3 1.5 collective-permute-start.8
  31.5 1.2 copy-done
  32.7 6.1 %shard_map.37 = (f32[896,256]{1,0:T(8,128)S(1)}, s32[8,128]{1,0:T(8,128)S(1)}, bf16[2,256,448]{2,1,0:T(8,128)(2,1)S(1)}, bf16[2,256,448]{2,1,0:T(8,128)(2,1)S(1)}, f32[128,128]{1,0:T(8,128)S(1)}) custom-call(s32[3]{0:T(128)S(1)} %pad_add_fusion.place, f32[896,7168]{1,0:T(8,128)} %block.11, f32[896,128]{1,0:T(8,128)S(1)} %collective-permute-done.refs_0_.refs_4_, ...), custom_call_target="tpu_custom_call" | custom-call | flops 2466250752 | bytes 6422528 | tf_op jit(solution)/shard_map/pallas_call | solution.py:140
  40.0 0.7 collective-permute-done.4.refs_4_.refs_12_
  40.7 2.0 %collective-permute-done.8.refs_2_.refs_6_ = f32[896,128]{1,0:T(8,128)S(1)} collective-permute-done((f32[896,128]{1,0:T(8,128)S(1)}, f32[896,128]{1,0:T(8,128)S(1)}, u32[]{:S(2)}, u32[]{:S(2)}) %collective-permute-start.8) | collective-permute-done | bytes 458784 | tf_op jit(solution)/shard_map/ppermute | solution.py:281
  42.7 7.6 %collective-permute-done.11.refs_6_.refs_14_ = f32[896,128]{1,0:T(8,128)S(1)} collective-permute-done((f32[896,128]{1,0:T(8,128)S(1)}, f32[896,128]{1,0:T(8,128)S(1)}, u32[]{:S(2)}, u32[]{:S(2)}) %collective-permute-start.11) | collective-permute-done | bytes 458784 | tf_op jit(solution)/shard_map/ppermute | solution.py:281
  50.3 1.5 collective-permute-done.6.refs_0_.refs_4_
  51.8 0.8 collective-permute-start.14
  52.7 1.6 collective-permute-start.5
  54.4 9.7 %shard_map.38 = (f32[896,256]{1,0:T(8,128)S(1)}, s32[8,128]{1,0:T(8,128)S(1)}) custom-call(s32[3]{0:T(128)S(1)} %pad_add_fusion.place, f32[896,7168]{1,0:T(8,128)} %block.11, f32[896,128]{1,0:T(8,128)S(1)} %collective-permute-done.6.refs_0_.refs_4_, f32[896,128]{1,0:T(8,128)S(1)} %collective-permute-done.7.refs_1_.refs_5_, ...), custom_call_target="tpu_custom_call" | custom-call | flops 4932501504 | bytes 12845056 | tf_op jit(solution)/shard_map/pallas_call | solution.py:140
  65.4 0.8 broadcast_select_fusion.4
  66.2 0.8 broadcast_select_fusion.6
  67.6 0.8 collective-permute-done.15.refs_3_.refs_7_
  68.4 1.0 collective-permute-done.13.refs_1_.refs_5_
  69.4 1.2 copy-done.19
  70.6 1.0 copy-done.21
  71.7 1.0 copy-done.23
  72.7 7.6 %shard_map.39 = (f32[896,128]{1,0:T(8,128)S(1)}, f32[896,128]{1,0:T(8,128)S(1)}, f32[4,128,128]{2,1,0:T(8,128)S(1)}) custom-call(s32[3]{0:T(128)S(1)} %pad_add_fusion.place, f32[896,7168]{1,0:T(8,128)} %block.11, f32[896,128]{1,0:T(8,128)S(1)} %collective-permute-done.5.refs_0_.refs_4_, f32[896,128]{1,0:T(8,128)} %collective-permute-done.13.refs_1_.refs_5_, ...), custom_call_target="tpu_custom_call" | custom-call | flops 2466250752 | bytes 6422528 | tf_op jit(solution)/shard_map/pallas_call | solution.py:140
  80.3 3.4 %collective-permute-start.16 = (f32[896,128]{1,0:T(8,128)S(1)}, f32[896,128]{1,0:T(8,128)S(1)}, u32[]{:S(2)}, u32[]{:S(2)}) collective-permute-start(f32[896,128]{1,0:T(8,128)S(1)} %get-tuple-element.32), channel_id=1, source_target_pairs={{0,1},{1,0},{2,3},{3,2},{4,5},{5,4},{6,7},{7,6},{8,9},{9,8},{10,11... | collective-permute-start | bytes 1376264 | tf_op jit(solution)/shard_map/ppermute | solution.py:281
  83.9 1.3 collective-permute-done.18
  85.3 9.8 %collective-permute-done.16 = f32[896,128]{1,0:T(8,128)S(1)} collective-permute-done((f32[896,128]{1,0:T(8,128)S(1)}, f32[896,128]{1,0:T(8,128)S(1)}, u32[]{:S(2)}, u32[]{:S(2)}) %collective-permute-start.16) | collective-permute-done | bytes 458784 | tf_op jit(solution)/shard_map/ppermute | solution.py:281
  95.1 0.8 add.27.mine
  95.9 5.1 %collective-permute-start.24 = (f32[896,128]{1,0:T(8,128)}, f32[896,128]{1,0:T(8,128)}, u32[]{:S(2)}, u32[]{:S(2)}) collective-permute-start(f32[896,128]{1,0:T(8,128)} %add.27.mine), channel_id=1, source_target_pairs={{0,0},{1,16},{2,2},{3,18},{4,4},{5,20},{6,6},{7,22},{8,8},{9,24},{... | collective-permute-start | bytes 1376264 | tf_op jit(solution)/shard_map/ppermute | solution.py:293
  100.9 1.4 collective-permute-start.25
  103.0 4.4 %collective-permute-done.20 = f32[2,128,128]{2,1,0:T(8,128)S(1)} collective-permute-done((f32[2,128,128]{2,1,0:T(8,128)S(1)}, f32[2,128,128]{2,1,0:T(8,128)S(1)}, u32[]{:S(2)}, u32[]{:S(2)}) %collective-permute-start.20) | collective-permute-done | bytes 131104 | tf_op jit(solution)/shard_map/ppermute | solution.py:281
  107.4 0.8 collective-permute-start.21
  108.3 6.1 %collective-permute-done.21 = f32[2,128,128]{2,1,0:T(8,128)S(1)} collective-permute-done((f32[2,128,128]{2,1,0:T(8,128)S(1)}, f32[2,128,128]{2,1,0:T(8,128)S(1)}, u32[]{:S(2)}, u32[]{:S(2)}) %collective-permute-start.21) | collective-permute-done | bytes 131104 | tf_op jit(solution)/shard_map/ppermute | solution.py:281
  114.4 1.1 collective-permute-start.22
  115.4 2.7 %collective-permute-start.17 = (f32[896,128]{1,0:T(8,128)}, f32[896,128]{1,0:T(8,128)}, u32[]{:S(2)}, u32[]{:S(2)}) collective-permute-start(f32[896,128]{1,0:T(8,128)} %add.27.mine), channel_id=1, source_target_pairs={{0,1},{1,0},{2,3},{3,2},{4,5},{5,4},{6,7},{7,6},{8,9},{9,8},{10,11... | collective-permute-start | bytes 1376264 | tf_op jit(solution)/shard_map/ppermute | solution.py:281
  118.2 9.0 %collective-permute-done.22 = f32[2,128,128]{2,1,0:T(8,128)S(1)} collective-permute-done((f32[2,128,128]{2,1,0:T(8,128)S(1)}, f32[2,128,128]{2,1,0:T(8,128)S(1)}, u32[]{:S(2)}, u32[]{:S(2)}) %collective-permute-start.22) | collective-permute-done | bytes 131104 | tf_op jit(solution)/shard_map/ppermute | solution.py:281
  128.0 0.8 collective-permute-done.23
  128.8 0.9 broadcast_select_fusion.9
  130.3 1.6 collective-permute-start.32
  132.1 4.8 %shard_map.40 = (bf16[896,512]{1,0:T(8,128)(2,1)S(1)}, bf16[896,512]{1,0:T(8,128)(2,1)S(1)}) custom-call(s32[3]{0:T(128)S(1)} %pad_add_fusion.place, f32[2,896,128]{2,1,0:T(8,128)S(1)} %copy-done.1, f32[896,128]{1,0:T(8,128)} %add.27.mine, f32[896,128]{1,0:T(8,128)} %collective-permute-done.17.other, f32[4,128,128]{2,1,0:T(8,128)S(1)} %pad_maximum_fusion.inner, ...), custom_call_target="tpu_custom_call" | custom-call | flops 1409286144 | bytes 3670016 | tf_op jit(solution)/shard_map/pallas_call | solution.py:197
  136.9 1.8 collective-permute-start.35
  138.8 1.0 copy-done.13
  139.8 1.0 copy-done.15
  140.8 1.0 copy-done.17
  141.8 10.8 %shard_map.42 = (f32[896,7168]{1,0:T(8,128)}, s32[8,128]{1,0:T(8,128)S(1)}) custom-call(s32[3]{0:T(128)S(1)} %pad_add_fusion.place, f32[896,7168]{1,0:T(8,128)} %block.11, bf16[896,512]{1,0:T(8,128)(2,1)S(1)} %get-tuple-element.34.high, bf16[896,512]{1,0:T(8,128)(2,1)S(1)} %get-tuple-element.35.low, f32[896,128]{1,0:T(8,128)} %get-tuple-element.36.refs_0_, ...), custom_call_target="tpu_custom_call" | custom-call | flops 4932501504 | bytes 12845056 | tf_op jit(solution)/shard_map/pallas_call | solution.py:234
  157.6 17.1 %shard_map.43 = (f32[896,7168]{1,0:T(8,128)}, s32[8,128]{1,0:T(8,128)S(1)}) custom-call(s32[3]{0:T(128)S(1)} %pad_add_fusion.place, f32[896,7168]{1,0:T(8,128)} %block.11, bf16[896,512]{1,0:T(8,128)(2,1)S(1)} %get-tuple-element.34.high, bf16[896,512]{1,0:T(8,128)(2,1)S(1)} %get-tuple-element.35.low, ...), custom_call_target="tpu_custom_call", output_to_operand_aliasing={{0}: (20, {})} | custom-call | flops 9865003008 | bytes 25690112 | tf_op jit(solution)/shard_map/pallas_call | solution.py:234
  176.6 1.2 collective-permute-done.39.refs_3_
  177.8 0.7 collective-permute-done.37.refs_1_
  178.5 10.7 %shard_map.44 = (f32[896,7168]{1,0:T(8,128)}, s32[8,128]{1,0:T(8,128)}) custom-call(s32[3]{0:T(128)S(1)} %pad_add_fusion.place, f32[896,7168]{1,0:T(8,128)} %block.11, bf16[896,512]{1,0:T(8,128)(2,1)S(1)} %get-tuple-element.34.high, bf16[896,512]{1,0:T(8,128)(2,1)S(1)} %get-tuple-element.35.low, ...), custom_call_target="tpu_custom_call", output_to_operand_aliasing={{0}: (12, {})} | custom-call | flops 4932501504 | bytes 12845056 | tf_op jit(solution)/shard_map/pallas_call | solution.py:234
  (113 shorter events, 10.7 us)
Async XLA Ops:
  1.2 7.3 %collective-permute-start = (f32[896,128]{1,0:T(8,128)S(1)}, f32[896,128]{1,0:T(8,128)S(1)}, u32[]{:S(2)}, u32[]{:S(2)}) collective-permute-start(f32[896,128]{1,0:T(8,128)S(1)} %get-tuple-element.44), channel_id=1, source_target_pairs={{0,0},{1,16},{2,2},{3,18},{4,4},{5,20},{6,6},{7,22},{8,8},{9,24},{... | collective-permute-start | bytes 1376264 | tf_op jit(solution)/shard_map/ppermute | solution.py:293
  1.9 17.0 %collective-permute-start.2 = (f32[896,128]{1,0:T(8,128)S(1)}, f32[896,128]{1,0:T(8,128)S(1)}, u32[]{:S(2)}, u32[]{:S(2)}) collective-permute-start(f32[896,128]{1,0:T(8,128)S(1)} %get-tuple-element.43), channel_id=1, source_target_pairs={{0,16},{1,0},{2,18},{3,2},{4,20},{5,4},{6,22},{7,6},{8,24},{9,8},{... | collective-permute-start | bytes 1376264 | tf_op jit(solution)/shard_map/ppermute | solution.py:293
  8.5 43.3 %copy-start.12 = (f32[896,128]{1,0:T(8,128)}, f32[896,128]{1,0:T(8,128)S(1)}, u32[]{:S(2)}) copy-start(f32[896,128]{1,0:T(8,128)S(1)} %collective-permute-done.refs_0_.refs_4_) | copy-start | bytes 1376260
  8.5 22.4 %collective-permute-start.1 = (f32[896,128]{1,0:T(8,128)S(1)}, f32[896,128]{1,0:T(8,128)S(1)}, u32[]{:S(2)}, u32[]{:S(2)}) collective-permute-start(f32[896,128]{1,0:T(8,128)S(1)} %collective-permute-done.refs_0_.refs_4_), channel_id=1, source_target_pairs={{0,2},{1,3},{2,0},{3,1},{4,6},{5,7},{6,4},{7,5},{8,10},{9,11},{10,... | collective-permute-start | bytes 1376264 | tf_op jit(solution)/shard_map/ppermute | solution.py:281
  18.9 33.8 %copy-start.14 = (f32[896,128]{1,0:T(8,128)}, f32[896,128]{1,0:T(8,128)S(1)}, u32[]{:S(2)}) copy-start(f32[896,128]{1,0:T(8,128)S(1)} %collective-permute-done.2.refs_2_.refs_6_) | copy-start | bytes 1376260
  18.9 12.6 %collective-permute-start.3 = (f32[896,128]{1,0:T(8,128)S(1)}, f32[896,128]{1,0:T(8,128)}, u32[]{:S(2)}, u32[]{:S(2)}) collective-permute-start(f32[896,128]{1,0:T(8,128)S(1)} %collective-permute-done.2.refs_2_.refs_6_), channel_id=1, source_target_pairs={{0,2},{1,3},{2,0},{3,1},{4,6},{5,7},{6,4},{7,5},{8,10},{9,11},{10,... | collective-permute-start | bytes 1376264 | tf_op jit(solution)/shard_map/ppermute | solution.py:281
  18.9 21.7 %collective-permute-start.4 = (f32[896,128]{1,0:T(8,128)S(1)}, f32[896,128]{1,0:T(8,128)S(1)}, u32[]{:S(2)}, u32[]{:S(2)}) collective-permute-start(f32[896,128]{1,0:T(8,128)S(1)} %collective-permute-done.refs_0_.refs_4_), channel_id=1, source_target_pairs={{0,8},{1,9},{2,10},{3,11},{4,12},{5,13},{6,14},{7,15},{8,0},{9,1},... | collective-permute-start | bytes 1376264 | tf_op jit(solution)/shard_map/ppermute | solution.py:281
  29.3 13.4 %collective-permute-start.8 = (f32[896,128]{1,0:T(8,128)S(1)}, f32[896,128]{1,0:T(8,128)S(1)}, u32[]{:S(2)}, u32[]{:S(2)}) collective-permute-start(f32[896,128]{1,0:T(8,128)S(1)} %collective-permute-done.2.refs_2_.refs_6_), channel_id=1, source_target_pairs={{0,4},{1,5},{2,6},{3,7},{4,0},{5,1},{6,2},{7,3},{8,12},{9,13},{10,... | collective-permute-start | bytes 1376264 | tf_op jit(solution)/shard_map/ppermute | solution.py:281
  30.8 19.5 %collective-permute-start.11 = (f32[896,128]{1,0:T(8,128)S(1)}, f32[896,128]{1,0:T(8,128)S(1)}, u32[]{:S(2)}, u32[]{:S(2)}) collective-permute-start(f32[896,128]{1,0:T(8,128)S(1)} %collective-permute-done.2.refs_2_.refs_6_), channel_id=1, source_target_pairs={{0,8},{1,9},{2,10},{3,11},{4,12},{5,13},{6,14},{7,15},{8,0},{9,1},... | collective-permute-start | bytes 1376264 | tf_op jit(solution)/shard_map/ppermute | solution.py:281
  30.9 20.9 %collective-permute-start.6 = (f32[896,128]{1,0:T(8,128)S(1)}, f32[896,128]{1,0:T(8,128)S(1)}, u32[]{:S(2)}, u32[]{:S(2)}) collective-permute-start(f32[896,128]{1,0:T(8,128)S(1)} %collective-permute-done.refs_0_.refs_4_), channel_id=1, source_target_pairs={{0,4},{1,5},{2,6},{3,7},{4,0},{5,1},{6,2},{7,3},{8,12},{9,13},{10,... | collective-permute-start | bytes 1376264 | tf_op jit(solution)/shard_map/ppermute | solution.py:281
  40.7 12.0 %collective-permute-start.10 = (f32[896,128]{1,0:T(8,128)S(1)}, f32[896,128]{1,0:T(8,128)S(1)}, u32[]{:S(2)}, u32[]{:S(2)}) collective-permute-start(f32[896,128]{1,0:T(8,128)S(1)} %collective-permute-done.4.refs_4_.refs_12_), channel_id=1, source_target_pairs={{0,2},{1,3},{2,0},{3,1},{4,6},{5,7},{6,4},{7,5},{8,10},{9,11},{10,... | collective-permute-start | bytes 1376264 | tf_op jit(solution)/shard_map/ppermute | solution.py:281
  42.7 11.7 %collective-permute-start.9 = (f32[896,128]{1,0:T(8,128)S(1)}, f32[896,128]{1,0:T(8,128)S(1)}, u32[]{:S(2)}, u32[]{:S(2)}) collective-permute-start(f32[896,128]{1,0:T(8,128)S(1)} %collective-permute-done.8.refs_2_.refs_6_), channel_id=1, source_target_pairs={{0,2},{1,3},{2,0},{3,1},{4,6},{5,7},{6,4},{7,5},{8,10},{9,11},{10,... | collective-permute-start | bytes 1376264 | tf_op jit(solution)/shard_map/ppermute | solution.py:281
  50.3 4.0 %collective-permute-start.12 = (f32[896,128]{1,0:T(8,128)S(1)}, f32[896,128]{1,0:T(8,128)S(1)}, u32[]{:S(2)}, u32[]{:S(2)}) collective-permute-start(f32[896,128]{1,0:T(8,128)S(1)} %collective-permute-done.11.refs_6_.refs_14_), channel_id=1, source_target_pairs={{0,2},{1,3},{2,0},{3,1},{4,6},{5,7},{6,4},{7,5},{8,10},{9,11},{10,... | collective-permute-start | bytes 1376264 | tf_op jit(solution)/shard_map/ppermute | solution.py:281
  51.8 28.5 %copy-start.2 = (f32[896,128]{1,0:T(8,128)}, f32[896,128]{1,0:T(8,128)S(1)}, u32[]{:S(2)}) copy-start(f32[896,128]{1,0:T(8,128)S(1)} %collective-permute-done.6.refs_0_.refs_4_) | copy-start | bytes 1376260
  51.8 2.6 %collective-permute-start.7 = (f32[896,128]{1,0:T(8,128)S(1)}, f32[896,128]{1,0:T(8,128)S(1)}, u32[]{:S(2)}, u32[]{:S(2)}) collective-permute-start(f32[896,128]{1,0:T(8,128)S(1)} %collective-permute-done.6.refs_0_.refs_4_), channel_id=1, source_target_pairs={{0,2},{1,3},{2,0},{3,1},{4,6},{5,7},{6,4},{7,5},{8,10},{9,11},{10,... | collective-permute-start | bytes 1376264 | tf_op jit(solution)/shard_map/ppermute | solution.py:281
  51.8 13.6 %collective-permute-start.14 = (f32[896,128]{1,0:T(8,128)S(1)}, f32[896,128]{1,0:T(8,128)S(1)}, u32[]{:S(2)}, u32[]{:S(2)}) collective-permute-start(f32[896,128]{1,0:T(8,128)S(1)} %broadcast_select_fusion.5), channel_id=1, source_target_pairs={{0,8},{1,9},{2,10},{3,11},{4,12},{5,13},{6,14},{7,15},{8,0},{9,1},... | collective-permute-start | bytes 1376264 | tf_op jit(solution)/shard_map/ppermute | solution.py:281
  52.7 13.5 %collective-permute-start.5 = (f32[896,128]{1,0:T(8,128)S(1)}, f32[896,128]{1,0:T(8,128)S(1)}, u32[]{:S(2)}, u32[]{:S(2)}) collective-permute-start(f32[896,128]{1,0:T(8,128)S(1)} %broadcast_select_fusion.7), channel_id=1, source_target_pairs={{0,4},{1,5},{2,6},{3,7},{4,0},{5,1},{6,2},{7,3},{8,12},{9,13},{10,... | collective-permute-start | bytes 1376264 | tf_op jit(solution)/shard_map/ppermute | solution.py:281
  66.2 2.2 %collective-permute-start.15 = (f32[896,128]{1,0:T(8,128)}, f32[896,128]{1,0:T(8,128)}, u32[]{:S(2)}, u32[]{:S(2)}) collective-permute-start(f32[896,128]{1,0:T(8,128)} %broadcast_select_fusion.4), channel_id=1, source_target_pairs={{0,2},{1,3},{2,0},{3,1},{4,6},{5,7},{6,4},{7,5},{8,10},{9,11},{10,... | collective-permute-start | bytes 1376264 | tf_op jit(solution)/shard_map/ppermute | solution.py:281
  67.1 2.4 %collective-permute-start.13 = (f32[896,128]{1,0:T(8,128)}, f32[896,128]{1,0:T(8,128)}, u32[]{:S(2)}, u32[]{:S(2)}) collective-permute-start(f32[896,128]{1,0:T(8,128)} %broadcast_select_fusion.6), channel_id=1, source_target_pairs={{0,2},{1,3},{2,0},{3,1},{4,6},{5,7},{6,4},{7,5},{8,10},{9,11},{10,... | collective-permute-start | bytes 1376264 | tf_op jit(solution)/shard_map/ppermute | solution.py:281
  80.3 14.8 %collective-permute-start.16 = (f32[896,128]{1,0:T(8,128)S(1)}, f32[896,128]{1,0:T(8,128)S(1)}, u32[]{:S(2)}, u32[]{:S(2)}) collective-permute-start(f32[896,128]{1,0:T(8,128)S(1)} %get-tuple-element.32), channel_id=1, source_target_pairs={{0,1},{1,0},{2,3},{3,2},{4,5},{5,4},{6,7},{7,6},{8,9},{9,8},{10,11... | collective-permute-start | bytes 1376264 | tf_op jit(solution)/shard_map/ppermute | solution.py:281
  83.7 1.4 collective-permute-start.18
  85.2 17.2 %collective-permute-start.19 = (f32[2,128,128]{2,1,0:T(8,128)S(1)}, f32[2,128,128]{2,1,0:T(8,128)S(1)}, u32[]{:S(2)}, u32[]{:S(2)}) collective-permute-start(f32[2,128,128]{2,1,0:T(8,128)S(1)} %select_add_fusion), channel_id=1, source_target_pairs={{0,1},{1,0},{2,3},{3,2},{4,5},{5,4},{6,7},{7,6},{8,9},{9,8},{10,11... | collective-permute-start | bytes 393224 | tf_op jit(solution)/shard_map/ppermute | solution.py:281
  95.9 31.4 %collective-permute-start.24 = (f32[896,128]{1,0:T(8,128)}, f32[896,128]{1,0:T(8,128)}, u32[]{:S(2)}, u32[]{:S(2)}) collective-permute-start(f32[896,128]{1,0:T(8,128)} %add.27.mine), channel_id=1, source_target_pairs={{0,0},{1,16},{2,2},{3,18},{4,4},{5,20},{6,6},{7,22},{8,8},{9,24},{... | collective-permute-start | bytes 1376264 | tf_op jit(solution)/shard_map/ppermute | solution.py:293
  100.9 26.4 %collective-permute-start.25 = (f32[896,128]{1,0:T(8,128)}, f32[896,128]{1,0:T(8,128)}, u32[]{:S(2)}, u32[]{:S(2)}) collective-permute-start(f32[896,128]{1,0:T(8,128)} %add.27.mine), channel_id=1, source_target_pairs={{0,16},{1,0},{2,18},{3,2},{4,20},{5,4},{6,22},{7,6},{8,24},{9,8},{... | collective-permute-start | bytes 1376264 | tf_op jit(solution)/shard_map/ppermute | solution.py:293
  102.4 5.0 %collective-permute-start.20 = (f32[2,128,128]{2,1,0:T(8,128)S(1)}, f32[2,128,128]{2,1,0:T(8,128)S(1)}, u32[]{:S(2)}, u32[]{:S(2)}) collective-permute-start(f32[2,128,128]{2,1,0:T(8,128)S(1)} %add.30), channel_id=1, source_target_pairs={{0,4},{1,5},{2,6},{3,7},{4,0},{5,1},{6,2},{7,3},{8,12},{9,13},{10,... | collective-permute-start | bytes 393224 | tf_op jit(solution)/shard_map/ppermute | solution.py:281
  107.4 6.9 %collective-permute-start.21 = (f32[2,128,128]{2,1,0:T(8,128)S(1)}, f32[2,128,128]{2,1,0:T(8,128)S(1)}, u32[]{:S(2)}, u32[]{:S(2)}) collective-permute-start(f32[2,128,128]{2,1,0:T(8,128)S(1)} %add.31), channel_id=1, source_target_pairs={{0,8},{1,9},{2,10},{3,11},{4,12},{5,13},{6,14},{7,15},{8,0},{9,1},... | collective-permute-start | bytes 393224 | tf_op jit(solution)/shard_map/ppermute | solution.py:281
  114.4 12.8 %collective-permute-start.22 = (f32[2,128,128]{2,1,0:T(8,128)S(1)}, f32[2,128,128]{2,1,0:T(8,128)S(1)}, u32[]{:S(2)}, u32[]{:S(2)}) collective-permute-start(f32[2,128,128]{2,1,0:T(8,128)S(1)} %add.32), channel_id=1, source_target_pairs={{0,16},{1,17},{2,18},{3,19},{4,20},{5,21},{6,22},{7,23},{8,24},{9,... | collective-permute-start | bytes 393224 | tf_op jit(solution)/shard_map/ppermute | solution.py:281
  115.4 16.4 %collective-permute-start.17 = (f32[896,128]{1,0:T(8,128)}, f32[896,128]{1,0:T(8,128)}, u32[]{:S(2)}, u32[]{:S(2)}) collective-permute-start(f32[896,128]{1,0:T(8,128)} %add.27.mine), channel_id=1, source_target_pairs={{0,1},{1,0},{2,3},{3,2},{4,5},{5,4},{6,7},{7,6},{8,9},{9,8},{10,11... | collective-permute-start | bytes 1376264 | tf_op jit(solution)/shard_map/ppermute | solution.py:281
  127.3 1.5 collective-permute-start.23
  127.4 30.2 %copy-start.3 = (f32[896,128]{1,0:T(8,128)S(1)}, f32[896,128]{1,0:T(8,128)}, u32[]{:S(2)}) copy-start(f32[896,128]{1,0:T(8,128)} %copy-done.2) | copy-start | bytes 1376260
  127.4 30.2 %copy-start.5 = (f32[896,128]{1,0:T(8,128)S(1)}, f32[896,128]{1,0:T(8,128)}, u32[]{:S(2)}) copy-start(f32[896,128]{1,0:T(8,128)} %copy-done.4) | copy-start | bytes 1376260
  127.4 30.2 %copy-start.7 = (f32[896,128]{1,0:T(8,128)S(1)}, f32[896,128]{1,0:T(8,128)}, u32[]{:S(2)}) copy-start(f32[896,128]{1,0:T(8,128)} %copy-done.6) | copy-start | bytes 1376260
  127.4 30.2 %copy-start.9 = (f32[896,128]{1,0:T(8,128)S(1)}, f32[896,128]{1,0:T(8,128)}, u32[]{:S(2)}) copy-start(f32[896,128]{1,0:T(8,128)} %copy-done.8) | copy-start | bytes 1376260
  127.4 30.2 %copy-start.11 = (f32[896,128]{1,0:T(8,128)S(1)}, f32[896,128]{1,0:T(8,128)}, u32[]{:S(2)}) copy-start(f32[896,128]{1,0:T(8,128)} %copy-done.10) | copy-start | bytes 1376260
  127.4 9.5 %collective-permute-start.26 = (f32[896,128]{1,0:T(8,128)}, f32[896,128]{1,0:T(8,128)S(1)}, u32[]{:S(2)}, u32[]{:S(2)}) collective-permute-start(f32[896,128]{1,0:T(8,128)} %get-tuple-element.36.refs_0_), channel_id=1, source_target_pairs={{0,2},{1,3},{2,0},{3,1},{4,6},{5,7},{6,4},{7,5},{8,10},{9,11},{10,... | collective-permute-start | bytes 1376264 | tf_op jit(solution)/shard_map/ppermute | solution.py:281
  127.9 10.8 %collective-permute-start.27 = (f32[896,128]{1,0:T(8,128)}, f32[896,128]{1,0:T(8,128)S(1)}, u32[]{:S(2)}, u32[]{:S(2)}) collective-permute-start(f32[896,128]{1,0:T(8,128)} %get-tuple-element.37.refs_2_), channel_id=1, source_target_pairs={{0,2},{1,3},{2,0},{3,1},{4,6},{5,7},{6,4},{7,5},{8,10},{9,11},{10,... | collective-permute-start | bytes 1376264 | tf_op jit(solution)/shard_map/ppermute | solution.py:281
  129.8 24.0 %collective-permute-start.30 = (f32[896,128]{1,0:T(8,128)}, f32[896,128]{1,0:T(8,128)S(1)}, u32[]{:S(2)}, u32[]{:S(2)}) collective-permute-start(f32[896,128]{1,0:T(8,128)} %get-tuple-element.36.refs_0_), channel_id=1, source_target_pairs={{0,4},{1,5},{2,6},{3,7},{4,0},{5,1},{6,2},{7,3},{8,12},{9,13},{10,... | collective-permute-start | bytes 1376264 | tf_op jit(solution)/shard_map/ppermute | solution.py:281
  130.3 23.5 %collective-permute-start.32 = (f32[896,128]{1,0:T(8,128)}, f32[896,128]{1,0:T(8,128)S(1)}, u32[]{:S(2)}, u32[]{:S(2)}) collective-permute-start(f32[896,128]{1,0:T(8,128)} %get-tuple-element.37.refs_2_), channel_id=1, source_target_pairs={{0,4},{1,5},{2,6},{3,7},{4,0},{5,1},{6,2},{7,3},{8,12},{9,13},{10,... | collective-permute-start | bytes 1376264 | tf_op jit(solution)/shard_map/ppermute | solution.py:281
  131.8 22.5 %collective-permute-start.28 = (f32[896,128]{1,0:T(8,128)}, f32[896,128]{1,0:T(8,128)S(1)}, u32[]{:S(2)}, u32[]{:S(2)}) collective-permute-start(f32[896,128]{1,0:T(8,128)} %get-tuple-element.36.refs_0_), channel_id=1, source_target_pairs={{0,8},{1,9},{2,10},{3,11},{4,12},{5,13},{6,14},{7,15},{8,0},{9,1},... | collective-permute-start | bytes 1376264 | tf_op jit(solution)/shard_map/ppermute | solution.py:281
  136.9 17.5 %collective-permute-start.35 = (f32[896,128]{1,0:T(8,128)}, f32[896,128]{1,0:T(8,128)S(1)}, u32[]{:S(2)}, u32[]{:S(2)}) collective-permute-start(f32[896,128]{1,0:T(8,128)} %get-tuple-element.37.refs_2_), channel_id=1, source_target_pairs={{0,8},{1,9},{2,10},{3,11},{4,12},{5,13},{6,14},{7,15},{8,0},{9,1},... | collective-permute-start | bytes 1376264 | tf_op jit(solution)/shard_map/ppermute | solution.py:281
  153.7 1.9 collective-permute-start.31
  153.8 2.4 %collective-permute-start.33 = (f32[896,128]{1,0:T(8,128)S(1)}, f32[896,128]{1,0:T(8,128)S(1)}, u32[]{:S(2)}, u32[]{:S(2)}) collective-permute-start(f32[896,128]{1,0:T(8,128)S(1)} %collective-permute-done.32.refs_2_), channel_id=1, source_target_pairs={{0,2},{1,3},{2,0},{3,1},{4,6},{5,7},{6,4},{7,5},{8,10},{9,11},{10,... | collective-permute-start | bytes 1376264 | tf_op jit(solution)/shard_map/ppermute | solution.py:281
  154.3 2.6 %collective-permute-start.34 = (f32[896,128]{1,0:T(8,128)S(1)}, f32[896,128]{1,0:T(8,128)S(1)}, u32[]{:S(2)}, u32[]{:S(2)}) collective-permute-start(f32[896,128]{1,0:T(8,128)S(1)} %collective-permute-done.28.refs_8_), channel_id=1, source_target_pairs={{0,2},{1,3},{2,0},{3,1},{4,6},{5,7},{6,4},{7,5},{8,10},{9,11},{10,... | collective-permute-start | bytes 1376264 | tf_op jit(solution)/shard_map/ppermute | solution.py:281
  154.4 3.2 %collective-permute-start.36 = (f32[896,128]{1,0:T(8,128)S(1)}, f32[896,128]{1,0:T(8,128)S(1)}, u32[]{:S(2)}, u32[]{:S(2)}) collective-permute-start(f32[896,128]{1,0:T(8,128)S(1)} %collective-permute-done.35.refs_10_), channel_id=1, source_target_pairs={{0,2},{1,3},{2,0},{3,1},{4,6},{5,7},{6,4},{7,5},{8,10},{9,11},{10,... | collective-permute-start | bytes 1376264 | tf_op jit(solution)/shard_map/ppermute | solution.py:281
  154.9 21.0 %collective-permute-start.38 = (f32[896,128]{1,0:T(8,128)S(1)}, f32[896,128]{1,0:T(8,128)S(1)}, u32[]{:S(2)}, u32[]{:S(2)}) collective-permute-start(f32[896,128]{1,0:T(8,128)S(1)} %broadcast_select_fusion.1), channel_id=1, source_target_pairs={{0,8},{1,9},{2,10},{3,11},{4,12},{5,13},{6,14},{7,15},{8,0},{9,1},... | collective-permute-start | bytes 1376264 | tf_op jit(solution)/shard_map/ppermute | solution.py:281
  155.6 20.5 %collective-permute-start.29 = (f32[896,128]{1,0:T(8,128)S(1)}, f32[896,128]{1,0:T(8,128)S(1)}, u32[]{:S(2)}, u32[]{:S(2)}) collective-permute-start(f32[896,128]{1,0:T(8,128)S(1)} %broadcast_select_fusion.3), channel_id=1, source_target_pairs={{0,4},{1,5},{2,6},{3,7},{4,0},{5,1},{6,2},{7,3},{8,12},{9,13},{10,... | collective-permute-start | bytes 1376264 | tf_op jit(solution)/shard_map/ppermute | solution.py:281
  175.9 1.9 collective-permute-start.39
  176.2 2.3 %collective-permute-start.37 = (f32[896,128]{1,0:T(8,128)S(1)}, f32[896,128]{1,0:T(8,128)S(1)}, u32[]{:S(2)}, u32[]{:S(2)}) collective-permute-start(f32[896,128]{1,0:T(8,128)S(1)} %broadcast_select_fusion.2), channel_id=1, source_target_pairs={{0,2},{1,3},{2,0},{3,1},{4,6},{5,7},{6,4},{7,5},{8,10},{9,11},{10,... | collective-permute-start | bytes 1376264 | tf_op jit(solution)/shard_map/ppermute | solution.py:281
  (17 other events, 153.5 us)

commit v5 on v4

--- a/solution.py
+++ b/solution.py
@@ -29,9 +29,7 @@
 
 
 def small(former, latter, dims=PLAIN):
-    return lax.dot_general(
-        former, latter, dims, precision=lax.Precision.HIGHEST, preferred_element_type=F32
-    )
+    return product(split(former), split(latter), dims)
 
 
 def in_order(place, joined, blocks):

time: 190 us -> 190 us (level)
  transfers between devices with their start and end apart: 40 -> 40, of which waited for: 19 -> 19; matrix products, arithmetic and copies ran while one was open for 3% -> 3% of each run, Pallas kernels for 26% -> 25%
where the time goes in v5:
time: 190 us; the launch traced here: 189 us
  Pallas kernels  66.2 us (35%)
  waiting for transfers between devices  59 us (31%)
  starting transfers between devices  45.7 us (24%)
  local copies, waits for them, and re-layouts  11 us (6%)
  other arithmetic  3.74 us (2%)
  between operations  2.98 us (2%)
    ppermute x36, waiting for transfers between devices, flip(): lax.ppermute(values, ('row', 'col'), [(n, n ^ mask) for n in range(everyo...  48.5 us
    pallas_call x3, Pallas kernels, update_step(): pl.pallas_call(functools.partial(update_kernel, count), grid_spec=pltpu.P...  38.6 us
    ppermute x36, starting transfers between devices, flip(): lax.ppermute(values, ('row', 'col'), [(n, n ^ mask) for n in range(everyo...  31.9 us
    pallas_call x3, Pallas kernels, forward_step(): pl.pallas_call(functools.partial(forward_kernel, first, last, count, shar...  23.3 us
    ppermute x4, starting transfers between devices, transpose(): return lax.ppermute(values, ('row', 'col'), pairs)  13.7 us
    ppermute x4, waiting for transfers between devices, transpose(): return lax.ppermute(values, ('row', 'col'), pairs)  10.4 us
    unnamed x50, local copies, waits for them, and re-layouts  7.58 us
    pallas_call x1, Pallas kernels, mix(): pl.pallas_call(mix_kernel, in_specs=[pl.BlockSpec(memory_space=pltpu.SMEM...  4.32 us
  transfers between devices with their start and end apart: 40, of which 19 were waited for; matrix products, arithmetic and copies ran while one was open for 3% of the time, Pallas kernels for 25%

profile of v5, /device:TPU:0, one launch (start us, length us, event | category | flops | bytes accessed | tf_op | source)
XLA Modules:
  0.0 188.6 jit_solution(16178344852788274146)
XLA Ops:
  0.0 1.2 slice_bitcast_fusion
  1.2 0.7 collective-permute-start
  1.9 6.6 %collective-permute-start.2 = (f32[896,128]{1,0:T(8,128)S(1)}, f32[896,128]{1,0:T(8,128)S(1)}, u32[]{:S(2)}, u32[]{:S(2)}) collective-permute-start(f32[896,128]{1,0:T(8,128)S(1)} %get-tuple-element.43), channel_id=1, source_target_pairs={{0,16},{1,0},{2,18},{3,2},{4,20},{5,4},{6,22},{7,6},{8,24},{9,8},{... | collective-permute-start | bytes 1376264 | tf_op jit(solution)/shard_map/ppermute | solution.py:291
  8.5 10.4 %collective-permute-done.2.refs_2_.refs_6_ = f32[896,128]{1,0:T(8,128)S(1)} collective-permute-done((f32[896,128]{1,0:T(8,128)S(1)}, f32[896,128]{1,0:T(8,128)S(1)}, u32[]{:S(2)}, u32[]{:S(2)}) %collective-permute-start.2) | collective-permute-done | bytes 458784 | tf_op jit(solution)/shard_map/ppermute | solution.py:291
  18.9 10.4 %collective-permute-start.4 = (f32[896,128]{1,0:T(8,128)S(1)}, f32[896,128]{1,0:T(8,128)S(1)}, u32[]{:S(2)}, u32[]{:S(2)}) collective-permute-start(f32[896,128]{1,0:T(8,128)S(1)} %collective-permute-done.refs_0_.refs_4_), channel_id=1, source_target_pairs={{0,8},{1,9},{2,10},{3,11},{4,12},{5,13},{6,14},{7,15},{8,0},{9,1},... | collective-permute-start | bytes 1376264 | tf_op jit(solution)/shard_map/ppermute | solution.py:279
  29.3 1.5 collective-permute-start.8
  31.5 1.2 copy-done
  32.7 6.1 %shard_map.37 = (f32[896,256]{1,0:T(8,128)S(1)}, s32[8,128]{1,0:T(8,128)S(1)}, bf16[2,256,448]{2,1,0:T(8,128)(2,1)S(1)}, bf16[2,256,448]{2,1,0:T(8,128)(2,1)S(1)}, f32[128,128]{1,0:T(8,128)S(1)}) custom-call(s32[3]{0:T(128)S(1)} %pad_add_fusion.place, f32[896,7168]{1,0:T(8,128)} %block.11, f32[896,128]{1,0:T(8,128)S(1)} %collective-permute-done.refs_0_.refs_4_, ...), custom_call_target="tpu_custom_call" | custom-call | flops 2466250752 | bytes 6422528 | tf_op jit(solution)/shard_map/pallas_call | solution.py:138
  40.0 0.7 collective-permute-done.4.refs_4_.refs_12_
  40.7 2.0 %collective-permute-done.8.refs_2_.refs_6_ = f32[896,128]{1,0:T(8,128)S(1)} collective-permute-done((f32[896,128]{1,0:T(8,128)S(1)}, f32[896,128]{1,0:T(8,128)S(1)}, u32[]{:S(2)}, u32[]{:S(2)}) %collective-permute-start.8) | collective-permute-done | bytes 458784 | tf_op jit(solution)/shard_map/ppermute | solution.py:279
  42.7 7.6 %collective-permute-done.11.refs_6_.refs_14_ = f32[896,128]{1,0:T(8,128)S(1)} collective-permute-done((f32[896,128]{1,0:T(8,128)S(1)}, f32[896,128]{1,0:T(8,128)S(1)}, u32[]{:S(2)}, u32[]{:S(2)}) %collective-permute-start.11) | collective-permute-done | bytes 458784 | tf_op jit(solution)/shard_map/ppermute | solution.py:279
  50.3 1.5 collective-permute-done.6.refs_0_.refs_4_
  51.8 0.8 collective-permute-start.14
  52.7 1.6 collective-permute-start.5
  54.4 9.7 %shard_map.38 = (f32[896,256]{1,0:T(8,128)S(1)}, s32[8,128]{1,0:T(8,128)S(1)}) custom-call(s32[3]{0:T(128)S(1)} %pad_add_fusion.place, f32[896,7168]{1,0:T(8,128)} %block.11, f32[896,128]{1,0:T(8,128)S(1)} %collective-permute-done.6.refs_0_.refs_4_, f32[896,128]{1,0:T(8,128)S(1)} %collective-permute-done.7.refs_1_.refs_5_, ...), custom_call_target="tpu_custom_call" | custom-call | flops 4932501504 | bytes 12845056 | tf_op jit(solution)/shard_map/pallas_call | solution.py:138
  65.4 0.8 broadcast_select_fusion.4
  66.2 0.8 broadcast_select_fusion.6
  67.6 0.8 collective-permute-done.15.refs_3_.refs_7_
  68.4 1.0 collective-permute-done.13.refs_1_.refs_5_
  69.4 1.2 copy-done.19
  70.6 1.0 copy-done.21
  71.7 1.0 copy-done.23
  72.7 7.6 %shard_map.39 = (f32[896,128]{1,0:T(8,128)S(1)}, f32[896,128]{1,0:T(8,128)S(1)}, f32[4,128,128]{2,1,0:T(8,128)S(1)}) custom-call(s32[3]{0:T(128)S(1)} %pad_add_fusion.place, f32[896,7168]{1,0:T(8,128)} %block.11, f32[896,128]{1,0:T(8,128)S(1)} %collective-permute-done.5.refs_0_.refs_4_, f32[896,128]{1,0:T(8,128)} %collective-permute-done.13.refs_1_.refs_5_, ...), custom_call_target="tpu_custom_call" | custom-call | flops 2466250752 | bytes 6422528 | tf_op jit(solution)/shard_map/pallas_call | solution.py:138
  80.3 3.4 %collective-permute-start.16 = (f32[896,128]{1,0:T(8,128)S(1)}, f32[896,128]{1,0:T(8,128)S(1)}, u32[]{:S(2)}, u32[]{:S(2)}) collective-permute-start(f32[896,128]{1,0:T(8,128)S(1)} %get-tuple-element.32), channel_id=1, source_target_pairs={{0,1},{1,0},{2,3},{3,2},{4,5},{5,4},{6,7},{7,6},{8,9},{9,8},{10,11... | collective-permute-start | bytes 1376264 | tf_op jit(solution)/shard_map/ppermute | solution.py:279
  83.9 1.3 collective-permute-done.18
  85.3 9.8 %collective-permute-done.16 = f32[896,128]{1,0:T(8,128)S(1)} collective-permute-done((f32[896,128]{1,0:T(8,128)S(1)}, f32[896,128]{1,0:T(8,128)S(1)}, u32[]{:S(2)}, u32[]{:S(2)}) %collective-permute-start.16) | collective-permute-done | bytes 458784 | tf_op jit(solution)/shard_map/ppermute | solution.py:279
  95.1 0.8 add.27.mine
  95.9 5.1 %collective-permute-start.24 = (f32[896,128]{1,0:T(8,128)}, f32[896,128]{1,0:T(8,128)}, u32[]{:S(2)}, u32[]{:S(2)}) collective-permute-start(f32[896,128]{1,0:T(8,128)} %add.27.mine), channel_id=1, source_target_pairs={{0,0},{1,16},{2,2},{3,18},{4,4},{5,20},{6,6},{7,22},{8,8},{9,24},{... | collective-permute-start | bytes 1376264 | tf_op jit(solution)/shard_map/ppermute | solution.py:291
  100.9 1.4 collective-permute-start.25
  103.0 4.4 %collective-permute-done.20 = f32[2,128,128]{2,1,0:T(8,128)S(1)} collective-permute-done((f32[2,128,128]{2,1,0:T(8,128)S(1)}, f32[2,128,128]{2,1,0:T(8,128)S(1)}, u32[]{:S(2)}, u32[]{:S(2)}) %collective-permute-start.20) | collective-permute-done | bytes 131104 | tf_op jit(solution)/shard_map/ppermute | solution.py:279
  107.4 0.8 collective-permute-start.21
  108.3 6.1 %collective-permute-done.21 = f32[2,128,128]{2,1,0:T(8,128)S(1)} collective-permute-done((f32[2,128,128]{2,1,0:T(8,128)S(1)}, f32[2,128,128]{2,1,0:T(8,128)S(1)}, u32[]{:S(2)}, u32[]{:S(2)}) %collective-permute-start.21) | collective-permute-done | bytes 131104 | tf_op jit(solution)/shard_map/ppermute | solution.py:279
  114.4 1.1 collective-permute-start.22
  115.4 2.7 %collective-permute-start.17 = (f32[896,128]{1,0:T(8,128)}, f32[896,128]{1,0:T(8,128)}, u32[]{:S(2)}, u32[]{:S(2)}) collective-permute-start(f32[896,128]{1,0:T(8,128)} %add.27.mine), channel_id=1, source_target_pairs={{0,1},{1,0},{2,3},{3,2},{4,5},{5,4},{6,7},{7,6},{8,9},{9,8},{10,11... | collective-permute-start | bytes 1376264 | tf_op jit(solution)/shard_map/ppermute | solution.py:279
  118.2 9.0 %collective-permute-done.22 = f32[2,128,128]{2,1,0:T(8,128)S(1)} collective-permute-done((f32[2,128,128]{2,1,0:T(8,128)S(1)}, f32[2,128,128]{2,1,0:T(8,128)S(1)}, u32[]{:S(2)}, u32[]{:S(2)}) %collective-permute-start.22) | collective-permute-done | bytes 131104 | tf_op jit(solution)/shard_map/ppermute | solution.py:279
  128.0 0.8 collective-permute-done.23
  128.8 0.9 broadcast_select_fusion.9
  130.3 1.6 collective-permute-start.32
  132.1 4.3 %shard_map.40 = (bf16[896,512]{1,0:T(8,128)(2,1)S(1)}, bf16[896,512]{1,0:T(8,128)(2,1)S(1)}) custom-call(s32[3]{0:T(128)S(1)} %pad_add_fusion.place, f32[2,896,128]{2,1,0:T(8,128)S(1)} %copy-done.1, f32[896,128]{1,0:T(8,128)} %add.27.mine, f32[896,128]{1,0:T(8,128)} %collective-permute-done.17.other, f32[4,128,128]{2,1,0:T(8,128)S(1)} %pad_maximum_fusion.inner, ...), custom_call_target="tpu_custom_call" | custom-call | flops 1409286144 | bytes 3670016 | tf_op jit(solution)/shard_map/pallas_call | solution.py:195
  136.4 1.8 collective-permute-start.35
  138.3 1.0 copy-done.13
  139.3 1.0 copy-done.15
  140.3 1.0 copy-done.17
  141.3 10.8 %shard_map.42 = (f32[896,7168]{1,0:T(8,128)}, s32[8,128]{1,0:T(8,128)S(1)}) custom-call(s32[3]{0:T(128)S(1)} %pad_add_fusion.place, f32[896,7168]{1,0:T(8,128)} %block.11, bf16[896,512]{1,0:T(8,128)(2,1)S(1)} %get-tuple-element.34.high, bf16[896,512]{1,0:T(8,128)(2,1)S(1)} %get-tuple-element.35.low, f32[896,128]{1,0:T(8,128)} %get-tuple-element.36.refs_0_, ...), custom_call_target="tpu_custom_call" | custom-call | flops 4932501504 | bytes 12845056 | tf_op jit(solution)/shard_map/pallas_call | solution.py:232
  157.1 17.1 %shard_map.43 = (f32[896,7168]{1,0:T(8,128)}, s32[8,128]{1,0:T(8,128)S(1)}) custom-call(s32[3]{0:T(128)S(1)} %pad_add_fusion.place, f32[896,7168]{1,0:T(8,128)} %block.11, bf16[896,512]{1,0:T(8,128)(2,1)S(1)} %get-tuple-element.34.high, bf16[896,512]{1,0:T(8,128)(2,1)S(1)} %get-tuple-element.35.low, ...), custom_call_target="tpu_custom_call", output_to_operand_aliasing={{0}: (20, {})} | custom-call | flops 9865003008 | bytes 25690112 | tf_op jit(solution)/shard_map/pallas_call | solution.py:232
  176.1 1.2 collective-permute-done.39.refs_3_
  177.3 0.7 collective-permute-done.37.refs_1_
  178.0 10.7 %shard_map.44 = (f32[896,7168]{1,0:T(8,128)}, s32[8,128]{1,0:T(8,128)}) custom-call(s32[3]{0:T(128)S(1)} %pad_add_fusion.place, f32[896,7168]{1,0:T(8,128)} %block.11, bf16[896,512]{1,0:T(8,128)(2,1)S(1)} %get-tuple-element.34.high, bf16[896,512]{1,0:T(8,128)(2,1)S(1)} %get-tuple-element.35.low, ...), custom_call_target="tpu_custom_call", output_to_operand_aliasing={{0}: (12, {})} | custom-call | flops 4932501504 | bytes 12845056 | tf_op jit(solution)/shard_map/pallas_call | solution.py:232
  (113 shorter events, 10.7 us)
Async XLA Ops:
  1.2 7.3 %collective-permute-start = (f32[896,128]{1,0:T(8,128)S(1)}, f32[896,128]{1,0:T(8,128)S(1)}, u32[]{:S(2)}, u32[]{:S(2)}) collective-permute-start(f32[896,128]{1,0:T(8,128)S(1)} %get-tuple-element.44), channel_id=1, source_target_pairs={{0,0},{1,16},{2,2},{3,18},{4,4},{5,20},{6,6},{7,22},{8,8},{9,24},{... | collective-permute-start | bytes 1376264 | tf_op jit(solution)/shard_map/ppermute | solution.py:291
  1.9 17.0 %collective-permute-start.2 = (f32[896,128]{1,0:T(8,128)S(1)}, f32[896,128]{1,0:T(8,128)S(1)}, u32[]{:S(2)}, u32[]{:S(2)}) collective-permute-start(f32[896,128]{1,0:T(8,128)S(1)} %get-tuple-element.43), channel_id=1, source_target_pairs={{0,16},{1,0},{2,18},{3,2},{4,20},{5,4},{6,22},{7,6},{8,24},{9,8},{... | collective-permute-start | bytes 1376264 | tf_op jit(solution)/shard_map/ppermute | solution.py:291
  8.5 43.3 %copy-start.12 = (f32[896,128]{1,0:T(8,128)}, f32[896,128]{1,0:T(8,128)S(1)}, u32[]{:S(2)}) copy-start(f32[896,128]{1,0:T(8,128)S(1)} %collective-permute-done.refs_0_.refs_4_) | copy-start | bytes 1376260
  8.5 22.4 %collective-permute-start.1 = (f32[896,128]{1,0:T(8,128)S(1)}, f32[896,128]{1,0:T(8,128)S(1)}, u32[]{:S(2)}, u32[]{:S(2)}) collective-permute-start(f32[896,128]{1,0:T(8,128)S(1)} %collective-permute-done.refs_0_.refs_4_), channel_id=1, source_target_pairs={{0,2},{1,3},{2,0},{3,1},{4,6},{5,7},{6,4},{7,5},{8,10},{9,11},{10,... | collective-permute-start | bytes 1376264 | tf_op jit(solution)/shard_map/ppermute | solution.py:279
  18.9 33.8 %copy-start.14 = (f32[896,128]{1,0:T(8,128)}, f32[896,128]{1,0:T(8,128)S(1)}, u32[]{:S(2)}) copy-start(f32[896,128]{1,0:T(8,128)S(1)} %collective-permute-done.2.refs_2_.refs_6_) | copy-start | bytes 1376260
  18.9 12.6 %collective-permute-start.3 = (f32[896,128]{1,0:T(8,128)S(1)}, f32[896,128]{1,0:T(8,128)}, u32[]{:S(2)}, u32[]{:S(2)}) collective-permute-start(f32[896,128]{1,0:T(8,128)S(1)} %collective-permute-done.2.refs_2_.refs_6_), channel_id=1, source_target_pairs={{0,2},{1,3},{2,0},{3,1},{4,6},{5,7},{6,4},{7,5},{8,10},{9,11},{10,... | collective-permute-start | bytes 1376264 | tf_op jit(solution)/shard_map/ppermute | solution.py:279
  18.9 21.7 %collective-permute-start.4 = (f32[896,128]{1,0:T(8,128)S(1)}, f32[896,128]{1,0:T(8,128)S(1)}, u32[]{:S(2)}, u32[]{:S(2)}) collective-permute-start(f32[896,128]{1,0:T(8,128)S(1)} %collective-permute-done.refs_0_.refs_4_), channel_id=1, source_target_pairs={{0,8},{1,9},{2,10},{3,11},{4,12},{5,13},{6,14},{7,15},{8,0},{9,1},... | collective-permute-start | bytes 1376264 | tf_op jit(solution)/shard_map/ppermute | solution.py:279
  29.3 13.4 %collective-permute-start.8 = (f32[896,128]{1,0:T(8,128)S(1)}, f32[896,128]{1,0:T(8,128)S(1)}, u32[]{:S(2)}, u32[]{:S(2)}) collective-permute-start(f32[896,128]{1,0:T(8,128)S(1)} %collective-permute-done.2.refs_2_.refs_6_), channel_id=1, source_target_pairs={{0,4},{1,5},{2,6},{3,7},{4,0},{5,1},{6,2},{7,3},{8,12},{9,13},{10,... | collective-permute-start | bytes 1376264 | tf_op jit(solution)/shard_map/ppermute | solution.py:279
  30.8 19.5 %collective-permute-start.11 = (f32[896,128]{1,0:T(8,128)S(1)}, f32[896,128]{1,0:T(8,128)S(1)}, u32[]{:S(2)}, u32[]{:S(2)}) collective-permute-start(f32[896,128]{1,0:T(8,128)S(1)} %collective-permute-done.2.refs_2_.refs_6_), channel_id=1, source_target_pairs={{0,8},{1,9},{2,10},{3,11},{4,12},{5,13},{6,14},{7,15},{8,0},{9,1},... | collective-permute-start | bytes 1376264 | tf_op jit(solution)/shard_map/ppermute | solution.py:279
  30.9 20.9 %collective-permute-start.6 = (f32[896,128]{1,0:T(8,128)S(1)}, f32[896,128]{1,0:T(8,128)S(1)}, u32[]{:S(2)}, u32[]{:S(2)}) collective-permute-start(f32[896,128]{1,0:T(8,128)S(1)} %collective-permute-done.refs_0_.refs_4_), channel_id=1, source_target_pairs={{0,4},{1,5},{2,6},{3,7},{4,0},{5,1},{6,2},{7,3},{8,12},{9,13},{10,... | collective-permute-start | bytes 1376264 | tf_op jit(solution)/shard_map/ppermute | solution.py:279
  40.7 12.0 %collective-permute-start.10 = (f32[896,128]{1,0:T(8,128)S(1)}, f32[896,128]{1,0:T(8,128)S(1)}, u32[]{:S(2)}, u32[]{:S(2)}) collective-permute-start(f32[896,128]{1,0:T(8,128)S(1)} %collective-permute-done.4.refs_4_.refs_12_), channel_id=1, source_target_pairs={{0,2},{1,3},{2,0},{3,1},{4,6},{5,7},{6,4},{7,5},{8,10},{9,11},{10,... | collective-permute-start | bytes 1376264 | tf_op jit(solution)/shard_map/ppermute | solution.py:279
  42.7 11.7 %collective-permute-start.9 = (f32[896,128]{1,0:T(8,128)S(1)}, f32[896,128]{1,0:T(8,128)S(1)}, u32[]{:S(2)}, u32[]{:S(2)}) collective-permute-start(f32[896,128]{1,0:T(8,128)S(1)} %collective-permute-done.8.refs_2_.refs_6_), channel_id=1, source_target_pairs={{0,2},{1,3},{2,0},{3,1},{4,6},{5,7},{6,4},{7,5},{8,10},{9,11},{10,... | collective-permute-start | bytes 1376264 | tf_op jit(solution)/shard_map/ppermute | solution.py:279
  50.3 4.0 %collective-permute-start.12 = (f32[896,128]{1,0:T(8,128)S(1)}, f32[896,128]{1,0:T(8,128)S(1)}, u32[]{:S(2)}, u32[]{:S(2)}) collective-permute-start(f32[896,128]{1,0:T(8,128)S(1)} %collective-permute-done.11.refs_6_.refs_14_), channel_id=1, source_target_pairs={{0,2},{1,3},{2,0},{3,1},{4,6},{5,7},{6,4},{7,5},{8,10},{9,11},{10,... | collective-permute-start | bytes 1376264 | tf_op jit(solution)/shard_map/ppermute | solution.py:279
  51.8 28.5 %copy-start.2 = (f32[896,128]{1,0:T(8,128)}, f32[896,128]{1,0:T(8,128)S(1)}, u32[]{:S(2)}) copy-start(f32[896,128]{1,0:T(8,128)S(1)} %collective-permute-done.6.refs_0_.refs_4_) | copy-start | bytes 1376260
  51.8 2.6 %collective-permute-start.7 = (f32[896,128]{1,0:T(8,128)S(1)}, f32[896,128]{1,0:T(8,128)S(1)}, u32[]{:S(2)}, u32[]{:S(2)}) collective-permute-start(f32[896,128]{1,0:T(8,128)S(1)} %collective-permute-done.6.refs_0_.refs_4_), channel_id=1, source_target_pairs={{0,2},{1,3},{2,0},{3,1},{4,6},{5,7},{6,4},{7,5},{8,10},{9,11},{10,... | collective-permute-start | bytes 1376264 | tf_op jit(solution)/shard_map/ppermute | solution.py:279
  51.8 13.6 %collective-permute-start.14 = (f32[896,128]{1,0:T(8,128)S(1)}, f32[896,128]{1,0:T(8,128)S(1)}, u32[]{:S(2)}, u32[]{:S(2)}) collective-permute-start(f32[896,128]{1,0:T(8,128)S(1)} %broadcast_select_fusion.5), channel_id=1, source_target_pairs={{0,8},{1,9},{2,10},{3,11},{4,12},{5,13},{6,14},{7,15},{8,0},{9,1},... | collective-permute-start | bytes 1376264 | tf_op jit(solution)/shard_map/ppermute | solution.py:279
  52.7 13.5 %collective-permute-start.5 = (f32[896,128]{1,0:T(8,128)S(1)}, f32[896,128]{1,0:T(8,128)S(1)}, u32[]{:S(2)}, u32[]{:S(2)}) collective-permute-start(f32[896,128]{1,0:T(8,128)S(1)} %broadcast_select_fusion.7), channel_id=1, source_target_pairs={{0,4},{1,5},{2,6},{3,7},{4,0},{5,1},{6,2},{7,3},{8,12},{9,13},{10,... | collective-permute-start | bytes 1376264 | tf_op jit(solution)/shard_map/ppermute | solution.py:279
  66.2 2.2 %collective-permute-start.15 = (f32[896,128]{1,0:T(8,128)}, f32[896,128]{1,0:T(8,128)}, u32[]{:S(2)}, u32[]{:S(2)}) collective-permute-start(f32[896,128]{1,0:T(8,128)} %broadcast_select_fusion.4), channel_id=1, source_target_pairs={{0,2},{1,3},{2,0},{3,1},{4,6},{5,7},{6,4},{7,5},{8,10},{9,11},{10,... | collective-permute-start | bytes 1376264 | tf_op jit(solution)/shard_map/ppermute | solution.py:279
  67.1 2.4 %collective-permute-start.13 = (f32[896,128]{1,0:T(8,128)}, f32[896,128]{1,0:T(8,128)}, u32[]{:S(2)}, u32[]{:S(2)}) collective-permute-start(f32[896,128]{1,0:T(8,128)} %broadcast_select_fusion.6), channel_id=1, source_target_pairs={{0,2},{1,3},{2,0},{3,1},{4,6},{5,7},{6,4},{7,5},{8,10},{9,11},{10,... | collective-permute-start | bytes 1376264 | tf_op jit(solution)/shard_map/ppermute | solution.py:279
  80.3 14.8 %collective-permute-start.16 = (f32[896,128]{1,0:T(8,128)S(1)}, f32[896,128]{1,0:T(8,128)S(1)}, u32[]{:S(2)}, u32[]{:S(2)}) collective-permute-start(f32[896,128]{1,0:T(8,128)S(1)} %get-tuple-element.32), channel_id=1, source_target_pairs={{0,1},{1,0},{2,3},{3,2},{4,5},{5,4},{6,7},{7,6},{8,9},{9,8},{10,11... | collective-permute-start | bytes 1376264 | tf_op jit(solution)/shard_map/ppermute | solution.py:279
  83.7 1.4 collective-permute-start.18
  85.2 17.2 %collective-permute-start.19 = (f32[2,128,128]{2,1,0:T(8,128)S(1)}, f32[2,128,128]{2,1,0:T(8,128)S(1)}, u32[]{:S(2)}, u32[]{:S(2)}) collective-permute-start(f32[2,128,128]{2,1,0:T(8,128)S(1)} %select_add_fusion), channel_id=1, source_target_pairs={{0,1},{1,0},{2,3},{3,2},{4,5},{5,4},{6,7},{7,6},{8,9},{9,8},{10,11... | collective-permute-start | bytes 393224 | tf_op jit(solution)/shard_map/ppermute | solution.py:279
  95.9 31.4 %collective-permute-start.24 = (f32[896,128]{1,0:T(8,128)}, f32[896,128]{1,0:T(8,128)}, u32[]{:S(2)}, u32[]{:S(2)}) collective-permute-start(f32[896,128]{1,0:T(8,128)} %add.27.mine), channel_id=1, source_target_pairs={{0,0},{1,16},{2,2},{3,18},{4,4},{5,20},{6,6},{7,22},{8,8},{9,24},{... | collective-permute-start | bytes 1376264 | tf_op jit(solution)/shard_map/ppermute | solution.py:291
  100.9 26.4 %collective-permute-start.25 = (f32[896,128]{1,0:T(8,128)}, f32[896,128]{1,0:T(8,128)}, u32[]{:S(2)}, u32[]{:S(2)}) collective-permute-start(f32[896,128]{1,0:T(8,128)} %add.27.mine), channel_id=1, source_target_pairs={{0,16},{1,0},{2,18},{3,2},{4,20},{5,4},{6,22},{7,6},{8,24},{9,8},{... | collective-permute-start | bytes 1376264 | tf_op jit(solution)/shard_map/ppermute | solution.py:291
  102.4 5.0 %collective-permute-start.20 = (f32[2,128,128]{2,1,0:T(8,128)S(1)}, f32[2,128,128]{2,1,0:T(8,128)S(1)}, u32[]{:S(2)}, u32[]{:S(2)}) collective-permute-start(f32[2,128,128]{2,1,0:T(8,128)S(1)} %add.30), channel_id=1, source_target_pairs={{0,4},{1,5},{2,6},{3,7},{4,0},{5,1},{6,2},{7,3},{8,12},{9,13},{10,... | collective-permute-start | bytes 393224 | tf_op jit(solution)/shard_map/ppermute | solution.py:279
  107.4 6.9 %collective-permute-start.21 = (f32[2,128,128]{2,1,0:T(8,128)S(1)}, f32[2,128,128]{2,1,0:T(8,128)S(1)}, u32[]{:S(2)}, u32[]{:S(2)}) collective-permute-start(f32[2,128,128]{2,1,0:T(8,128)S(1)} %add.31), channel_id=1, source_target_pairs={{0,8},{1,9},{2,10},{3,11},{4,12},{5,13},{6,14},{7,15},{8,0},{9,1},... | collective-permute-start | bytes 393224 | tf_op jit(solution)/shard_map/ppermute | solution.py:279
  114.4 12.8 %collective-permute-start.22 = (f32[2,128,128]{2,1,0:T(8,128)S(1)}, f32[2,128,128]{2,1,0:T(8,128)S(1)}, u32[]{:S(2)}, u32[]{:S(2)}) collective-permute-start(f32[2,128,128]{2,1,0:T(8,128)S(1)} %add.32), channel_id=1, source_target_pairs={{0,16},{1,17},{2,18},{3,19},{4,20},{5,21},{6,22},{7,23},{8,24},{9,... | collective-permute-start | bytes 393224 | tf_op jit(solution)/shard_map/ppermute | solution.py:279
  115.4 16.4 %collective-permute-start.17 = (f32[896,128]{1,0:T(8,128)}, f32[896,128]{1,0:T(8,128)}, u32[]{:S(2)}, u32[]{:S(2)}) collective-permute-start(f32[896,128]{1,0:T(8,128)} %add.27.mine), channel_id=1, source_target_pairs={{0,1},{1,0},{2,3},{3,2},{4,5},{5,4},{6,7},{7,6},{8,9},{9,8},{10,11... | collective-permute-start | bytes 1376264 | tf_op jit(solution)/shard_map/ppermute | solution.py:279
  127.3 1.5 collective-permute-start.23
  127.4 29.7 %copy-start.3 = (f32[896,128]{1,0:T(8,128)S(1)}, f32[896,128]{1,0:T(8,128)}, u32[]{:S(2)}) copy-start(f32[896,128]{1,0:T(8,128)} %copy-done.2) | copy-start | bytes 1376260
  127.4 29.7 %copy-start.5 = (f32[896,128]{1,0:T(8,128)S(1)}, f32[896,128]{1,0:T(8,128)}, u32[]{:S(2)}) copy-start(f32[896,128]{1,0:T(8,128)} %copy-done.4) | copy-start | bytes 1376260
  127.4 29.7 %copy-start.7 = (f32[896,128]{1,0:T(8,128)S(1)}, f32[896,128]{1,0:T(8,128)}, u32[]{:S(2)}) copy-start(f32[896,128]{1,0:T(8,128)} %copy-done.6) | copy-start | bytes 1376260
  127.4 29.7 %copy-start.9 = (f32[896,128]{1,0:T(8,128)S(1)}, f32[896,128]{1,0:T(8,128)}, u32[]{:S(2)}) copy-start(f32[896,128]{1,0:T(8,128)} %copy-done.8) | copy-start | bytes 1376260
  127.4 29.7 %copy-start.11 = (f32[896,128]{1,0:T(8,128)S(1)}, f32[896,128]{1,0:T(8,128)}, u32[]{:S(2)}) copy-start(f32[896,128]{1,0:T(8,128)} %copy-done.10) | copy-start | bytes 1376260
  127.4 9.0 %collective-permute-start.26 = (f32[896,128]{1,0:T(8,128)}, f32[896,128]{1,0:T(8,128)S(1)}, u32[]{:S(2)}, u32[]{:S(2)}) collective-permute-start(f32[896,128]{1,0:T(8,128)} %get-tuple-element.36.refs_0_), channel_id=1, source_target_pairs={{0,2},{1,3},{2,0},{3,1},{4,6},{5,7},{6,4},{7,5},{8,10},{9,11},{10,... | collective-permute-start | bytes 1376264 | tf_op jit(solution)/shard_map/ppermute | solution.py:279
  127.9 10.3 %collective-permute-start.27 = (f32[896,128]{1,0:T(8,128)}, f32[896,128]{1,0:T(8,128)S(1)}, u32[]{:S(2)}, u32[]{:S(2)}) collective-permute-start(f32[896,128]{1,0:T(8,128)} %get-tuple-element.37.refs_2_), channel_id=1, source_target_pairs={{0,2},{1,3},{2,0},{3,1},{4,6},{5,7},{6,4},{7,5},{8,10},{9,11},{10,... | collective-permute-start | bytes 1376264 | tf_op jit(solution)/shard_map/ppermute | solution.py:279
  129.8 23.5 %collective-permute-start.30 = (f32[896,128]{1,0:T(8,128)}, f32[896,128]{1,0:T(8,128)S(1)}, u32[]{:S(2)}, u32[]{:S(2)}) collective-permute-start(f32[896,128]{1,0:T(8,128)} %get-tuple-element.36.refs_0_), channel_id=1, source_target_pairs={{0,4},{1,5},{2,6},{3,7},{4,0},{5,1},{6,2},{7,3},{8,12},{9,13},{10,... | collective-permute-start | bytes 1376264 | tf_op jit(solution)/shard_map/ppermute | solution.py:279
  130.3 23.0 %collective-permute-start.32 = (f32[896,128]{1,0:T(8,128)}, f32[896,128]{1,0:T(8,128)S(1)}, u32[]{:S(2)}, u32[]{:S(2)}) collective-permute-start(f32[896,128]{1,0:T(8,128)} %get-tuple-element.37.refs_2_), channel_id=1, source_target_pairs={{0,4},{1,5},{2,6},{3,7},{4,0},{5,1},{6,2},{7,3},{8,12},{9,13},{10,... | collective-permute-start | bytes 1376264 | tf_op jit(solution)/shard_map/ppermute | solution.py:279
  131.8 22.0 %collective-permute-start.28 = (f32[896,128]{1,0:T(8,128)}, f32[896,128]{1,0:T(8,128)S(1)}, u32[]{:S(2)}, u32[]{:S(2)}) collective-permute-start(f32[896,128]{1,0:T(8,128)} %get-tuple-element.36.refs_0_), channel_id=1, source_target_pairs={{0,8},{1,9},{2,10},{3,11},{4,12},{5,13},{6,14},{7,15},{8,0},{9,1},... | collective-permute-start | bytes 1376264 | tf_op jit(solution)/shard_map/ppermute | solution.py:279
  136.4 17.5 %collective-permute-start.35 = (f32[896,128]{1,0:T(8,128)}, f32[896,128]{1,0:T(8,128)S(1)}, u32[]{:S(2)}, u32[]{:S(2)}) collective-permute-start(f32[896,128]{1,0:T(8,128)} %get-tuple-element.37.refs_2_), channel_id=1, source_target_pairs={{0,8},{1,9},{2,10},{3,11},{4,12},{5,13},{6,14},{7,15},{8,0},{9,1},... | collective-permute-start | bytes 1376264 | tf_op jit(solution)/shard_map/ppermute | solution.py:279
  153.2 1.9 collective-permute-start.31
  153.3 2.4 %collective-permute-start.33 = (f32[896,128]{1,0:T(8,128)S(1)}, f32[896,128]{1,0:T(8,128)S(1)}, u32[]{:S(2)}, u32[]{:S(2)}) collective-permute-start(f32[896,128]{1,0:T(8,128)S(1)} %collective-permute-done.32.refs_2_), channel_id=1, source_target_pairs={{0,2},{1,3},{2,0},{3,1},{4,6},{5,7},{6,4},{7,5},{8,10},{9,11},{10,... | collective-permute-start | bytes 1376264 | tf_op jit(solution)/shard_map/ppermute | solution.py:279
  153.8 2.6 %collective-permute-start.34 = (f32[896,128]{1,0:T(8,128)S(1)}, f32[896,128]{1,0:T(8,128)S(1)}, u32[]{:S(2)}, u32[]{:S(2)}) collective-permute-start(f32[896,128]{1,0:T(8,128)S(1)} %collective-permute-done.28.refs_8_), channel_id=1, source_target_pairs={{0,2},{1,3},{2,0},{3,1},{4,6},{5,7},{6,4},{7,5},{8,10},{9,11},{10,... | collective-permute-start | bytes 1376264 | tf_op jit(solution)/shard_map/ppermute | solution.py:279
  153.9 3.2 %collective-permute-start.36 = (f32[896,128]{1,0:T(8,128)S(1)}, f32[896,128]{1,0:T(8,128)S(1)}, u32[]{:S(2)}, u32[]{:S(2)}) collective-permute-start(f32[896,128]{1,0:T(8,128)S(1)} %collective-permute-done.35.refs_10_), channel_id=1, source_target_pairs={{0,2},{1,3},{2,0},{3,1},{4,6},{5,7},{6,4},{7,5},{8,10},{9,11},{10,... | collective-permute-start | bytes 1376264 | tf_op jit(solution)/shard_map/ppermute | solution.py:279
  154.4 21.0 %collective-permute-start.38 = (f32[896,128]{1,0:T(8,128)S(1)}, f32[896,128]{1,0:T(8,128)S(1)}, u32[]{:S(2)}, u32[]{:S(2)}) collective-permute-start(f32[896,128]{1,0:T(8,128)S(1)} %broadcast_select_fusion.1), channel_id=1, source_target_pairs={{0,8},{1,9},{2,10},{3,11},{4,12},{5,13},{6,14},{7,15},{8,0},{9,1},... | collective-permute-start | bytes 1376264 | tf_op jit(solution)/shard_map/ppermute | solution.py:279
  155.1 20.5 %collective-permute-start.29 = (f32[896,128]{1,0:T(8,128)S(1)}, f32[896,128]{1,0:T(8,128)S(1)}, u32[]{:S(2)}, u32[]{:S(2)}) collective-permute-start(f32[896,128]{1,0:T(8,128)S(1)} %broadcast_select_fusion.3), channel_id=1, source_target_pairs={{0,4},{1,5},{2,6},{3,7},{4,0},{5,1},{6,2},{7,3},{8,12},{9,13},{10,... | collective-permute-start | bytes 1376264 | tf_op jit(solution)/shard_map/ppermute | solution.py:279
  175.4 1.9 collective-permute-start.39
  175.7 2.3 %collective-permute-start.37 = (f32[896,128]{1,0:T(8,128)S(1)}, f32[896,128]{1,0:T(8,128)S(1)}, u32[]{:S(2)}, u32[]{:S(2)}) collective-permute-start(f32[896,128]{1,0:T(8,128)S(1)} %broadcast_select_fusion.2), channel_id=1, source_target_pairs={{0,2},{1,3},{2,0},{3,1},{4,6},{5,7},{6,4},{7,5},{8,10},{9,11},{10,... | collective-permute-start | bytes 1376264 | tf_op jit(solution)/shard_map/ppermute | solution.py:279
  (17 other events, 153.5 us)
